TPU v7x, 32 devices: a whole 2x2x4 slice. The times are simulated.
32 devices in a mesh: dp: 8 (over z, y), blk: 4 (over x, core).
Axes of the slice: x: 2, y: 2, z: 4, core: 2. Of those that a mesh axis runs over, the one named last changes fastest.
Arguments:
- grad_partial: bfloat16 [8, 8, 1024, 1024], P('dp', 'blk'), may hold values from -1 to 1
- left_stat: float32 [8, 1024, 1024], P('blk', 'dp'), may hold values from -0.5 to 10, as said below
- right_stat: float32 [8, 1024, 1024], P('blk', 'dp'), may hold values from -0.5 to 10, as said below
- left_root: bfloat16 [8, 1024, 1024], P('blk', 'dp'), may hold values from -0.2 to 2, as said below
- right_root: bfloat16 [8, 1024, 1024], P('blk', 'dp'), may hold values from -0.2 to 2, as said below
- second_moment: float32 [8, 1024, 1024], P('blk', 'dp'), may hold values from 0.0003 to 0.01
Outputs:
- update: bfloat16 [8, 1024, 1024], P('blk')
- left_new: float32 [8, 1024, 1024], P('blk', 'dp')
- right_new: float32 [8, 1024, 1024], P('blk', 'dp')
- moment_new: float32 [8, 1024, 1024], P('blk', 'dp')
Inputs may be any that keep to these rules, and one draw needn't show every extreme that they name: `left_stat`: each block is symmetric. `right_stat`: each block is symmetric. `left_root`: each block is symmetric. `right_root`: each block is symmetric.
All inputs are finite; a program needn't handle non-finite values.
Results may differ from a plain program's by a relative error of at most 0.027.
Values may be sent and summed in bfloat16 or wider, within the bound.
No kernel may reach another device: no remote copies, remote signals or barrier semaphores. Data moves between devices by JAX's collectives and lax.ppermute only.
A program may use at most 128 MiB of HBM per device.

v0:
```python
import jax
import jax.numpy as jnp
from jax import lax
from jax.sharding import PartitionSpec as P

stat_decay = 0.95
moment_decay = 0.999
epsilon = 1e-08


def per_device(grad_partial, left_stat, right_stat, left_root, right_root, second_moment):
    row_count = left_stat.shape[1]
    row_start = lax.axis_index("dp") * row_count
    own_term = grad_partial[0].astype(jnp.float32)
    summed = lax.psum(own_term.astype(jnp.bfloat16), "dp").astype(jnp.float32)
    grad_rows = lax.dynamic_slice_in_dim(summed, row_start, row_count, 1)
    grad_low = summed.astype(jnp.bfloat16)
    moment_new = moment_decay * second_moment + (1.0 - moment_decay) * grad_rows * grad_rows
    adam_dir = grad_rows / (jnp.sqrt(moment_new) + epsilon)
    adam_part = jnp.sum(adam_dir * adam_dir)
    rows_low = grad_rows.astype(jnp.bfloat16)
    cols_low = lax.dynamic_slice_in_dim(grad_low, row_start, row_count, 2)
    left_new = stat_decay * left_stat + (1.0 - stat_decay) * jnp.einsum(
        "nrk,njk->nrj", rows_low, grad_low, preferred_element_type=jnp.float32
    )
    right_new = stat_decay * right_stat + (1.0 - stat_decay) * jnp.einsum(
        "nkr,nkj->nrj", cols_low, grad_low, preferred_element_type=jnp.float32
    )
    mixed_left = jnp.einsum(
        "nrk,nkj->nrj", left_root, grad_low, preferred_element_type=jnp.float32
    ).astype(jnp.bfloat16)
    precond = jnp.einsum(
        "nrk,nkj->nrj",
        mixed_left,
        lax.all_gather(right_root, "dp", axis=1, tiled=True),
        preferred_element_type=jnp.float32,
    ).astype(jnp.bfloat16)
    precond_wide = precond.astype(jnp.float32)
    adam_total, precond_total = lax.psum(
        (adam_part, jnp.sum(precond_wide * precond_wide)), ("dp", "blk")
    )
    factor = jnp.sqrt(adam_total / precond_total)
    update = lax.all_gather((factor * precond_wide).astype(jnp.bfloat16), "dp", axis=1, tiled=True)
    return (update, left_new, right_new, moment_new)


def solution(mesh):
    in_specs = (
        P("dp", "blk", None, None),
        P("blk", "dp", None),
        P("blk", "dp", None),
        P("blk", "dp", None),
        P("blk", "dp", None),
        P("blk", "dp", None),
    )
    out_specs = (
        P("blk", None, None),
        P("blk", "dp", None),
        P("blk", "dp", None),
        P("blk", "dp", None),
    )
    return jax.shard_map(
        per_device, mesh=mesh, in_specs=in_specs, out_specs=out_specs, check_vma=False
    )
```

profile of v0, /device:TPU:0, one launch (start us, length us, event | category | flops | bytes accessed | tf_op | source)
XLA Modules:
  0.0 377.4 jit_solution(12530037467889012614)
XLA Ops:
  7.2 0.0 copy-start
  7.2 0.0 copy-start.3
  7.2 0.0 all-reduce.3.cloned.1.call-start
  7.2 0.7 all-reduce.3.cloned.1.call-update
  7.9 0.0 all-gather.3.cloned.1.call-start
  8.0 0.7 all-gather.3.cloned.1.call-update
  8.7 0.0 all-gather.5.cloned.1.call-start
  8.7 162.0 %all-reduce.3.cloned.1.call-done = bf16[2,1024,1024]{2,1,0:T(8,128)(2,1)} async-done(((bf16[2,1024,1024]{2,1,0:T(8,128)(2,1)}), bf16[2,1024,1024]{2,1,0:T(8,128)(2,1)}) %all-reduce.3.cloned.1.call-update) | async-done | bytes 4194320 | tf_op jit(solution)/shard_map/psum | solution.py:15
  170.7 0.0 copy-done.3
  170.7 3.2 fusion.6
  173.9 0.0 copy-start.2
  173.9 71.4 %all-gather.3.cloned.1.call-done = bf16[2,1024,1024]{2,1,0:T(8,128)(2,1)} async-done(((bf16[2,128,1024]{2,1,0:T(8,128)(2,1)}), bf16[2,1024,1024]{2,1,0:T(8,128)(2,1)}) %all-gather.3.cloned.1.call-update) | async-done | bytes 4194320 | tf_op jit(solution)/shard_map/all_gather | solution.py:35
  245.3 0.0 copy-done
  245.3 5.4 %fusion.2 = (f32[]{:T(128)}, bf16[2,128,1024]{2,1,0:T(8,128)(2,1)S(1)}) fusion(bf16[2,1024,1024]{2,1,0:T(8,128)(2,1)} %all-gather.3.cloned.1.call-done, bf16[2,128,1024]{2,1,0:T(8,128)(2,1)S(1)} %copy-done, bf16[2,1024,1024]{2,1,0:T(8,128)(2,1)} %all-reduce.3.cloned.1.call-done), kind=kOutput, calls=%fused_computation.12 | convolution fusion | flops 1075052544 | bytes 9437188 | tf_op jit(solution)/shard_map/nrk,nkj->nrj/dot_general | solution.py:32
  250.7 38.9 %all-reduce = (f32[]{:T(128)}, f32[]{:T(128)}) all-reduce(f32[]{:T(128)} %get-tuple-element.6, f32[]{:T(128)} %get-tuple-element.8), channel_id=1, replica_groups=mesh['dp'=8,'blk'=4] {'dp','blk'}, use_global_device_ids=true, to_apply=%region_2.0 | all-reduce | flops 2 | bytes 16 | tf_op jit(solution)/shard_map/psum | solution.py:39
  291.0 0.9 fusion.3
  291.9 0.0 all-gather.5.cloned.1.call-update
  291.9 0.0 copy-done.2
  291.9 0.0 copy-start.1
  291.9 0.0 copy-start.4
  291.9 4.4 %fusion = f32[2,128,1024]{2,1,0:T(8,128)} fusion(bf16[2,1024,1024]{2,1,0:T(8,128)(2,1)} %all-reduce.3.cloned.1.call-done, f32[2,128,1024]{2,1,0:T(8,128)S(1)} %copy-done.2, s32[]{:T(128)S(6)} %select_n.4), kind=kOutput, calls=%fused_computation.5 | convolution fusion | flops 537657344 | bytes 6815748 | tf_op jit(solution)/shard_map/nkr,nkj->nrj/dot_general | solution.py:26
  296.3 0.0 copy-done.1
  296.3 0.0 copy-done.4
  296.3 2.5 fusion.1
  298.8 67.4 %all-gather.5.cloned.1.call-done = bf16[2,1024,1024]{2,1,0:T(8,128)(2,1)} async-done(((bf16[2,128,1024]{2,1,0:T(8,128)(2,1)}), bf16[2,1024,1024]{2,1,0:T(8,128)(2,1)}) %all-gather.5.cloned.1.call-update) | async-done | bytes 4194320 | tf_op jit(solution)/shard_map/all_gather | solution.py:43
  366.2 4.6 %copy.15 = bf16[2,1024,1024]{2,1,0:T(8,128)(2,1)} copy(bf16[2,1024,1024]{2,1,0:T(8,128)(2,1)} %all-gather.5.cloned.1.call-done) | data formatting | bytes 8388608
Async XLA Ops:
  7.2 238.2 %copy-start = (bf16[2,128,1024]{2,1,0:T(8,128)(2,1)S(1)}, bf16[2,128,1024]{2,1,0:T(8,128)(2,1)}, u32[]{:S(2)}) copy-start(bf16[2,128,1024]{2,1,0:T(8,128)(2,1)} %param.9) | copy-start | bytes 1572868
  7.2 163.6 %copy-start.3 = (f32[2,128,1024]{2,1,0:T(8,128)S(1)}, f32[2,128,1024]{2,1,0:T(8,128)}, u32[]{:S(2)}) copy-start(f32[2,128,1024]{2,1,0:T(8,128)} %param.11) | copy-start | bytes 3145732
  7.2 163.5 %all-reduce.3.cloned.1.call-start = ((), (), s32[]{:S(2)}) async-start(), calls=%async_computation | async-start | bytes 8388608 | tf_op jit(solution)/shard_map/psum | solution.py:15
  7.9 237.4 %all-gather.3.cloned.1.call-start = ((), (), s32[]{:S(2)}) async-start(), calls=%async_computation.1 | async-start | bytes 4718592 | tf_op jit(solution)/shard_map/all_gather | solution.py:35
  8.7 357.6 %all-gather.5.cloned.1.call-start = ((), (), s32[]{:S(2)}) async-start(), calls=%async_computation.2 | async-start | bytes 4718592 | tf_op jit(solution)/shard_map/all_gather | solution.py:43
  173.9 118.0 %copy-start.2 = (f32[2,128,1024]{2,1,0:T(8,128)S(1)}, f32[2,128,1024]{2,1,0:T(8,128)}, u32[]{:S(2)}) copy-start(f32[2,128,1024]{2,1,0:T(8,128)} %param.8) | copy-start | bytes 3145732
  291.9 4.4 %copy-start.1 = (bf16[2,1024,1024]{2,1,0:T(8,128)(2,1)S(1)}, bf16[2,1024,1024]{2,1,0:T(8,128)(2,1)}, u32[]{:S(2)}) copy-start(bf16[2,1024,1024]{2,1,0:T(8,128)(2,1)} %all-reduce.3.cloned.1.call-done) | copy-start | bytes 12582916
  291.9 4.4 %copy-start.4 = (f32[2,128,1024]{2,1,0:T(8,128)S(1)}, f32[2,128,1024]{2,1,0:T(8,128)}, u32[]{:S(2)}) copy-start(f32[2,128,1024]{2,1,0:T(8,128)} %param.7) | copy-start | bytes 3145732
Sparse Core Ops, SparseCore 0:
  11.7 158.9 all-reduce.2
  172.9 72.3 all-gather.2
  292.0 74.1 all-gather.4
where the time goes:
time: 378 us; the launch traced here: 377 us
  waiting for transfers between devices  302 us (80%)
  blocking collectives  38.9 us (10%)
  between operations  15.2 us (4%)
  matrix products  12.3 us (3%)
  local copies, waits for them, and re-layouts  4.67 us (1%)
  other arithmetic  4.08 us (1%)
    psum x1, waiting for transfers between devices, per_device(): summed = lax.psum(own_term.astype(jnp.bfloat16), 'dp').astype(jnp.float32)  162 us
    all_gather x1, waiting for transfers between devices, per_device(): lax.all_gather(right_root, 'dp', axis=1, tiled=True)  71.4 us
    all_gather x1, waiting for transfers between devices, per_device(): lax.all_gather((factor * precond_wide).astype(jnp.bfloat16), 'dp', axis=1...  67.4 us
    psum x1, blocking collectives, per_device(): lax.psum((adam_part, jnp.sum(precond_wide * precond_wide)), ('dp', 'blk'))  38.9 us
  transfers between devices with their start and end apart: 3, of which 3 were waited for; matrix products, arithmetic and copies ran while one was open for 3% of the time, Pallas kernels for 0%

commit v1 on v0

v1 whole, which is shorter than its diff:
```python
import functools

import jax
import jax.numpy as jnp
from jax import lax
from jax.experimental import pallas as pl
from jax.experimental.pallas import tpu as pltpu
from jax.sharding import PartitionSpec as P

stat_decay = 0.95
moment_decay = 0.999
epsilon = 1e-08

f32 = jnp.float32
bf16 = jnp.bfloat16


def bits_of(count):
    bits = count.bit_length() - 1
    assert count == 1 << bits
    return bits


VMEM = pl.BlockSpec(memory_space=pltpu.VMEM)
SMEM = pl.BlockSpec(memory_space=pltpu.SMEM)


def call(kernel, out_shape, name, flops=0):
    def run(place, *arrays):
        size = sum(a.size * a.dtype.itemsize for a in arrays)
        return pl.pallas_call(
            kernel,
            out_shape=out_shape,
            in_specs=[SMEM] + [VMEM] * len(arrays),
            out_specs=jax.tree.map(lambda _: VMEM, out_shape),
            compiler_params=pltpu.CompilerParams(vmem_limit_bytes=24 * 2**20),
            cost_estimate=pl.CostEstimate(flops=flops, bytes_accessed=size, transcendentals=0),
            name=name,
        )(place, *arrays)

    return run


def block_span(members, rows, part, member):
    return pl.ds(pl.multiple_of((part * members + member) * rows, rows), rows)


def cut_kernel(bits, orders, flip, grads_ref, *refs):
    out_refs, sems = refs[:-1], refs[-1]
    index = lax.axis_index("dp")
    copies = []
    for part, (first, out_ref) in enumerate(zip(orders, out_refs)):
        own = (index >> first) & 1
        for i in range(out_ref.shape[0]):
            rest = [(i >> j) & 1 for j in range(bits - 1)]
            rest.insert(first, 1 - own if flip else own)
            member = sum(bit << j for j, bit in enumerate(rest[:-1]))
            source = grads_ref.at[rest[-1], part, member]
            copy = pltpu.make_async_copy(source, out_ref.at[i], sems.at[len(copies)])
            copy.start()
            copies.append(copy)
    for copy in copies:
        copy.wait()


def cut(grads, bits, orders, flip):
    members, rows, width = grads.shape[2:]
    shape = jax.ShapeDtypeStruct((members, rows, width), bf16)
    return pl.pallas_call(
        functools.partial(cut_kernel, bits, orders, flip),
        out_shape=(shape, shape),
        in_specs=[pl.BlockSpec(memory_space=pl.ANY)],
        out_specs=(VMEM, VMEM),
        scratch_shapes=[pltpu.SemaphoreType.DMA((2 * members,))],
        compiler_params=pltpu.CompilerParams(vmem_limit_bytes=(56 if flip else 24) * 2**20),
        cost_estimate=pl.CostEstimate(flops=0, bytes_accessed=8 * members * rows * width, transcendentals=0),
        name="cut",
    )(grads)


def sum_kernel(axes_lists, places, free, place_ref, *refs):
    index, out_ref = place_ref[2], refs[-1]
    for i in range(1 << len(free)):
        total = None
        for axes, ref in zip(axes_lists, refs):
            at = 0
            for axis in axes:
                if axis in places:
                    bit = (index >> axis) & 1
                    at = at * 2 + (1 - bit if places[axis] else bit)
                else:
                    at = at * 2 + ((i >> (len(free) - 1 - free.index(axis))) & 1)
            piece = ref[at].astype(f32)
            total = piece if total is None else total + piece
        out_ref[i] = total.astype(bf16)


def sum_pieces(place, terms, places):
    arrays = [array.reshape((-1,) + array.shape[-2:]) for array, _ in terms]
    axes_lists = [axes for _, axes in terms]
    free = [axis for axis in axes_lists[0] if axis not in places]
    shape = arrays[0].shape[-2:]
    kernel = functools.partial(sum_kernel, axes_lists, places, free)
    out = call(kernel, jax.ShapeDtypeStruct((1 << len(free),) + shape, bf16), "sum_pieces")(place, *arrays)
    return out.reshape([2] * len(free) + list(shape))


def neighbour_of(member):
    return member ^ (1 + ((member ^ (member >> 1)) & 1))


def pack_kernel(members, rows, place_ref, own_ref, partner_ref, pair_ref, message_ref):
    member, half = place_ref[0], place_ref[1]
    pair_ref[half] = own_ref[half]
    pair_ref[1 - half] = partner_ref[...]
    role = member >> 1
    blocks = [(0, 0, member), (0, 1, member), (1, 1, member)]
    blocks += [(row_part, part, neighbour_of(member)) for row_part in range(2) for part in range(2)]
    blocks += [(0, role, member ^ 3), (role, 1, member ^ 3)]
    for i, (row_part, part, column) in enumerate(blocks):
        message_ref[i] = pair_ref[row_part, :, block_span(members, rows, part, column)]


def pack(place, own, partner, members):
    rows, width = own.shape[1:]
    out_shape = (jax.ShapeDtypeStruct((2, rows, width), bf16), jax.ShapeDtypeStruct((9, rows, rows), bf16))
    return call(functools.partial(pack_kernel, members, rows), out_shape, "pack")(place, own, partner)


def unfold_kernel(members, rows, place_ref, pair_ref, *refs):
    message_refs, whole_ref = refs[:-1], refs[-1]
    member = place_ref[0]

    def put(row_part, row_member, part, column_member, block):
        whole_ref[
            block_span(members, rows, row_part, row_member), block_span(members, rows, part, column_member)
        ] = block

    for row_part in range(2):
        whole_ref[block_span(members, rows, row_part, member), :] = pair_ref[row_part]
    for k, message_ref in enumerate(message_refs, 1):
        sender = member ^ k
        neighbour, opposite, role = neighbour_of(sender), sender ^ 3, sender >> 1
        for row_part in range(2):
            for part in range(2):
                mine = pair_ref[row_part, :, block_span(members, rows, part, sender)]
                put(part, sender, row_part, member, mine.T)
                block = message_ref[3 + 2 * row_part + part]
                put(row_part, sender, part, neighbour, block)
                put(part, neighbour, row_part, sender, block.T)
        put(0, sender, 0, sender, message_ref[0])
        put(0, sender, 1, sender, message_ref[1])
        put(1, sender, 0, sender, message_ref[1].T)
        put(1, sender, 1, sender, message_ref[2])
        put(0, sender, role, opposite, message_ref[7])
        put(role, opposite, 0, sender, message_ref[7].T)
        put(role, sender, 1, opposite, message_ref[8])
        put(1, opposite, role, sender, message_ref[8].T)


def unfold(place, pair, messages, members):
    rows, width = pair.shape[1:]
    out_shape = jax.ShapeDtypeStruct((2 * members * rows, width), bf16)
    return call(functools.partial(unfold_kernel, members, rows), out_shape, "unfold")(place, pair, *messages)


def place_kernel(members, rows, place_ref, *refs):
    for k in range(members):
        for part in range(2):
            refs[-1][block_span(members, rows, part, place_ref[0] ^ k), :] = refs[k][part]


def place_rows(place, pieces):
    members = len(pieces)
    rows, width = pieces[0].shape[1:]
    out_shape = jax.ShapeDtypeStruct((2 * members * rows, width), bf16)
    return call(functools.partial(place_kernel, members, rows), out_shape, "place_rows")(place, *pieces)


def two_products(left, grad_ref, right_ref):
    mixed_left = jnp.dot(left, grad_ref[...], preferred_element_type=f32).astype(bf16)
    return jnp.dot(mixed_left, right_ref[...], preferred_element_type=f32).astype(bf16)


def product_kernel(members, rows, place_ref, *refs):
    grad_pieces = refs[: 2 * members]
    right_ref, left_ref, precond_ref, grad_ref, square_ref = refs[2 * members :]
    for part in range(2):
        for k in range(members):
            grad_ref[block_span(members, rows, part, place_ref[0] ^ k), :] = grad_pieces[part * members + k][...]
    precond = two_products(left_ref[...], grad_ref, right_ref)
    precond_ref[...] = precond
    precond_wide = precond.astype(f32)
    square_ref[...] = jnp.full(square_ref.shape, jnp.sum(precond_wide * precond_wide))


def product(place, grad_pieces, right_full, left_pair):
    members = len(grad_pieces) // 2
    rows, width = grad_pieces[0].shape
    out_shape = (
        jax.ShapeDtypeStruct((2 * rows, width), bf16),
        jax.ShapeDtypeStruct((2 * rows * members, width), bf16),
        jax.ShapeDtypeStruct((8, 128), f32),
    )
    kernel = functools.partial(product_kernel, members, rows)
    return call(kernel, out_shape, "product", 8 * rows * width * width)(place, *grad_pieces, right_full, left_pair)


def per_device(devices, groups, grad_partial, left_stat, right_stat, left_root, right_root, second_moment):
    bits = bits_of(devices)
    top = bits - 1
    members = devices // 2
    index = lax.axis_index("dp")
    member, half = index % members, index // members
    rows, width = left_stat.shape[1:]

    def swap(array, bit):
        return lax.ppermute(array, "dp", [(i, i ^ (1 << bit)) for i in range(devices)])

    def after(array, *arrays):
        return lax.optimization_barrier((array, *arrays))[0]

    def gather_pieces(own, *before_forward):
        pieces = {0: own}
        for bit in range(top - 1, -1, -1):
            for k in list(pieces):
                source = after(pieces[k], *before_forward) if k and before_forward else pieces[k]
                pieces[k ^ (1 << bit)] = swap(source, bit)
        return pieces

    def gather_direct(own):
        pieces = {0: own}
        for k in range(members - 1, 0, -1):
            pieces[k] = lax.ppermute(own, "dp", [(i, i ^ k) for i in range(devices)])
        return pieces

    def by_half(own, partner):
        return jnp.stack([jnp.where(half == 0, own, partner), jnp.where(half == 0, partner, own)])

    def choose(stack, place):
        return lax.dynamic_index_in_dim(stack, place, 0, keepdims=False)

    member_axes = list(range(top - 1, -1, -1))
    grads = grad_partial[0].reshape(2, 2, members, rows, width)
    lower = list(range(top))
    orders = (lower + [top], lower[::-1] + [top])
    first_sends = cut(grads, bits, [order[0] for order in orders], True)
    first_own = cut(after(grads, *first_sends), bits, [order[0] for order in orders], False)
    terms, places = [[], []], [{}, {}]
    right_partner = swap(choose(right_root, 1 - half), top)

    place = jnp.stack([member, half, index])

    def reduce_step(part, step, *arrays):
        bit = orders[part][step]
        if step == 0:
            send = first_sends[part]
        else:
            if arrays:
                array, axes = terms[part][-1]
                terms[part][-1] = (after(array, *arrays), axes)
            send = sum_pieces(place, terms[part], {**places[part], bit: True})
        places[part][bit] = False
        axes = [b for b in [top] + member_axes if b not in places[part]]
        if step == 0:
            terms[part] = [(first_own[part], axes)]
        terms[part].append((swap(send, bit), axes))
        return send

    def reduced(part):
        return sum_pieces(place, terms[part], places[part])

    reduce_step(1, 0)
    reduce_step(0, 0)
    left_partner = swap(after(choose(left_root, 1 - half), terms[0][-1][0], terms[1][-1][0]), top)
    for step in range(1, bits - 1):
        for part in range(2):
            reduce_step(part, step, right_partner)
    round_ends = [t[-1][0] for t in terms]

    halved = members == 4 and rows % 128 == 0

    def pair_rows(own, partner):
        if halved:
            return pack(place, own, partner, members)
        pair = by_half(choose(own, half), partner)
        return pair, pair

    def whole_matrix(pair, pieces):
        if halved:
            return unfold(place, pair, [pieces[k] for k in range(1, members)], members)
        return place_rows(place, [pieces[k] for k in range(members)])

    def exchanged(pieces):
        return [pieces[1 << bit] for bit in member_axes]

    last_send = reduce_step(0, bits - 1, *round_ends, left_partner)
    right_pair, right_message = pair_rows(right_root, right_partner)
    right_pieces = gather_pieces(after(right_message, last_send))
    low = [reduced(0)]
    reduce_step(1, bits - 1, low[0])
    grad_pieces = [gather_pieces(after(low[0], *exchanged(right_pieces)))]
    right_full = whole_matrix(right_pair, right_pieces)
    low.append(after(reduced(1), *exchanged(grad_pieces[0])))
    grad_pieces.append(gather_direct(low[1]))
    own_low = jnp.stack(low)
    theirs = swap(choose(own_low, 1 - half), top)

    span = 2 * rows
    left_pair = by_half(choose(left_root, half), left_partner)
    precond, grad_low, precond_part = product(
        place,
        [pieces[k] for pieces in grad_pieces for k in range(members)],
        right_full,
        left_pair.reshape(span, width),
    )
    precond = precond.reshape(2, rows, width)
    theirs, own_low, grad_low = (after(array, precond) for array in (theirs, own_low, grad_low))

    first_pieces = {0: precond}
    for bit in range(top - 1, 0, -1):
        for k in list(first_pieces):
            first_pieces[k ^ (1 << bit)] = swap(first_pieces[k], bit)
    first_pieces[1] = swap(precond, 0)
    partner = swap(precond, top)

    grad_rows = by_half(choose(own_low, half), theirs).astype(f32)
    moment_new = moment_decay * second_moment + (1.0 - moment_decay) * grad_rows * grad_rows
    adam_dir = grad_rows / (jnp.sqrt(moment_new) + epsilon)
    adam_part = jnp.sum(adam_dir * adam_dir)

    lane = lax.broadcasted_iota(jnp.int32, (8, 128), 1)
    sums = jnp.where(lane == 0, adam_part, precond_part)
    for bit in range(bits_of(groups)):
        sums = sums + lax.ppermute(sums, "blk", [(i, i ^ (1 << bit)) for i in range(groups)])
    for bit in range(bits):
        if bit == top:
            sums = after(sums, partner, *first_pieces.values())
        sums = sums + swap(sums, bit)

    def columns(part):
        return lax.dynamic_slice_in_dim(grad_low, part * members * rows + member * rows, rows, 1)

    contract_rows = (((0,), (0,)), ((), ()))
    contract_cols = (((1,), (1,)), ((), ()))
    right_gram = [lax.dot_general(columns(p), grad_low, contract_rows, preferred_element_type=f32) for p in range(2)]
    right_gram = jnp.stack(right_gram)
    left_gram = lax.dot_general(own_low.reshape(span, width), grad_low, contract_cols, preferred_element_type=f32)
    left_gram = left_gram.reshape(2, rows, width)
    left_away = choose(left_gram, 1 - half).astype(bf16)
    right_away = choose(right_gram, 1 - half).astype(bf16)

    partner, *arrived = lax.optimization_barrier((partner, *first_pieces.values()))
    first_pieces = dict(zip(first_pieces, arrived))
    onward = [k for k in first_pieces if k > 1]
    neighbour = swap(jnp.stack([first_pieces[k] for k in onward] + [partner]), 0)
    for i, k in enumerate(onward):
        first_pieces[k ^ 1] = neighbour[i]
    second_pieces = {0: partner, 1: neighbour[-1]}
    for k in range(members - 1, 1, -1):
        second_pieces[k] = lax.ppermute(partner, "dp", [(i, i ^ k) for i in range(devices)])
    grams_away = after(jnp.stack([left_away, right_away]), partner)
    grams_partner = swap(grams_away, top)

    factor = jnp.sqrt(sums[0, 0] / sums[0, 1])
    update = jnp.zeros((2, 2, members, rows, width), bf16)
    for block, pieces in ((half, first_pieces), (1 - half, second_pieces)):
        for k, piece in pieces.items():
            scaled = (factor * piece.astype(f32)).astype(bf16)
            update = lax.dynamic_update_slice(update, scaled[None, :, None], (block, 0, member ^ k, 0, 0))
    update = update.reshape(2, width, width)
    left_partner, right_partner = after(grams_partner, update)

    def new_stat(stat, gram, partner):
        return stat_decay * stat + (1.0 - stat_decay) * by_half(choose(gram, half), partner.astype(f32))

    left_new = new_stat(left_stat, left_gram, left_partner)
    right_new = new_stat(right_stat, right_gram, right_partner)
    return (update, left_new, right_new, moment_new)


def solution(mesh):
    in_specs = (
        P("dp", "blk", None, None),
        P("blk", "dp", None),
        P("blk", "dp", None),
        P("blk", "dp", None),
        P("blk", "dp", None),
        P("blk", "dp", None),
    )
    out_specs = (
        P("blk", None, None),
        P("blk", "dp", None),
        P("blk", "dp", None),
        P("blk", "dp", None),
    )

    def body(*arrays):
        return per_device(mesh.shape["dp"], mesh.shape["blk"], *arrays)

    return jax.shard_map(body, mesh=mesh, in_specs=in_specs, out_specs=out_specs, check_vma=False)
```

time: 378 us -> 171 us (0.45)
  waiting for transfers between devices: 302 us -> 91 us
  starting transfers between devices: 0.11 us -> 44.3 us
  blocking collectives: 38.9 us -> 0 us
  Pallas kernels: 0 us -> 12.8 us
  between operations: 15.2 us -> 2.46 us
  matrix products: 12.3 us -> 1.76 us
  other arithmetic: 4.08 us -> 9.07 us
  local copies, waits for them, and re-layouts: 4.67 us -> 9.46 us
    psum x1 -> x0, waiting for transfers between devices: 162 us -> none  [per_device(): summed = lax.psum(own_term.astype(jnp.bfloat16), 'dp').astype(jnp.float32)]
    all_gather x2 -> x0, waiting for transfers between devices: 139 us -> none  [the longest x1 71.4 us: per_device(): lax.all_gather(right_root, 'dp', axis=1, tiled=True)]
    ppermute x0 -> x30, waiting for transfers between devices: none -> 91 us  [the longest x23 87.4 us: swap(): lax.ppermute(array, 'dp', [(i, i ^ 1 << bit) for i in range(devices)])]
    ppermute x0 -> x30, starting transfers between devices: none -> 44.3 us  [the longest x23 36.7 us: swap(): lax.ppermute(array, 'dp', [(i, i ^ 1 << bit) for i in range(devices)])]
    psum x1 -> x0, blocking collectives: 38.9 us -> none  [per_device(): lax.psum((adam_part, jnp.sum(precond_wide * precond_wide)), ('dp', 'blk'))]
    pallas_call x0 -> x11, Pallas kernels: none -> 12.8 us  [the longest x9 9.62 us: run(): pl.pallas_call(kernel, out_shape=out_shape, in_specs=[SMEM] + [VMEM] * le...]
    dot_general x3, matrix products: 12.3 us -> 1.76 us  [the longest x2 0.96 us: per_device(): lax.dot_general(columns(p), grad_low, contract_rows, preferred_element_ty...]
    unnamed x11 -> x44, local copies, waits for them, and re-layouts: 4.67 us -> 7.61 us
  transfers between devices with their start and end apart: 3 -> 30, of which waited for: 3 -> 16; matrix products, arithmetic and copies ran while one was open for 3% -> 6% of each run, Pallas kernels for 0% -> 5%
where the time goes in v1:
time: 171 us
  waiting for transfers between devices  91 us (53%)
  starting transfers between devices  44.3 us (26%)
  Pallas kernels  12.8 us (7%)
  local copies, waits for them, and re-layouts  9.46 us (6%)
  other arithmetic  9.07 us (5%)
  between operations  2.46 us (1%)
  matrix products  1.76 us (1%)
    ppermute x23, waiting for transfers between devices, swap(): lax.ppermute(array, 'dp', [(i, i ^ 1 << bit) for i in range(devices)])  87.4 us
    ppermute x23, starting transfers between devices, swap(): lax.ppermute(array, 'dp', [(i, i ^ 1 << bit) for i in range(devices)])  36.7 us
    pallas_call x9, Pallas kernels, run(): pl.pallas_call(kernel, out_shape=out_shape, in_specs=[SMEM] + [VMEM] * le...  9.62 us
    unnamed x44, local copies, waits for them, and re-layouts  7.61 us
    ppermute x3, starting transfers between devices, gather_direct(): pieces[k] = lax.ppermute(own, 'dp', [(i, i ^ k) for i in range(devices)])  4.05 us
  transfers between devices with their start and end apart: 30, of which 16 were waited for; matrix products, arithmetic and copies ran while one was open for 6% of the time, Pallas kernels for 5%

profile of v1, /device:TPU:0, one launch (start us, length us, event | category | flops | bytes accessed | tf_op | source)
XLA Modules:
  0.0 170.8 jit_solution(13889587298749349120)
XLA Ops:
  0.6 3.0 %cut.2 = (bf16[4,128,1024]{2,1,0:T(8,128)(2,1)}, bf16[4,128,1024]{2,1,0:T(8,128)(2,1)}) custom-call(bf16[2,2,4,128,1024]{4,3,2,1,0:T(8,128)(2,1)} %bitcast.103), custom_call_target="tpu_custom_call" | custom-call | bytes 4194304 | tf_op jit(solution)/shard_map/cut/pallas_call | solution.py:69
  3.6 3.0 %collective-permute-start = (bf16[4,128,1024]{2,1,0:T(8,128)(2,1)}, bf16[4,128,1024]{2,1,0:T(8,128)(2,1)S(1)}, u32[]{:S(2)}, u32[]{:S(2)}) collective-permute-start(bf16[4,128,1024]{2,1,0:T(8,128)(2,1)} %get-tuple-element.32), channel_id=1, source_target_pairs={{0,4},{4,0},{8,12},{12,8},{16,20},{20,16},{24,28},{28,24},{1,5},{5... | collective-permute-start | bytes 3145736 | tf_op jit(solution)/shard_map/ppermute | solution.py:218
  6.6 1.6 collective-permute-start.3
  8.2 0.7 dynamic-slice_bitcast_fusion.1
  8.9 2.6 %collective-permute-start.1 = (bf16[128,1024]{1,0:T(8,128)(2,1)}, bf16[128,1024]{1,0:T(8,128)(2,1)S(1)}, u32[]{:S(2)}, u32[]{:S(2)}) collective-permute-start(bf16[128,1024]{1,0:T(8,128)(2,1)} %dynamic-slice_bitcast_fusion.1), channel_id=1, source_target_pairs={{0,16},{4,20},{8,24},{12,28},{16,0},{20,4},{24,8},{28,12},{1,17},{... | collective-permute-start | bytes 786440 | tf_op jit(solution)/shard_map/ppermute | solution.py:218
  11.5 2.2 %copy-done = bf16[1,2,1024,1024]{3,2,1,0:T(8,128)(2,1)S(1)} copy-done((bf16[1,2,1024,1024]{3,2,1,0:T(8,128)(2,1)S(1)}, bf16[1,2,1024,1024]{3,2,1,0:T(8,128)(2,1)}, u32[]{:S(2)}) %copy-start) | copy-done | bytes 4194328
  14.0 1.0 copy-done.1
  15.0 21.3 %collective-permute-done.1.partner_ref = bf16[128,1024]{1,0:T(8,128)(2,1)S(1)} collective-permute-done((bf16[128,1024]{1,0:T(8,128)(2,1)}, bf16[128,1024]{1,0:T(8,128)(2,1)S(1)}, u32[]{:S(2)}, u32[]{:S(2)}) %collective-permute-start.1) | collective-permute-done | bytes 262176 | tf_op jit(solution)/shard_map/ppermute | solution.py:218
  36.3 0.7 copy-done.14
  37.0 1.2 copy-done.2
  38.2 0.7 sum_pieces.6
  38.9 3.5 %collective-permute-start.2 = (bf16[2,128,1024]{2,1,0:T(8,128)(2,1)S(1)}, bf16[2,128,1024]{2,1,0:T(8,128)(2,1)S(1)}, u32[]{:S(2)}, u32[]{:S(2)}) collective-permute-start(bf16[2,128,1024]{2,1,0:T(8,128)(2,1)S(1)} %sum_pieces.6), channel_id=1, source_target_pairs={{0,8},{4,12},{8,0},{12,4},{16,24},{20,28},{24,16},{28,20},{1,9},{5... | collective-permute-start | bytes 1572872 | tf_op jit(solution)/shard_map/ppermute | solution.py:218
  42.4 0.7 sum_pieces.7
  43.0 0.6 collective-permute-start.4
  43.7 0.7 pack.1
  44.4 13.6 %collective-permute-done.5 = bf16[128,1024]{1,0:T(8,128)(2,1)S(1)} collective-permute-done((bf16[128,1024]{1,0:T(8,128)(2,1)S(1)}, bf16[128,1024]{1,0:T(8,128)(2,1)S(1)}, u32[]{:S(2)}, u32[]{:S(2)}) %collective-permute-start.5) | collective-permute-done | bytes 262176 | tf_op jit(solution)/shard_map/ppermute | solution.py:218
  58.0 0.7 collective-permute-done.2.refs_2_
  58.7 0.6 sum_pieces.8
  59.4 1.7 %collective-permute-start.8 = (bf16[9,128,128]{2,1,0:T(8,128)(2,1)S(1)}, bf16[9,128,128]{2,1,0:T(8,128)(2,1)S(1)}, u32[]{:S(2)}, u32[]{:S(2)}) collective-permute-start(bf16[9,128,128]{2,1,0:T(8,128)(2,1)S(1)} %get-tuple-element.43), channel_id=1, source_target_pairs={{0,8},{4,12},{8,0},{12,4},{16,24},{20,28},{24,16},{28,20},{1,9},{5... | collective-permute-start | bytes 884744 | tf_op jit(solution)/shard_map/ppermute | solution.py:218
  61.1 0.5 collective-permute-start.9
  61.6 1.1 collective-permute-start.6
  62.7 8.5 %collective-permute-done.6 = bf16[128,1024]{1,0:T(8,128)(2,1)S(1)} collective-permute-done((bf16[128,1024]{1,0:T(8,128)(2,1)S(1)}, bf16[128,1024]{1,0:T(8,128)(2,1)S(1)}, u32[]{:S(2)}, u32[]{:S(2)}) %collective-permute-start.6) | collective-permute-done | bytes 262176 | tf_op jit(solution)/shard_map/ppermute | solution.py:218
  71.2 0.7 sum_pieces.9
  71.9 1.3 sum_pieces.10
  73.2 3.2 %collective-permute-start.7 = (bf16[128,1024]{1,0:T(8,128)(2,1)}, bf16[128,1024]{1,0:T(8,128)(2,1)}, u32[]{:S(2)}, u32[]{:S(2)}) collective-permute-start(bf16[128,1024]{1,0:T(8,128)(2,1)} %bitcast.9), channel_id=1, source_target_pairs={{0,16},{4,20},{8,24},{12,28},{16,0},{20,4},{24,8},{28,12},{1,17},{... | collective-permute-start | bytes 786440 | tf_op jit(solution)/shard_map/ppermute | solution.py:218
  76.5 0.7 copy-done.10
  77.2 0.7 copy-done.12
  77.9 1.3 collective-permute-start.11
  79.2 2.4 %collective-permute-start.10 = (bf16[128,1024]{1,0:T(8,128)(2,1)S(1)}, bf16[128,1024]{1,0:T(8,128)(2,1)}, u32[]{:S(2)}, u32[]{:S(2)}) collective-permute-start(bf16[128,1024]{1,0:T(8,128)(2,1)S(1)} %bitcast.106), channel_id=1, source_target_pairs={{0,8},{4,12},{8,0},{12,4},{16,24},{20,28},{24,16},{28,20},{1,9},{5... | collective-permute-start | bytes 786440 | tf_op jit(solution)/shard_map/ppermute | solution.py:218
  81.6 0.6 collective-permute-start.16
  82.2 1.1 fusion.30
  83.2 2.2 %collective-permute-done.7 = bf16[128,1024]{1,0:T(8,128)(2,1)} collective-permute-done((bf16[128,1024]{1,0:T(8,128)(2,1)}, bf16[128,1024]{1,0:T(8,128)(2,1)}, u32[]{:S(2)}, u32[]{:S(2)}) %collective-permute-start.7) | collective-permute-done | bytes 262176 | tf_op jit(solution)/shard_map/ppermute | solution.py:218
  85.4 1.0 copy-done.5
  86.5 1.1 sum_pieces.11
  87.7 2.3 %collective-permute-start.13 = (bf16[128,1024]{1,0:T(8,128)(2,1)S(1)}, bf16[128,1024]{1,0:T(8,128)(2,1)S(1)}, u32[]{:S(2)}, u32[]{:S(2)}) collective-permute-start(bf16[128,1024]{1,0:T(8,128)(2,1)S(1)} %bitcast.108), channel_id=1, source_target_pairs={{0,4},{4,0},{8,12},{12,8},{16,20},{20,16},{24,28},{28,24},{1,5},{5... | collective-permute-start | bytes 786440 | tf_op jit(solution)/shard_map/ppermute | solution.py:234
  90.3 1.5 collective-permute-start.15
  91.8 1.8 %collective-permute-start.12 = (bf16[128,1024]{1,0:T(8,128)(2,1)}, bf16[128,1024]{1,0:T(8,128)(2,1)S(1)}, u32[]{:S(2)}, u32[]{:S(2)}) collective-permute-start(bf16[128,1024]{1,0:T(8,128)(2,1)} %collective-permute-done.10.refs_2_), channel_id=1, source_target_pairs={{0,4},{4,0},{8,12},{12,8},{16,20},{20,16},{24,28},{28,24},{1,5},{5... | collective-permute-start | bytes 786440 | tf_op jit(solution)/shard_map/ppermute | solution.py:218
  93.7 0.7 collective-permute-start.17
  94.5 1.1 unfold.1.refs_8_
  95.6 9.8 %collective-permute-done.12.refs_3_ = bf16[128,1024]{1,0:T(8,128)(2,1)S(1)} collective-permute-done((bf16[128,1024]{1,0:T(8,128)(2,1)}, bf16[128,1024]{1,0:T(8,128)(2,1)S(1)}, u32[]{:S(2)}, u32[]{:S(2)}) %collective-permute-start.12) | collective-permute-done | bytes 262176 | tf_op jit(solution)/shard_map/ppermute | solution.py:218
  105.4 2.7 %product.1 = (bf16[256,1024]{1,0:T(8,128)(2,1)S(1)}, bf16[1024,1024]{1,0:T(8,128)(2,1)S(1)}, f32[8,128]{1,0:T(8,128)S(1)}) custom-call(s32[3]{0:T(128)S(1)} %pad_add_fusion.place_ref, bf16[128,1024]{1,0:T(8,128)(2,1)S(1)} %bitcast.107, bf16[128,1024]{1,0:T(8,128)(2,1)S(1)} %collective-permute-done.11.refs_1_, ...), custom_call_target="tpu_custom_call" | custom-call | flops 1073741824 | bytes 4718592 | tf_op jit(solution)/shard_map/product/pallas_call | solution.py:31
  108.1 4.0 %collective-permute-start.22 = (bf16[2,128,1024]{2,1,0:T(8,128)(2,1)S(1)}, bf16[2,128,1024]{2,1,0:T(8,128)(2,1)S(1)}, u32[]{:S(2)}, u32[]{:S(2)}) collective-permute-start(bf16[2,128,1024]{2,1,0:T(8,128)(2,1)S(1)} %bitcast.113), channel_id=1, source_target_pairs={{0,16},{4,20},{8,24},{12,28},{16,0},{20,4},{24,8},{28,12},{1,17},{... | collective-permute-start | bytes 1572872 | tf_op jit(solution)/shard_map/ppermute | solution.py:218
  112.1 4.0 %collective-permute-start.24 = (bf16[2,128,1024]{2,1,0:T(8,128)(2,1)S(1)}, bf16[2,128,1024]{2,1,0:T(8,128)(2,1)S(1)}, u32[]{:S(2)}, u32[]{:S(2)}) collective-permute-start(bf16[2,128,1024]{2,1,0:T(8,128)(2,1)S(1)} %bitcast.115), channel_id=1, source_target_pairs={{0,4},{4,0},{8,12},{12,8},{16,20},{20,16},{24,28},{28,24},{1,5},{5... | collective-permute-start | bytes 1572872 | tf_op jit(solution)/shard_map/ppermute | solution.py:218
  116.2 2.1 %fusion.6 = (f32[]{:T(128)}, f32[2,128,1024]{2,1,0:T(8,128)}) fusion(bf16[1,128,1024]{2,1,0:T(8,128)(2,1)S(1)} %get-tuple-element.67, bf16[1,128,1024]{2,1,0:T(8,128)(2,1)S(1)} %get-tuple-element.66, f32[2,128,1024]{2,1,0:T(8,128)S(1)} %copy-done.19), kind=kLoop, calls=%fused_computation.25 | loop fusion | flops 2621439 | bytes 2621444 | tf_op jit(solution)/shard_map/reduce_sum | solution.py:330
  118.3 0.6 broadcast_select_fusion
  119.1 0.8 fusion
  120.2 0.6 fusion.41
  120.9 1.6 collective-permute-start.19
  122.4 0.5 convolution_bitcast_fusion.1
  122.9 1.6 collective-permute-done.19
  125.0 3.1 %collective-permute-done.20 = f32[8,128]{1,0:T(8,128)S(1)} collective-permute-done((f32[8,128]{1,0:T(8,128)S(1)}, f32[8,128]{1,0:T(8,128)S(1)}, u32[]{:S(2)}, u32[]{:S(2)}) %collective-permute-start.20) | collective-permute-done | bytes 4128 | tf_op jit(solution)/shard_map/ppermute | solution.py:218
  128.2 1.7 collective-permute-done.22
  129.8 1.1 collective-permute-done.23
  131.3 0.5 collective-permute-done.21
  131.8 2.3 %collective-permute-start.25 = (f32[8,128]{1,0:T(8,128)S(1)}, f32[8,128]{1,0:T(8,128)S(1)}, u32[]{:S(2)}, u32[]{:S(2)}) collective-permute-start(f32[8,128]{1,0:T(8,128)S(1)} %add.92), channel_id=1, source_target_pairs={{0,16},{4,20},{8,24},{12,28},{16,0},{20,4},{24,8},{28,12},{1,17},{... | collective-permute-start | bytes 12296 | tf_op jit(solution)/shard_map/ppermute | solution.py:218
  134.1 1.3 collective-permute-start.27
  135.4 0.6 collective-permute-start.28
  136.0 1.8 %collective-permute-start.29 = (bf16[2,128,1024]{2,1,0:T(8,128)(2,1)S(1)}, bf16[2,128,1024]{2,1,0:T(8,128)(2,1)S(1)}, u32[]{:S(2)}, u32[]{:S(2)}) collective-permute-start(bf16[2,128,1024]{2,1,0:T(8,128)(2,1)S(1)} %pad_maximum_fusion.4), channel_id=1, source_target_pairs={{0,16},{4,20},{8,24},{12,28},{16,0},{20,4},{24,8},{28,12},{1,17},{... | collective-permute-start | bytes 1572872 | tf_op jit(solution)/shard_map/ppermute | solution.py:218
  137.9 0.6 fusion.37
  139.8 0.5 broadcast_in_dim.27
  140.7 24.4 %collective-permute-done.26 = bf16[2,2,128,1024]{3,2,1,0:T(8,128)(2,1)S(1)} collective-permute-done((bf16[2,2,128,1024]{3,2,1,0:T(8,128)(2,1)S(1)}, bf16[2,2,128,1024]{3,2,1,0:T(8,128)(2,1)S(1)}, u32[]{:S(2)}, u32[]{:S(2)}) %collective-permute-start.26) | collective-permute-done | bytes 1048608 | tf_op jit(solution)/shard_map/ppermute | solution.py:218
  165.6 1.6 collective-permute-done.28
  168.0 1.7 fusion.4
  169.7 1.2 fusion.5
  (86 shorter events, 3.9 us)
Async XLA Ops:
  0.6 7.6 %copy-start.6 = (bf16[2,128,1024]{2,1,0:T(8,128)(2,1)S(1)}, bf16[2,128,1024]{2,1,0:T(8,128)(2,1)}, u32[]{:S(2)}) copy-start(bf16[2,128,1024]{2,1,0:T(8,128)(2,1)} %own_ref.1) | copy-start | bytes 1572868
  3.6 33.4 %collective-permute-start = (bf16[4,128,1024]{2,1,0:T(8,128)(2,1)}, bf16[4,128,1024]{2,1,0:T(8,128)(2,1)S(1)}, u32[]{:S(2)}, u32[]{:S(2)}) collective-permute-start(bf16[4,128,1024]{2,1,0:T(8,128)(2,1)} %get-tuple-element.32), channel_id=1, source_target_pairs={{0,4},{4,0},{8,12},{12,8},{16,20},{20,16},{24,28},{28,24},{1,5},{5... | collective-permute-start | bytes 3145736 | tf_op jit(solution)/shard_map/ppermute | solution.py:218
  6.6 35.7 %collective-permute-start.3 = (bf16[4,128,1024]{2,1,0:T(8,128)(2,1)}, bf16[4,128,1024]{2,1,0:T(8,128)(2,1)S(1)}, u32[]{:S(2)}, u32[]{:S(2)}) collective-permute-start(bf16[4,128,1024]{2,1,0:T(8,128)(2,1)} %get-tuple-element.33), channel_id=1, source_target_pairs={{0,8},{4,12},{8,0},{12,4},{16,24},{20,28},{24,16},{28,20},{1,9},{5... | collective-permute-start | bytes 3145736 | tf_op jit(solution)/shard_map/ppermute | solution.py:218
  8.9 27.3 %collective-permute-start.1 = (bf16[128,1024]{1,0:T(8,128)(2,1)}, bf16[128,1024]{1,0:T(8,128)(2,1)S(1)}, u32[]{:S(2)}, u32[]{:S(2)}) collective-permute-start(bf16[128,1024]{1,0:T(8,128)(2,1)} %dynamic-slice_bitcast_fusion.1), channel_id=1, source_target_pairs={{0,16},{4,20},{8,24},{12,28},{16,0},{20,4},{24,8},{28,12},{1,17},{... | collective-permute-start | bytes 786440 | tf_op jit(solution)/shard_map/ppermute | solution.py:218
  11.5 2.2 %copy-start = (bf16[1,2,1024,1024]{3,2,1,0:T(8,128)(2,1)S(1)}, bf16[1,2,1024,1024]{3,2,1,0:T(8,128)(2,1)}, u32[]{:S(2)}) copy-start(bf16[1,2,1024,1024]{3,2,1,0:T(8,128)(2,1)} %param.6) | copy-start | bytes 12582916
  13.9 1.0 copy-start.1
  36.3 0.7 copy-start.14
  37.0 1.2 copy-start.2
  38.2 5.4 %copy-start.20 = (bf16[2,128,1024]{2,1,0:T(8,128)(2,1)S(1)}, bf16[2,128,1024]{2,1,0:T(8,128)(2,1)}, u32[]{:S(2)}) copy-start(bf16[2,128,1024]{2,1,0:T(8,128)(2,1)} %param.9) | copy-start | bytes 1572868
  38.2 5.5 %copy-start.7 = (bf16[2,128,1024]{2,1,0:T(8,128)(2,1)S(1)}, bf16[2,128,1024]{2,1,0:T(8,128)(2,1)}, u32[]{:S(2)}) copy-start(bf16[2,128,1024]{2,1,0:T(8,128)(2,1)} %own_ref.1) | copy-start | bytes 1572868
  38.2 5.5 %copy-start.15 = (bf16[128,1024]{1,0:T(8,128)(2,1)S(1)}, bf16[128,1024]{1,0:T(8,128)(2,1)}, u32[]{:S(2)}) copy-start(bf16[128,1024]{1,0:T(8,128)(2,1)} %copy-done.14) | copy-start | bytes 786436
  38.2 20.5 %copy-start.3 = (bf16[4,128,1024]{2,1,0:T(8,128)(2,1)S(1)}, bf16[4,128,1024]{2,1,0:T(8,128)(2,1)}, u32[]{:S(2)}) copy-start(bf16[4,128,1024]{2,1,0:T(8,128)(2,1)} %copy-done.1) | copy-start | bytes 3145732
  38.9 19.8 %collective-permute-start.2 = (bf16[2,128,1024]{2,1,0:T(8,128)(2,1)S(1)}, bf16[2,128,1024]{2,1,0:T(8,128)(2,1)S(1)}, u32[]{:S(2)}, u32[]{:S(2)}) collective-permute-start(bf16[2,128,1024]{2,1,0:T(8,128)(2,1)S(1)} %sum_pieces.6), channel_id=1, source_target_pairs={{0,8},{4,12},{8,0},{12,4},{16,24},{20,28},{24,16},{28,20},{1,9},{5... | collective-permute-start | bytes 1572872 | tf_op jit(solution)/shard_map/ppermute | solution.py:218
  43.0 15.7 %collective-permute-start.4 = (bf16[2,128,1024]{2,1,0:T(8,128)(2,1)S(1)}, bf16[2,128,1024]{2,1,0:T(8,128)(2,1)S(1)}, u32[]{:S(2)}, u32[]{:S(2)}) collective-permute-start(bf16[2,128,1024]{2,1,0:T(8,128)(2,1)S(1)} %sum_pieces.7), channel_id=1, source_target_pairs={{0,4},{4,0},{8,12},{12,8},{16,20},{20,16},{24,28},{28,24},{1,5},{5... | collective-permute-start | bytes 1572872 | tf_op jit(solution)/shard_map/ppermute | solution.py:218
  43.6 14.3 %collective-permute-start.5 = (bf16[128,1024]{1,0:T(8,128)(2,1)S(1)}, bf16[128,1024]{1,0:T(8,128)(2,1)S(1)}, u32[]{:S(2)}, u32[]{:S(2)}) collective-permute-start(bf16[128,1024]{1,0:T(8,128)(2,1)S(1)} %dynamic-slice_bitcast_fusion), channel_id=1, source_target_pairs={{0,16},{4,20},{8,24},{12,28},{16,0},{20,4},{24,8},{28,12},{1,17},{... | collective-permute-start | bytes 786440 | tf_op jit(solution)/shard_map/ppermute | solution.py:218
  44.4 28.8 %copy-start.8 = (bf16[2,128,1024]{2,1,0:T(8,128)(2,1)}, bf16[2,128,1024]{2,1,0:T(8,128)(2,1)S(1)}, u32[]{:S(2)}) copy-start(bf16[2,128,1024]{2,1,0:T(8,128)(2,1)S(1)} %get-tuple-element.46.pair_ref) | copy-start | bytes 1572868
  58.0 15.2 %copy-start.21 = (bf16[128,1024]{1,0:T(8,128)(2,1)}, bf16[128,1024]{1,0:T(8,128)(2,1)S(1)}, u32[]{:S(2)}) copy-start(bf16[128,1024]{1,0:T(8,128)(2,1)S(1)} %collective-permute-done.5) | copy-start | bytes 786436
  58.7 14.5 %copy-start.4 = (bf16[2,128,1024]{2,1,0:T(8,128)(2,1)}, bf16[2,128,1024]{2,1,0:T(8,128)(2,1)S(1)}, u32[]{:S(2)}) copy-start(bf16[2,128,1024]{2,1,0:T(8,128)(2,1)S(1)} %collective-permute-done.4.refs_2_) | copy-start | bytes 1572868
  59.4 17.1 %collective-permute-start.8 = (bf16[9,128,128]{2,1,0:T(8,128)(2,1)S(1)}, bf16[9,128,128]{2,1,0:T(8,128)(2,1)S(1)}, u32[]{:S(2)}, u32[]{:S(2)}) collective-permute-start(bf16[9,128,128]{2,1,0:T(8,128)(2,1)S(1)} %get-tuple-element.43), channel_id=1, source_target_pairs={{0,8},{4,12},{8,0},{12,4},{16,24},{20,28},{24,16},{28,20},{1,9},{5... | collective-permute-start | bytes 884744 | tf_op jit(solution)/shard_map/ppermute | solution.py:218
  61.1 15.4 %collective-permute-start.9 = (bf16[9,128,128]{2,1,0:T(8,128)(2,1)S(1)}, bf16[9,128,128]{2,1,0:T(8,128)(2,1)S(1)}, u32[]{:S(2)}, u32[]{:S(2)}) collective-permute-start(bf16[9,128,128]{2,1,0:T(8,128)(2,1)S(1)} %get-tuple-element.43), channel_id=1, source_target_pairs={{0,4},{4,0},{8,12},{12,8},{16,20},{20,16},{24,28},{28,24},{1,5},{5... | collective-permute-start | bytes 884744 | tf_op jit(solution)/shard_map/ppermute | solution.py:218
  61.6 9.6 %collective-permute-start.6 = (bf16[128,1024]{1,0:T(8,128)(2,1)S(1)}, bf16[128,1024]{1,0:T(8,128)(2,1)S(1)}, u32[]{:S(2)}, u32[]{:S(2)}) collective-permute-start(bf16[128,1024]{1,0:T(8,128)(2,1)S(1)} %bitcast.117), channel_id=1, source_target_pairs={{0,16},{4,20},{8,24},{12,28},{16,0},{20,4},{24,8},{28,12},{1,17},{... | collective-permute-start | bytes 786440 | tf_op jit(solution)/shard_map/ppermute | solution.py:218
  73.2 21.2 %copy-start.9 = (bf16[2,128,1024]{2,1,0:T(8,128)(2,1)S(1)}, bf16[2,128,1024]{2,1,0:T(8,128)(2,1)}, u32[]{:S(2)}) copy-start(bf16[2,128,1024]{2,1,0:T(8,128)(2,1)} %copy-done.8) | copy-start | bytes 1572868
  73.2 12.2 %collective-permute-start.7 = (bf16[128,1024]{1,0:T(8,128)(2,1)}, bf16[128,1024]{1,0:T(8,128)(2,1)}, u32[]{:S(2)}, u32[]{:S(2)}) collective-permute-start(bf16[128,1024]{1,0:T(8,128)(2,1)} %bitcast.9), channel_id=1, source_target_pairs={{0,16},{4,20},{8,24},{12,28},{16,0},{20,4},{24,8},{28,12},{1,17},{... | collective-permute-start | bytes 786440 | tf_op jit(solution)/shard_map/ppermute | solution.py:218
  76.5 0.7 copy-start.10
  77.2 0.7 copy-start.12
  77.9 9.7 %collective-permute-start.11 = (bf16[128,1024]{1,0:T(8,128)(2,1)S(1)}, bf16[128,1024]{1,0:T(8,128)(2,1)S(1)}, u32[]{:S(2)}, u32[]{:S(2)}) collective-permute-start(bf16[128,1024]{1,0:T(8,128)(2,1)S(1)} %bitcast.105), channel_id=1, source_target_pairs={{0,4},{4,0},{8,12},{12,8},{16,20},{20,16},{24,28},{28,24},{1,5},{5... | collective-permute-start | bytes 786440 | tf_op jit(solution)/shard_map/ppermute | solution.py:218
  79.2 15.3 %copy-start.11 = (bf16[9,128,128]{2,1,0:T(8,128)(2,1)S(1)}, bf16[9,128,128]{2,1,0:T(8,128)(2,1)}, u32[]{:S(2)}) copy-start(bf16[9,128,128]{2,1,0:T(8,128)(2,1)} %copy-done.10) | copy-start | bytes 884740
  79.2 8.6 %collective-permute-start.10 = (bf16[128,1024]{1,0:T(8,128)(2,1)S(1)}, bf16[128,1024]{1,0:T(8,128)(2,1)}, u32[]{:S(2)}, u32[]{:S(2)}) collective-permute-start(bf16[128,1024]{1,0:T(8,128)(2,1)S(1)} %bitcast.106), channel_id=1, source_target_pairs={{0,8},{4,12},{8,0},{12,4},{16,24},{20,28},{24,16},{28,20},{1,9},{5... | collective-permute-start | bytes 786440 | tf_op jit(solution)/shard_map/ppermute | solution.py:218
  81.6 12.0 %collective-permute-start.16 = (bf16[9,128,128]{2,1,0:T(8,128)(2,1)}, bf16[9,128,128]{2,1,0:T(8,128)(2,1)S(1)}, u32[]{:S(2)}, u32[]{:S(2)}) collective-permute-start(bf16[9,128,128]{2,1,0:T(8,128)(2,1)} %copy-done.10), channel_id=1, source_target_pairs={{0,4},{4,0},{8,12},{12,8},{16,20},{20,16},{24,28},{28,24},{1,5},{5... | collective-permute-start | bytes 884744 | tf_op jit(solution)/shard_map/ppermute | solution.py:218
  85.4 1.0 copy-start.5
  86.5 8.0 %copy-start.13 = (bf16[9,128,128]{2,1,0:T(8,128)(2,1)S(1)}, bf16[9,128,128]{2,1,0:T(8,128)(2,1)}, u32[]{:S(2)}) copy-start(bf16[9,128,128]{2,1,0:T(8,128)(2,1)} %copy-done.12) | copy-start | bytes 884740
  87.7 17.7 %collective-permute-start.13 = (bf16[128,1024]{1,0:T(8,128)(2,1)S(1)}, bf16[128,1024]{1,0:T(8,128)(2,1)S(1)}, u32[]{:S(2)}, u32[]{:S(2)}) collective-permute-start(bf16[128,1024]{1,0:T(8,128)(2,1)S(1)} %bitcast.108), channel_id=1, source_target_pairs={{0,4},{4,0},{8,12},{12,8},{16,20},{20,16},{24,28},{28,24},{1,5},{5... | collective-permute-start | bytes 786440 | tf_op jit(solution)/shard_map/ppermute | solution.py:234
  90.1 15.4 %collective-permute-start.14 = (bf16[128,1024]{1,0:T(8,128)(2,1)S(1)}, bf16[128,1024]{1,0:T(8,128)(2,1)S(1)}, u32[]{:S(2)}, u32[]{:S(2)}) collective-permute-start(bf16[128,1024]{1,0:T(8,128)(2,1)S(1)} %bitcast.109), channel_id=1, source_target_pairs={{0,8},{4,12},{8,0},{12,4},{16,24},{20,28},{24,16},{28,20},{1,9},{5... | collective-permute-start | bytes 786440 | tf_op jit(solution)/shard_map/ppermute | solution.py:234
  90.3 15.1 %collective-permute-start.15 = (bf16[128,1024]{1,0:T(8,128)(2,1)S(1)}, bf16[128,1024]{1,0:T(8,128)(2,1)S(1)}, u32[]{:S(2)}, u32[]{:S(2)}) collective-permute-start(bf16[128,1024]{1,0:T(8,128)(2,1)S(1)} %bitcast.110), channel_id=1, source_target_pairs={{0,12},{4,8},{8,4},{12,0},{16,28},{20,24},{24,20},{28,16},{1,13},{... | collective-permute-start | bytes 786440 | tf_op jit(solution)/shard_map/ppermute | solution.py:234
  91.8 13.6 %collective-permute-start.12 = (bf16[128,1024]{1,0:T(8,128)(2,1)}, bf16[128,1024]{1,0:T(8,128)(2,1)S(1)}, u32[]{:S(2)}, u32[]{:S(2)}) collective-permute-start(bf16[128,1024]{1,0:T(8,128)(2,1)} %collective-permute-done.10.refs_2_), channel_id=1, source_target_pairs={{0,4},{4,0},{8,12},{12,8},{16,20},{20,16},{24,28},{28,24},{1,5},{5... | collective-permute-start | bytes 786440 | tf_op jit(solution)/shard_map/ppermute | solution.py:218
  93.7 22.5 %collective-permute-start.17 = (bf16[128,1024]{1,0:T(8,128)(2,1)S(1)}, bf16[128,1024]{1,0:T(8,128)(2,1)S(1)}, u32[]{:S(2)}, u32[]{:S(2)}) collective-permute-start(bf16[128,1024]{1,0:T(8,128)(2,1)S(1)} %fusion.27), channel_id=1, source_target_pairs={{0,16},{4,20},{8,24},{12,28},{16,0},{20,4},{24,8},{28,12},{1,17},{... | collective-permute-start | bytes 786440 | tf_op jit(solution)/shard_map/ppermute | solution.py:218
  94.5 21.7 %copy-start.19 = (f32[2,128,1024]{2,1,0:T(8,128)S(1)}, f32[2,128,1024]{2,1,0:T(8,128)}, u32[]{:S(2)}) copy-start(f32[2,128,1024]{2,1,0:T(8,128)} %param.11) | copy-start | bytes 3145732
  108.1 21.7 %collective-permute-start.22 = (bf16[2,128,1024]{2,1,0:T(8,128)(2,1)S(1)}, bf16[2,128,1024]{2,1,0:T(8,128)(2,1)S(1)}, u32[]{:S(2)}, u32[]{:S(2)}) collective-permute-start(bf16[2,128,1024]{2,1,0:T(8,128)(2,1)S(1)} %bitcast.113), channel_id=1, source_target_pairs={{0,16},{4,20},{8,24},{12,28},{16,0},{20,4},{24,8},{28,12},{1,17},{... | collective-permute-start | bytes 1572872 | tf_op jit(solution)/shard_map/ppermute | solution.py:218
  112.1 18.9 %collective-permute-start.23 = (bf16[2,128,1024]{2,1,0:T(8,128)(2,1)S(1)}, bf16[2,128,1024]{2,1,0:T(8,128)(2,1)S(1)}, u32[]{:S(2)}, u32[]{:S(2)}) collective-permute-start(bf16[2,128,1024]{2,1,0:T(8,128)(2,1)S(1)} %bitcast.114), channel_id=1, source_target_pairs={{0,8},{4,12},{8,0},{12,4},{16,24},{20,28},{24,16},{28,20},{1,9},{5... | collective-permute-start | bytes 1572872 | tf_op jit(solution)/shard_map/ppermute | solution.py:218
  112.1 18.9 %collective-permute-start.24 = (bf16[2,128,1024]{2,1,0:T(8,128)(2,1)S(1)}, bf16[2,128,1024]{2,1,0:T(8,128)(2,1)S(1)}, u32[]{:S(2)}, u32[]{:S(2)}) collective-permute-start(bf16[2,128,1024]{2,1,0:T(8,128)(2,1)S(1)} %bitcast.115), channel_id=1, source_target_pairs={{0,4},{4,0},{8,12},{12,8},{16,20},{20,16},{24,28},{28,24},{1,5},{5... | collective-permute-start | bytes 1572872 | tf_op jit(solution)/shard_map/ppermute | solution.py:218
  119.0 1.2 collective-permute-start.18
  120.9 3.7 %collective-permute-start.19 = (f32[8,128]{1,0:T(8,128)S(1)}, f32[8,128]{1,0:T(8,128)S(1)}, u32[]{:S(2)}, u32[]{:S(2)}) collective-permute-start(f32[8,128]{1,0:T(8,128)S(1)} %fusion.41), channel_id=1, source_target_pairs={{0,2},{1,3},{2,0},{3,1},{4,6},{5,7},{6,4},{7,5},{8,10},{9,11},{10,... | collective-permute-start | bytes 12296 | tf_op jit(solution)/shard_map/ppermute | solution.py:335
  124.6 3.6 %collective-permute-start.20 = (f32[8,128]{1,0:T(8,128)S(1)}, f32[8,128]{1,0:T(8,128)S(1)}, u32[]{:S(2)}, u32[]{:S(2)}) collective-permute-start(f32[8,128]{1,0:T(8,128)S(1)} %add.90), channel_id=1, source_target_pairs={{0,4},{4,0},{8,12},{12,8},{16,20},{20,16},{24,28},{28,24},{1,5},{5... | collective-permute-start | bytes 12296 | tf_op jit(solution)/shard_map/ppermute | solution.py:218
  128.2 3.6 %collective-permute-start.21 = (f32[8,128]{1,0:T(8,128)S(1)}, f32[8,128]{1,0:T(8,128)S(1)}, u32[]{:S(2)}, u32[]{:S(2)}) collective-permute-start(f32[8,128]{1,0:T(8,128)S(1)} %add.91), channel_id=1, source_target_pairs={{0,8},{4,12},{8,0},{12,4},{16,24},{20,28},{24,16},{28,20},{1,9},{5... | collective-permute-start | bytes 12296 | tf_op jit(solution)/shard_map/ppermute | solution.py:218
  131.1 34.1 %collective-permute-start.26 = (bf16[2,2,128,1024]{3,2,1,0:T(8,128)(2,1)S(1)}, bf16[2,2,128,1024]{3,2,1,0:T(8,128)(2,1)S(1)}, u32[]{:S(2)}, u32[]{:S(2)}) collective-permute-start(bf16[2,2,128,1024]{3,2,1,0:T(8,128)(2,1)S(1)} %pad_maximum_fusion), channel_id=1, source_target_pairs={{0,4},{4,0},{8,12},{12,8},{16,20},{20,16},{24,28},{28,24},{1,5},{5... | collective-permute-start | bytes 3145736 | tf_op jit(solution)/shard_map/ppermute | solution.py:218
  131.8 6.1 %collective-permute-start.25 = (f32[8,128]{1,0:T(8,128)S(1)}, f32[8,128]{1,0:T(8,128)S(1)}, u32[]{:S(2)}, u32[]{:S(2)}) collective-permute-start(f32[8,128]{1,0:T(8,128)S(1)} %add.92), channel_id=1, source_target_pairs={{0,16},{4,20},{8,24},{12,28},{16,0},{20,4},{24,8},{28,12},{1,17},{... | collective-permute-start | bytes 12296 | tf_op jit(solution)/shard_map/ppermute | solution.py:218
  134.1 31.3 %collective-permute-start.27 = (bf16[2,128,1024]{2,1,0:T(8,128)(2,1)S(1)}, bf16[2,128,1024]{2,1,0:T(8,128)(2,1)S(1)}, u32[]{:S(2)}, u32[]{:S(2)}) collective-permute-start(bf16[2,128,1024]{2,1,0:T(8,128)(2,1)S(1)} %collective-permute-done.22), channel_id=1, source_target_pairs={{0,12},{4,8},{8,4},{12,0},{16,28},{20,24},{24,20},{28,16},{1,13},{... | collective-permute-start | bytes 1572872 | tf_op jit(solution)/shard_map/ppermute | solution.py:361
  135.4 31.8 %collective-permute-start.28 = (bf16[2,128,1024]{2,1,0:T(8,128)(2,1)S(1)}, bf16[2,128,1024]{2,1,0:T(8,128)(2,1)S(1)}, u32[]{:S(2)}, u32[]{:S(2)}) collective-permute-start(bf16[2,128,1024]{2,1,0:T(8,128)(2,1)S(1)} %collective-permute-done.22), channel_id=1, source_target_pairs={{0,8},{4,12},{8,0},{12,4},{16,24},{20,28},{24,16},{28,20},{1,9},{5... | collective-permute-start | bytes 1572872 | tf_op jit(solution)/shard_map/ppermute | solution.py:361
  136.0 31.6 %collective-permute-start.29 = (bf16[2,128,1024]{2,1,0:T(8,128)(2,1)S(1)}, bf16[2,128,1024]{2,1,0:T(8,128)(2,1)S(1)}, u32[]{:S(2)}, u32[]{:S(2)}) collective-permute-start(bf16[2,128,1024]{2,1,0:T(8,128)(2,1)S(1)} %pad_maximum_fusion.4), channel_id=1, source_target_pairs={{0,16},{4,20},{8,24},{12,28},{16,0},{20,4},{24,8},{28,12},{1,17},{... | collective-permute-start | bytes 1572872 | tf_op jit(solution)/shard_map/ppermute | solution.py:218
  165.2 2.8 %copy-start.17 = (f32[2,128,1024]{2,1,0:T(8,128)S(1)}, f32[2,128,1024]{2,1,0:T(8,128)}, u32[]{:S(2)}) copy-start(f32[2,128,1024]{2,1,0:T(8,128)} %param.7) | copy-start | bytes 3145732
  165.6 4.1 %copy-start.18 = (f32[2,128,1024]{2,1,0:T(8,128)S(1)}, f32[2,128,1024]{2,1,0:T(8,128)}, u32[]{:S(2)}) copy-start(f32[2,128,1024]{2,1,0:T(8,128)} %param.8) | copy-start | bytes 3145732
  167.3 3.5 %copy-start.16 = (bf16[2,2,4,128,1024]{4,3,2,1,0:T(8,128)(2,1)}, bf16[2,2,4,128,1024]{4,3,2,1,0:T(8,128)(2,1)S(1)}, u32[]{:S(2)}) copy-start(bf16[2,2,4,128,1024]{4,3,2,1,0:T(8,128)(2,1)S(1)} %fusion.22) | copy-start | bytes 12582916

commit v2 on v1

--- a/solution.py
+++ b/solution.py
@@ -274,8 +274,7 @@
     reduce_step(0, 0)
     left_partner = swap(after(choose(left_root, 1 - half), terms[0][-1][0], terms[1][-1][0]), top)
     for step in range(1, bits - 1):
-        for part in range(2):
-            reduce_step(part, step, right_partner)
+        reduce_step(0, step, right_partner, reduce_step(1, step, right_partner))
     round_ends = [t[-1][0] for t in terms]
 
     halved = members == 4 and rows % 128 == 0
@@ -369,13 +368,24 @@
             scaled = (factor * piece.astype(f32)).astype(bf16)
             update = lax.dynamic_update_slice(update, scaled[None, :, None], (block, 0, member ^ k, 0, 0))
     update = update.reshape(2, width, width)
+    own_rows = [
+        stat_decay * choose(stat, half) + (1.0 - stat_decay) * choose(gram, half)
+        for stat, gram in ((left_stat, left_gram), (right_stat, right_gram))
+    ]
+    left_new, right_new = lax.optimization_barrier(
+        tuple(
+            lax.dynamic_update_slice(stat, rows_new[None], (half, 0, 0))
+            for stat, rows_new in zip((left_stat, right_stat), own_rows)
+        )
+    )
     left_partner, right_partner = after(grams_partner, update)
 
-    def new_stat(stat, gram, partner):
-        return stat_decay * stat + (1.0 - stat_decay) * by_half(choose(gram, half), partner.astype(f32))
-
-    left_new = new_stat(left_stat, left_gram, left_partner)
-    right_new = new_stat(right_stat, right_gram, right_partner)
+    def finish(new, stat, partner):
+        rows_new = stat_decay * choose(stat, 1 - half) + (1.0 - stat_decay) * partner.astype(f32)
+        return lax.dynamic_update_slice(new, rows_new[None], (1 - half, 0, 0))
+
+    left_new = finish(left_new, left_stat, left_partner)
+    right_new = finish(right_new, right_stat, right_partner)
     return (update, left_new, right_new, moment_new)
 
 

time: 171 us -> 174 us (1.018)
  waiting for transfers between devices: 91 us -> 96.8 us
  other arithmetic: 9.07 us -> 6.5 us
    ppermute x2, waiting for transfers between devices: 1.6 us -> 5.26 us  [per_device(): lax.ppermute(partner, 'dp', [(i, i ^ k) for i in range(devices)])]
    add x2 -> x0, other arithmetic: 2.85 us -> none  [new_stat(): stat_decay * stat]
    ppermute x23, waiting for transfers between devices: 87.4 us -> 89.9 us  [swap(): lax.ppermute(array, 'dp', [(i, i ^ 1 << bit) for i in range(devices)])]
    ppermute x23, starting transfers between devices: 36.7 us -> 34.7 us  [swap(): lax.ppermute(array, 'dp', [(i, i ^ 1 << bit) for i in range(devices)])]
    unnamed x44 -> x52, local copies, waits for them, and re-layouts: 7.61 us -> 8.96 us
  transfers between devices with their start and end apart: 30 -> 30, of which waited for: 16 -> 14; matrix products, arithmetic and copies ran while one was open for 6% -> 6% of each run, Pallas kernels for 5% -> 5%
where the time goes in v2:
time: 174 us
  waiting for transfers between devices  96.8 us (56%)
  starting transfers between devices  42.8 us (25%)
  Pallas kernels  12.8 us (7%)
  local copies, waits for them, and re-layouts  10.8 us (6%)
  other arithmetic  6.5 us (4%)
  between operations  2.54 us (1%)
    ppermute x23, waiting for transfers between devices, swap(): lax.ppermute(array, 'dp', [(i, i ^ 1 << bit) for i in range(devices)])  89.9 us
    ppermute x23, starting transfers between devices, swap(): lax.ppermute(array, 'dp', [(i, i ^ 1 << bit) for i in range(devices)])  34.7 us
    pallas_call x9, Pallas kernels, run(): pl.pallas_call(kernel, out_shape=out_shape, in_specs=[SMEM] + [VMEM] * le...  9.62 us
    unnamed x52, local copies, waits for them, and re-layouts  8.96 us
    ppermute x2, waiting for transfers between devices, per_device(): lax.ppermute(partner, 'dp', [(i, i ^ k) for i in range(devices)])  5.26 us
    ppermute x3, starting transfers between devices, gather_direct(): pieces[k] = lax.ppermute(own, 'dp', [(i, i ^ k) for i in range(devices)])  3.49 us
  transfers between devices with their start and end apart: 30, of which 14 were waited for; matrix products, arithmetic and copies ran while one was open for 6% of the time, Pallas kernels for 5%

profile of v2, /device:TPU:0, one launch (start us, length us, event | category | flops | bytes accessed | tf_op | source)
XLA Modules:
  0.0 173.9 jit_solution(11082666438953918640)
XLA Ops:
  0.6 3.0 %cut.2 = (bf16[4,128,1024]{2,1,0:T(8,128)(2,1)}, bf16[4,128,1024]{2,1,0:T(8,128)(2,1)}) custom-call(bf16[2,2,4,128,1024]{4,3,2,1,0:T(8,128)(2,1)} %bitcast.103), custom_call_target="tpu_custom_call" | custom-call | bytes 4194304 | tf_op jit(solution)/shard_map/cut/pallas_call | solution.py:69
  3.6 3.1 %collective-permute-start.2 = (bf16[4,128,1024]{2,1,0:T(8,128)(2,1)}, bf16[4,128,1024]{2,1,0:T(8,128)(2,1)S(1)}, u32[]{:S(2)}, u32[]{:S(2)}) collective-permute-start(bf16[4,128,1024]{2,1,0:T(8,128)(2,1)} %get-tuple-element.35), channel_id=1, source_target_pairs={{0,8},{4,12},{8,0},{12,4},{16,24},{20,28},{24,16},{28,20},{1,9},{5... | collective-permute-start | bytes 3145736 | tf_op jit(solution)/shard_map/ppermute | solution.py:218
  6.7 1.5 collective-permute-start
  8.2 0.7 dynamic-slice_bitcast_fusion.1
  8.9 2.6 %collective-permute-start.1 = (bf16[128,1024]{1,0:T(8,128)(2,1)}, bf16[128,1024]{1,0:T(8,128)(2,1)S(1)}, u32[]{:S(2)}, u32[]{:S(2)}) collective-permute-start(bf16[128,1024]{1,0:T(8,128)(2,1)} %dynamic-slice_bitcast_fusion.1), channel_id=1, source_target_pairs={{0,16},{4,20},{8,24},{12,28},{16,0},{20,4},{24,8},{28,12},{1,17},{... | collective-permute-start | bytes 786440 | tf_op jit(solution)/shard_map/ppermute | solution.py:218
  11.5 2.2 %copy-done = bf16[1,2,1024,1024]{3,2,1,0:T(8,128)(2,1)S(1)} copy-done((bf16[1,2,1024,1024]{3,2,1,0:T(8,128)(2,1)S(1)}, bf16[1,2,1024,1024]{3,2,1,0:T(8,128)(2,1)}, u32[]{:S(2)}) %copy-start) | copy-done | bytes 4194328
  14.0 1.0 copy-done.1
  15.0 20.0 %collective-permute-done.1.partner_ref = bf16[128,1024]{1,0:T(8,128)(2,1)S(1)} collective-permute-done((bf16[128,1024]{1,0:T(8,128)(2,1)}, bf16[128,1024]{1,0:T(8,128)(2,1)S(1)}, u32[]{:S(2)}, u32[]{:S(2)}) %collective-permute-start.1) | collective-permute-done | bytes 262176 | tf_op jit(solution)/shard_map/ppermute | solution.py:218
  35.0 0.7 copy-done.14
  35.7 0.7 sum_pieces.6
  36.4 1.2 copy-done.2
  37.7 0.7 sum_pieces.7
  38.3 3.5 %collective-permute-start.3 = (bf16[2,128,1024]{2,1,0:T(8,128)(2,1)S(1)}, bf16[2,128,1024]{2,1,0:T(8,128)(2,1)S(1)}, u32[]{:S(2)}, u32[]{:S(2)}) collective-permute-start(bf16[2,128,1024]{2,1,0:T(8,128)(2,1)S(1)} %sum_pieces.7), channel_id=1, source_target_pairs={{0,8},{4,12},{8,0},{12,4},{16,24},{20,28},{24,16},{28,20},{1,9},{5... | collective-permute-start | bytes 1572872 | tf_op jit(solution)/shard_map/ppermute | solution.py:218
  41.8 1.5 collective-permute-start.4
  43.3 0.9 collective-permute-start.5
  44.3 0.7 pack.1
  45.0 12.8 %collective-permute-done.5 = bf16[128,1024]{1,0:T(8,128)(2,1)S(1)} collective-permute-done((bf16[128,1024]{1,0:T(8,128)(2,1)S(1)}, bf16[128,1024]{1,0:T(8,128)(2,1)S(1)}, u32[]{:S(2)}, u32[]{:S(2)}) %collective-permute-start.5) | collective-permute-done | bytes 262176 | tf_op jit(solution)/shard_map/ppermute | solution.py:218
  57.7 0.7 collective-permute-done.3.refs_2_
  58.5 0.6 sum_pieces.8
  59.1 2.4 %collective-permute-start.8 = (bf16[9,128,128]{2,1,0:T(8,128)(2,1)S(1)}, bf16[9,128,128]{2,1,0:T(8,128)(2,1)S(1)}, u32[]{:S(2)}, u32[]{:S(2)}) collective-permute-start(bf16[9,128,128]{2,1,0:T(8,128)(2,1)S(1)} %get-tuple-element.45), channel_id=1, source_target_pairs={{0,8},{4,12},{8,0},{12,4},{16,24},{20,28},{24,16},{28,20},{1,9},{5... | collective-permute-start | bytes 884744 | tf_op jit(solution)/shard_map/ppermute | solution.py:218
  61.6 1.5 collective-permute-start.9
  63.1 1.1 collective-permute-start.6
  64.2 11.4 %collective-permute-done.6 = bf16[128,1024]{1,0:T(8,128)(2,1)S(1)} collective-permute-done((bf16[128,1024]{1,0:T(8,128)(2,1)S(1)}, bf16[128,1024]{1,0:T(8,128)(2,1)S(1)}, u32[]{:S(2)}, u32[]{:S(2)}) %collective-permute-start.6) | collective-permute-done | bytes 262176 | tf_op jit(solution)/shard_map/ppermute | solution.py:218
  75.6 0.7 sum_pieces.9
  76.3 1.3 sum_pieces.10
  77.7 0.7 copy-done.10
  78.4 0.7 copy-done.12
  79.1 1.0 collective-permute-start.11
  80.2 2.2 %collective-permute-start.10 = (bf16[128,1024]{1,0:T(8,128)(2,1)S(1)}, bf16[128,1024]{1,0:T(8,128)(2,1)}, u32[]{:S(2)}, u32[]{:S(2)}) collective-permute-start(bf16[128,1024]{1,0:T(8,128)(2,1)S(1)} %bitcast.106), channel_id=1, source_target_pairs={{0,8},{4,12},{8,0},{12,4},{16,24},{20,28},{24,16},{28,20},{1,9},{5... | collective-permute-start | bytes 786440 | tf_op jit(solution)/shard_map/ppermute | solution.py:218
  82.4 1.5 collective-permute-start.16
  84.0 1.1 fusion.31
  85.0 2.8 %collective-permute-done.7 = bf16[128,1024]{1,0:T(8,128)(2,1)} collective-permute-done((bf16[128,1024]{1,0:T(8,128)(2,1)}, bf16[128,1024]{1,0:T(8,128)(2,1)}, u32[]{:S(2)}, u32[]{:S(2)}) %collective-permute-start.7) | collective-permute-done | bytes 262176 | tf_op jit(solution)/shard_map/ppermute | solution.py:218
  87.8 1.1 sum_pieces.11
  89.0 0.9 collective-permute-done.10.refs_2_
  89.8 0.4 collective-permute-start.13
  90.2 2.4 %collective-permute-start.14 = (bf16[128,1024]{1,0:T(8,128)(2,1)S(1)}, bf16[128,1024]{1,0:T(8,128)(2,1)S(1)}, u32[]{:S(2)}, u32[]{:S(2)}) collective-permute-start(bf16[128,1024]{1,0:T(8,128)(2,1)S(1)} %bitcast.109), channel_id=1, source_target_pairs={{0,8},{4,12},{8,0},{12,4},{16,24},{20,28},{24,16},{28,20},{1,9},{5... | collective-permute-start | bytes 786440 | tf_op jit(solution)/shard_map/ppermute | solution.py:234
  92.5 0.8 collective-permute-start.15
  93.3 0.7 collective-permute-start.12
  94.1 2.3 %collective-permute-done.16.refs_2_ = bf16[9,128,128]{2,1,0:T(8,128)(2,1)S(1)} collective-permute-done((bf16[9,128,128]{2,1,0:T(8,128)(2,1)}, bf16[9,128,128]{2,1,0:T(8,128)(2,1)S(1)}, u32[]{:S(2)}, u32[]{:S(2)}) %collective-permute-start.16) | collective-permute-done | bytes 294944 | tf_op jit(solution)/shard_map/ppermute | solution.py:218
  96.6 1.1 unfold.1.refs_8_
  97.7 8.8 %collective-permute-done.12.refs_3_ = bf16[128,1024]{1,0:T(8,128)(2,1)S(1)} collective-permute-done((bf16[128,1024]{1,0:T(8,128)(2,1)}, bf16[128,1024]{1,0:T(8,128)(2,1)S(1)}, u32[]{:S(2)}, u32[]{:S(2)}) %collective-permute-start.12) | collective-permute-done | bytes 262176 | tf_op jit(solution)/shard_map/ppermute | solution.py:218
  106.5 2.8 %product.1 = (bf16[256,1024]{1,0:T(8,128)(2,1)S(1)}, bf16[1024,1024]{1,0:T(8,128)(2,1)S(1)}, f32[8,128]{1,0:T(8,128)S(1)}) custom-call(s32[3]{0:T(128)S(1)} %pad_add_fusion.place_ref, bf16[128,1024]{1,0:T(8,128)(2,1)S(1)} %bitcast.107, bf16[128,1024]{1,0:T(8,128)(2,1)} %collective-permute-done.11.refs_1_, bf16[128,1024]{1,0:T(8,128)(2,1)} %collective-permute-done.10.refs_2_, ...), custom_call_target="tpu_custom_call" | custom-call | flops 1073741824 | bytes 4718592 | tf_op jit(solution)/shard_map/product/pallas_call | solution.py:31
  109.3 2.0 %collective-permute-start.22 = (bf16[2,128,1024]{2,1,0:T(8,128)(2,1)S(1)}, bf16[2,128,1024]{2,1,0:T(8,128)(2,1)S(1)}, u32[]{:S(2)}, u32[]{:S(2)}) collective-permute-start(bf16[2,128,1024]{2,1,0:T(8,128)(2,1)S(1)} %bitcast.113), channel_id=1, source_target_pairs={{0,16},{4,20},{8,24},{12,28},{16,0},{20,4},{24,8},{28,12},{1,17},{... | collective-permute-start | bytes 1572872 | tf_op jit(solution)/shard_map/ppermute | solution.py:218
  111.3 3.4 %collective-permute-start.23 = (bf16[2,128,1024]{2,1,0:T(8,128)(2,1)S(1)}, bf16[2,128,1024]{2,1,0:T(8,128)(2,1)S(1)}, u32[]{:S(2)}, u32[]{:S(2)}) collective-permute-start(bf16[2,128,1024]{2,1,0:T(8,128)(2,1)S(1)} %bitcast.114), channel_id=1, source_target_pairs={{0,8},{4,12},{8,0},{12,4},{16,24},{20,28},{24,16},{28,20},{1,9},{5... | collective-permute-start | bytes 1572872 | tf_op jit(solution)/shard_map/ppermute | solution.py:218
  115.0 2.1 %fusion.4 = (f32[]{:T(128)}, f32[2,128,1024]{2,1,0:T(8,128)}) fusion(bf16[1,128,1024]{2,1,0:T(8,128)(2,1)S(1)} %get-tuple-element.67, bf16[1,128,1024]{2,1,0:T(8,128)(2,1)S(1)} %get-tuple-element.66, f32[2,128,1024]{2,1,0:T(8,128)S(1)} %copy-done.23), kind=kLoop, calls=%fused_computation.21 | loop fusion | flops 2621439 | bytes 2621444 | tf_op jit(solution)/shard_map/reduce_sum | solution.py:329
  117.1 0.6 broadcast_select_fusion
  117.9 0.7 fusion
  118.6 0.5 convolution_bitcast_fusion.1
  119.1 0.7 fusion.42
  119.8 1.6 collective-permute-start.19
  121.3 0.5 convolution_bitcast_fusion
  121.8 1.6 collective-permute-done.19
  123.5 1.7 collective-permute-start.20
  125.2 0.4 fusion.26
  125.6 1.5 collective-permute-done.20
  127.1 4.4 %collective-permute-done.22 = bf16[2,128,1024]{2,1,0:T(8,128)(2,1)S(1)} collective-permute-done((bf16[2,128,1024]{2,1,0:T(8,128)(2,1)S(1)}, bf16[2,128,1024]{2,1,0:T(8,128)(2,1)S(1)}, u32[]{:S(2)}, u32[]{:S(2)}) %collective-permute-start.22) | collective-permute-done | bytes 524320 | tf_op jit(solution)/shard_map/ppermute | solution.py:218
  131.6 1.3 collective-permute-start.26
  133.0 2.3 %collective-permute-start.25 = (f32[8,128]{1,0:T(8,128)S(1)}, f32[8,128]{1,0:T(8,128)S(1)}, u32[]{:S(2)}, u32[]{:S(2)}) collective-permute-start(f32[8,128]{1,0:T(8,128)S(1)} %add.110), channel_id=1, source_target_pairs={{0,16},{4,20},{8,24},{12,28},{16,0},{20,4},{24,8},{28,12},{1,17},{... | collective-permute-start | bytes 12296 | tf_op jit(solution)/shard_map/ppermute | solution.py:218
  135.4 2.7 %collective-permute-start.27 = (bf16[2,128,1024]{2,1,0:T(8,128)(2,1)S(1)}, bf16[2,128,1024]{2,1,0:T(8,128)(2,1)S(1)}, u32[]{:S(2)}, u32[]{:S(2)}) collective-permute-start(bf16[2,128,1024]{2,1,0:T(8,128)(2,1)S(1)} %collective-permute-done.22), channel_id=1, source_target_pairs={{0,12},{4,8},{8,4},{12,0},{16,28},{20,24},{24,20},{28,16},{1,13},{... | collective-permute-start | bytes 1572872 | tf_op jit(solution)/shard_map/ppermute | solution.py:360
  138.4 0.6 fusion.38
  140.4 0.5 broadcast_in_dim.31
  141.3 24.2 %collective-permute-done.26 = bf16[2,2,128,1024]{3,2,1,0:T(8,128)(2,1)S(1)} collective-permute-done((bf16[2,2,128,1024]{3,2,1,0:T(8,128)(2,1)S(1)}, bf16[2,2,128,1024]{3,2,1,0:T(8,128)(2,1)S(1)}, u32[]{:S(2)}, u32[]{:S(2)}) %collective-permute-start.26) | collective-permute-done | bytes 1048608 | tf_op jit(solution)/shard_map/ppermute | solution.py:218
  165.9 5.3 %collective-permute-done.28 = bf16[2,128,1024]{2,1,0:T(8,128)(2,1)S(1)} collective-permute-done((bf16[2,128,1024]{2,1,0:T(8,128)(2,1)S(1)}, bf16[2,128,1024]{2,1,0:T(8,128)(2,1)S(1)}, u32[]{:S(2)}, u32[]{:S(2)}) %collective-permute-start.28) | collective-permute-done | bytes 524320 | tf_op jit(solution)/shard_map/ppermute | solution.py:360
  171.6 1.7 copy-done.16
  (93 shorter events, 3.5 us)
Async XLA Ops:
  0.6 7.6 %copy-start.6 = (bf16[2,128,1024]{2,1,0:T(8,128)(2,1)S(1)}, bf16[2,128,1024]{2,1,0:T(8,128)(2,1)}, u32[]{:S(2)}) copy-start(bf16[2,128,1024]{2,1,0:T(8,128)(2,1)} %own_ref.1) | copy-start | bytes 1572868
  3.6 32.1 %collective-permute-start.2 = (bf16[4,128,1024]{2,1,0:T(8,128)(2,1)}, bf16[4,128,1024]{2,1,0:T(8,128)(2,1)S(1)}, u32[]{:S(2)}, u32[]{:S(2)}) collective-permute-start(bf16[4,128,1024]{2,1,0:T(8,128)(2,1)} %get-tuple-element.35), channel_id=1, source_target_pairs={{0,8},{4,12},{8,0},{12,4},{16,24},{20,28},{24,16},{28,20},{1,9},{5... | collective-permute-start | bytes 3145736 | tf_op jit(solution)/shard_map/ppermute | solution.py:218
  6.7 29.7 %collective-permute-start = (bf16[4,128,1024]{2,1,0:T(8,128)(2,1)}, bf16[4,128,1024]{2,1,0:T(8,128)(2,1)S(1)}, u32[]{:S(2)}, u32[]{:S(2)}) collective-permute-start(bf16[4,128,1024]{2,1,0:T(8,128)(2,1)} %get-tuple-element.34), channel_id=1, source_target_pairs={{0,4},{4,0},{8,12},{12,8},{16,20},{20,16},{24,28},{28,24},{1,5},{5... | collective-permute-start | bytes 3145736 | tf_op jit(solution)/shard_map/ppermute | solution.py:218
  8.9 26.1 %collective-permute-start.1 = (bf16[128,1024]{1,0:T(8,128)(2,1)}, bf16[128,1024]{1,0:T(8,128)(2,1)S(1)}, u32[]{:S(2)}, u32[]{:S(2)}) collective-permute-start(bf16[128,1024]{1,0:T(8,128)(2,1)} %dynamic-slice_bitcast_fusion.1), channel_id=1, source_target_pairs={{0,16},{4,20},{8,24},{12,28},{16,0},{20,4},{24,8},{28,12},{1,17},{... | collective-permute-start | bytes 786440 | tf_op jit(solution)/shard_map/ppermute | solution.py:218
  11.5 2.2 %copy-start = (bf16[1,2,1024,1024]{3,2,1,0:T(8,128)(2,1)S(1)}, bf16[1,2,1024,1024]{3,2,1,0:T(8,128)(2,1)}, u32[]{:S(2)}) copy-start(bf16[1,2,1024,1024]{3,2,1,0:T(8,128)(2,1)} %param.6) | copy-start | bytes 12582916
  13.9 1.0 copy-start.1
  14.9 28.4 %copy-start.24 = (bf16[2,128,1024]{2,1,0:T(8,128)(2,1)S(1)}, bf16[2,128,1024]{2,1,0:T(8,128)(2,1)}, u32[]{:S(2)}) copy-start(bf16[2,128,1024]{2,1,0:T(8,128)(2,1)} %param.9) | copy-start | bytes 1572868
  14.9 29.3 %copy-start.7 = (bf16[2,128,1024]{2,1,0:T(8,128)(2,1)S(1)}, bf16[2,128,1024]{2,1,0:T(8,128)(2,1)}, u32[]{:S(2)}) copy-start(bf16[2,128,1024]{2,1,0:T(8,128)(2,1)} %own_ref.1) | copy-start | bytes 1572868
  14.9 43.5 %copy-start.3 = (bf16[4,128,1024]{2,1,0:T(8,128)(2,1)S(1)}, bf16[4,128,1024]{2,1,0:T(8,128)(2,1)}, u32[]{:S(2)}) copy-start(bf16[4,128,1024]{2,1,0:T(8,128)(2,1)} %copy-done.1) | copy-start | bytes 3145732
  35.0 0.7 copy-start.14
  35.7 8.5 %copy-start.15 = (bf16[128,1024]{1,0:T(8,128)(2,1)S(1)}, bf16[128,1024]{1,0:T(8,128)(2,1)}, u32[]{:S(2)}) copy-start(bf16[128,1024]{1,0:T(8,128)(2,1)} %copy-done.14) | copy-start | bytes 786436
  36.4 1.2 copy-start.2
  38.3 20.1 %collective-permute-start.3 = (bf16[2,128,1024]{2,1,0:T(8,128)(2,1)S(1)}, bf16[2,128,1024]{2,1,0:T(8,128)(2,1)S(1)}, u32[]{:S(2)}, u32[]{:S(2)}) collective-permute-start(bf16[2,128,1024]{2,1,0:T(8,128)(2,1)S(1)} %sum_pieces.7), channel_id=1, source_target_pairs={{0,8},{4,12},{8,0},{12,4},{16,24},{20,28},{24,16},{28,20},{1,9},{5... | collective-permute-start | bytes 1572872 | tf_op jit(solution)/shard_map/ppermute | solution.py:218
  41.8 16.7 %collective-permute-start.4 = (bf16[2,128,1024]{2,1,0:T(8,128)(2,1)S(1)}, bf16[2,128,1024]{2,1,0:T(8,128)(2,1)S(1)}, u32[]{:S(2)}, u32[]{:S(2)}) collective-permute-start(bf16[2,128,1024]{2,1,0:T(8,128)(2,1)S(1)} %sum_pieces.6), channel_id=1, source_target_pairs={{0,4},{4,0},{8,12},{12,8},{16,20},{20,16},{24,28},{28,24},{1,5},{5... | collective-permute-start | bytes 1572872 | tf_op jit(solution)/shard_map/ppermute | solution.py:218
  43.3 14.4 %collective-permute-start.5 = (bf16[128,1024]{1,0:T(8,128)(2,1)S(1)}, bf16[128,1024]{1,0:T(8,128)(2,1)S(1)}, u32[]{:S(2)}, u32[]{:S(2)}) collective-permute-start(bf16[128,1024]{1,0:T(8,128)(2,1)S(1)} %dynamic-slice_bitcast_fusion), channel_id=1, source_target_pairs={{0,16},{4,20},{8,24},{12,28},{16,0},{20,4},{24,8},{28,12},{1,17},{... | collective-permute-start | bytes 786440 | tf_op jit(solution)/shard_map/ppermute | solution.py:218
  44.9 32.7 %copy-start.8 = (bf16[2,128,1024]{2,1,0:T(8,128)(2,1)}, bf16[2,128,1024]{2,1,0:T(8,128)(2,1)S(1)}, u32[]{:S(2)}) copy-start(bf16[2,128,1024]{2,1,0:T(8,128)(2,1)S(1)} %get-tuple-element.48.pair_ref) | copy-start | bytes 1572868
  57.7 0.7 copy-start.25
  58.5 19.1 %copy-start.4 = (bf16[2,128,1024]{2,1,0:T(8,128)(2,1)}, bf16[2,128,1024]{2,1,0:T(8,128)(2,1)S(1)}, u32[]{:S(2)}) copy-start(bf16[2,128,1024]{2,1,0:T(8,128)(2,1)S(1)} %collective-permute-done.4.refs_2_) | copy-start | bytes 1572868
  59.1 18.6 %collective-permute-start.8 = (bf16[9,128,128]{2,1,0:T(8,128)(2,1)S(1)}, bf16[9,128,128]{2,1,0:T(8,128)(2,1)S(1)}, u32[]{:S(2)}, u32[]{:S(2)}) collective-permute-start(bf16[9,128,128]{2,1,0:T(8,128)(2,1)S(1)} %get-tuple-element.45), channel_id=1, source_target_pairs={{0,8},{4,12},{8,0},{12,4},{16,24},{20,28},{24,16},{28,20},{1,9},{5... | collective-permute-start | bytes 884744 | tf_op jit(solution)/shard_map/ppermute | solution.py:218
  61.6 16.2 %collective-permute-start.9 = (bf16[9,128,128]{2,1,0:T(8,128)(2,1)S(1)}, bf16[9,128,128]{2,1,0:T(8,128)(2,1)S(1)}, u32[]{:S(2)}, u32[]{:S(2)}) collective-permute-start(bf16[9,128,128]{2,1,0:T(8,128)(2,1)S(1)} %get-tuple-element.45), channel_id=1, source_target_pairs={{0,4},{4,0},{8,12},{12,8},{16,20},{20,16},{24,28},{28,24},{1,5},{5... | collective-permute-start | bytes 884744 | tf_op jit(solution)/shard_map/ppermute | solution.py:218
  63.1 12.5 %collective-permute-start.6 = (bf16[128,1024]{1,0:T(8,128)(2,1)S(1)}, bf16[128,1024]{1,0:T(8,128)(2,1)S(1)}, u32[]{:S(2)}, u32[]{:S(2)}) collective-permute-start(bf16[128,1024]{1,0:T(8,128)(2,1)S(1)} %bitcast.117), channel_id=1, source_target_pairs={{0,16},{4,20},{8,24},{12,28},{16,0},{20,4},{24,8},{28,12},{1,17},{... | collective-permute-start | bytes 786440 | tf_op jit(solution)/shard_map/ppermute | solution.py:218
  77.6 10.2 %copy-start.5 = (bf16[2,128,1024]{2,1,0:T(8,128)(2,1)S(1)}, bf16[2,128,1024]{2,1,0:T(8,128)(2,1)}, u32[]{:S(2)}) copy-start(bf16[2,128,1024]{2,1,0:T(8,128)(2,1)} %copy-done.4) | copy-start | bytes 1572868
  77.6 10.2 %collective-permute-start.7 = (bf16[128,1024]{1,0:T(8,128)(2,1)}, bf16[128,1024]{1,0:T(8,128)(2,1)}, u32[]{:S(2)}, u32[]{:S(2)}) collective-permute-start(bf16[128,1024]{1,0:T(8,128)(2,1)} %bitcast.9), channel_id=1, source_target_pairs={{0,16},{4,20},{8,24},{12,28},{16,0},{20,4},{24,8},{28,12},{1,17},{... | collective-permute-start | bytes 786440 | tf_op jit(solution)/shard_map/ppermute | solution.py:218
  77.7 0.7 copy-start.10
  78.4 0.7 copy-start.12
  79.1 9.8 %collective-permute-start.11 = (bf16[128,1024]{1,0:T(8,128)(2,1)S(1)}, bf16[128,1024]{1,0:T(8,128)(2,1)}, u32[]{:S(2)}, u32[]{:S(2)}) collective-permute-start(bf16[128,1024]{1,0:T(8,128)(2,1)S(1)} %bitcast.105), channel_id=1, source_target_pairs={{0,4},{4,0},{8,12},{12,8},{16,20},{20,16},{24,28},{28,24},{1,5},{5... | collective-permute-start | bytes 786440 | tf_op jit(solution)/shard_map/ppermute | solution.py:218
  80.2 9.7 %collective-permute-start.10 = (bf16[128,1024]{1,0:T(8,128)(2,1)S(1)}, bf16[128,1024]{1,0:T(8,128)(2,1)}, u32[]{:S(2)}, u32[]{:S(2)}) collective-permute-start(bf16[128,1024]{1,0:T(8,128)(2,1)S(1)} %bitcast.106), channel_id=1, source_target_pairs={{0,8},{4,12},{8,0},{12,4},{16,24},{20,28},{24,16},{28,20},{1,9},{5... | collective-permute-start | bytes 786440 | tf_op jit(solution)/shard_map/ppermute | solution.py:218
  82.4 14.1 %copy-start.9 = (bf16[2,128,1024]{2,1,0:T(8,128)(2,1)S(1)}, bf16[2,128,1024]{2,1,0:T(8,128)(2,1)}, u32[]{:S(2)}) copy-start(bf16[2,128,1024]{2,1,0:T(8,128)(2,1)} %copy-done.8) | copy-start | bytes 1572868
  82.4 14.1 %copy-start.11 = (bf16[9,128,128]{2,1,0:T(8,128)(2,1)S(1)}, bf16[9,128,128]{2,1,0:T(8,128)(2,1)}, u32[]{:S(2)}) copy-start(bf16[9,128,128]{2,1,0:T(8,128)(2,1)} %copy-done.10) | copy-start | bytes 884740
  82.4 14.1 %copy-start.13 = (bf16[9,128,128]{2,1,0:T(8,128)(2,1)S(1)}, bf16[9,128,128]{2,1,0:T(8,128)(2,1)}, u32[]{:S(2)}) copy-start(bf16[9,128,128]{2,1,0:T(8,128)(2,1)} %copy-done.12) | copy-start | bytes 884740
  82.4 14.0 %collective-permute-start.16 = (bf16[9,128,128]{2,1,0:T(8,128)(2,1)}, bf16[9,128,128]{2,1,0:T(8,128)(2,1)S(1)}, u32[]{:S(2)}, u32[]{:S(2)}) collective-permute-start(bf16[9,128,128]{2,1,0:T(8,128)(2,1)} %copy-done.10), channel_id=1, source_target_pairs={{0,4},{4,0},{8,12},{12,8},{16,20},{20,16},{24,28},{28,24},{1,5},{5... | collective-permute-start | bytes 884744 | tf_op jit(solution)/shard_map/ppermute | solution.py:218
  89.8 16.6 %collective-permute-start.13 = (bf16[128,1024]{1,0:T(8,128)(2,1)S(1)}, bf16[128,1024]{1,0:T(8,128)(2,1)S(1)}, u32[]{:S(2)}, u32[]{:S(2)}) collective-permute-start(bf16[128,1024]{1,0:T(8,128)(2,1)S(1)} %bitcast.108), channel_id=1, source_target_pairs={{0,4},{4,0},{8,12},{12,8},{16,20},{20,16},{24,28},{28,24},{1,5},{5... | collective-permute-start | bytes 786440 | tf_op jit(solution)/shard_map/ppermute | solution.py:234
  90.2 16.3 %collective-permute-start.14 = (bf16[128,1024]{1,0:T(8,128)(2,1)S(1)}, bf16[128,1024]{1,0:T(8,128)(2,1)S(1)}, u32[]{:S(2)}, u32[]{:S(2)}) collective-permute-start(bf16[128,1024]{1,0:T(8,128)(2,1)S(1)} %bitcast.109), channel_id=1, source_target_pairs={{0,8},{4,12},{8,0},{12,4},{16,24},{20,28},{24,16},{28,20},{1,9},{5... | collective-permute-start | bytes 786440 | tf_op jit(solution)/shard_map/ppermute | solution.py:234
  92.5 13.9 %collective-permute-start.15 = (bf16[128,1024]{1,0:T(8,128)(2,1)S(1)}, bf16[128,1024]{1,0:T(8,128)(2,1)S(1)}, u32[]{:S(2)}, u32[]{:S(2)}) collective-permute-start(bf16[128,1024]{1,0:T(8,128)(2,1)S(1)} %bitcast.110), channel_id=1, source_target_pairs={{0,12},{4,8},{8,4},{12,0},{16,28},{20,24},{24,20},{28,16},{1,13},{... | collective-permute-start | bytes 786440 | tf_op jit(solution)/shard_map/ppermute | solution.py:234
  93.3 13.2 %collective-permute-start.12 = (bf16[128,1024]{1,0:T(8,128)(2,1)}, bf16[128,1024]{1,0:T(8,128)(2,1)S(1)}, u32[]{:S(2)}, u32[]{:S(2)}) collective-permute-start(bf16[128,1024]{1,0:T(8,128)(2,1)} %collective-permute-done.10.refs_2_), channel_id=1, source_target_pairs={{0,4},{4,0},{8,12},{12,8},{16,20},{20,16},{24,28},{28,24},{1,5},{5... | collective-permute-start | bytes 786440 | tf_op jit(solution)/shard_map/ppermute | solution.py:218
  96.4 18.5 %collective-permute-start.17 = (bf16[128,1024]{1,0:T(8,128)(2,1)S(1)}, bf16[128,1024]{1,0:T(8,128)(2,1)S(1)}, u32[]{:S(2)}, u32[]{:S(2)}) collective-permute-start(bf16[128,1024]{1,0:T(8,128)(2,1)S(1)} %fusion.28), channel_id=1, source_target_pairs={{0,16},{4,20},{8,24},{12,28},{16,0},{20,4},{24,8},{28,12},{1,17},{... | collective-permute-start | bytes 786440 | tf_op jit(solution)/shard_map/ppermute | solution.py:218
  96.5 18.4 %copy-start.23 = (f32[2,128,1024]{2,1,0:T(8,128)S(1)}, f32[2,128,1024]{2,1,0:T(8,128)}, u32[]{:S(2)}) copy-start(f32[2,128,1024]{2,1,0:T(8,128)} %param.11) | copy-start | bytes 3145732
  109.3 22.2 %collective-permute-start.22 = (bf16[2,128,1024]{2,1,0:T(8,128)(2,1)S(1)}, bf16[2,128,1024]{2,1,0:T(8,128)(2,1)S(1)}, u32[]{:S(2)}, u32[]{:S(2)}) collective-permute-start(bf16[2,128,1024]{2,1,0:T(8,128)(2,1)S(1)} %bitcast.113), channel_id=1, source_target_pairs={{0,16},{4,20},{8,24},{12,28},{16,0},{20,4},{24,8},{28,12},{1,17},{... | collective-permute-start | bytes 1572872 | tf_op jit(solution)/shard_map/ppermute | solution.py:218
  111.3 20.3 %collective-permute-start.23 = (bf16[2,128,1024]{2,1,0:T(8,128)(2,1)S(1)}, bf16[2,128,1024]{2,1,0:T(8,128)(2,1)S(1)}, u32[]{:S(2)}, u32[]{:S(2)}) collective-permute-start(bf16[2,128,1024]{2,1,0:T(8,128)(2,1)S(1)} %bitcast.114), channel_id=1, source_target_pairs={{0,8},{4,12},{8,0},{12,4},{16,24},{20,28},{24,16},{28,20},{1,9},{5... | collective-permute-start | bytes 1572872 | tf_op jit(solution)/shard_map/ppermute | solution.py:218
  114.6 16.9 %collective-permute-start.24 = (bf16[2,128,1024]{2,1,0:T(8,128)(2,1)S(1)}, bf16[2,128,1024]{2,1,0:T(8,128)(2,1)S(1)}, u32[]{:S(2)}, u32[]{:S(2)}) collective-permute-start(bf16[2,128,1024]{2,1,0:T(8,128)(2,1)S(1)} %bitcast.115), channel_id=1, source_target_pairs={{0,4},{4,0},{8,12},{12,8},{16,20},{20,16},{24,28},{28,24},{1,5},{5... | collective-permute-start | bytes 1572872 | tf_op jit(solution)/shard_map/ppermute | solution.py:218
  117.8 1.3 collective-permute-start.18
  117.9 7.4 %copy-start.19 = (f32[2,128,1024]{2,1,0:T(8,128)S(1)}, f32[2,128,1024]{2,1,0:T(8,128)}, u32[]{:S(2)}) copy-start(f32[2,128,1024]{2,1,0:T(8,128)} %param.8) | copy-start | bytes 3145732
  117.9 7.3 %copy-start.22 = (f32[2,128,1024]{2,1,0:T(8,128)S(1)}, f32[2,128,1024]{2,1,0:T(8,128)}, u32[]{:S(2)}) copy-start(f32[2,128,1024]{2,1,0:T(8,128)} %param.7) | copy-start | bytes 3145732
  119.8 3.7 %collective-permute-start.19 = (f32[8,128]{1,0:T(8,128)S(1)}, f32[8,128]{1,0:T(8,128)S(1)}, u32[]{:S(2)}, u32[]{:S(2)}) collective-permute-start(f32[8,128]{1,0:T(8,128)S(1)} %fusion.42), channel_id=1, source_target_pairs={{0,2},{1,3},{2,0},{3,1},{4,6},{5,7},{6,4},{7,5},{8,10},{9,11},{10,... | collective-permute-start | bytes 12296 | tf_op jit(solution)/shard_map/ppermute | solution.py:334
  123.5 3.6 %collective-permute-start.20 = (f32[8,128]{1,0:T(8,128)S(1)}, f32[8,128]{1,0:T(8,128)S(1)}, u32[]{:S(2)}, u32[]{:S(2)}) collective-permute-start(f32[8,128]{1,0:T(8,128)S(1)} %add.108), channel_id=1, source_target_pairs={{0,4},{4,0},{8,12},{12,8},{16,20},{20,16},{24,28},{28,24},{1,5},{5... | collective-permute-start | bytes 12296 | tf_op jit(solution)/shard_map/ppermute | solution.py:218
  127.1 5.9 %collective-permute-start.21 = (f32[8,128]{1,0:T(8,128)S(1)}, f32[8,128]{1,0:T(8,128)S(1)}, u32[]{:S(2)}, u32[]{:S(2)}) collective-permute-start(f32[8,128]{1,0:T(8,128)S(1)} %add.109), channel_id=1, source_target_pairs={{0,8},{4,12},{8,0},{12,4},{16,24},{20,28},{24,16},{28,20},{1,9},{5... | collective-permute-start | bytes 12296 | tf_op jit(solution)/shard_map/ppermute | solution.py:218
  131.6 33.8 %collective-permute-start.26 = (bf16[2,2,128,1024]{3,2,1,0:T(8,128)(2,1)S(1)}, bf16[2,2,128,1024]{3,2,1,0:T(8,128)(2,1)S(1)}, u32[]{:S(2)}, u32[]{:S(2)}) collective-permute-start(bf16[2,2,128,1024]{3,2,1,0:T(8,128)(2,1)S(1)} %pad_maximum_fusion), channel_id=1, source_target_pairs={{0,4},{4,0},{8,12},{12,8},{16,20},{20,16},{24,28},{28,24},{1,5},{5... | collective-permute-start | bytes 3145736 | tf_op jit(solution)/shard_map/ppermute | solution.py:218
  133.0 5.4 %collective-permute-start.25 = (f32[8,128]{1,0:T(8,128)S(1)}, f32[8,128]{1,0:T(8,128)S(1)}, u32[]{:S(2)}, u32[]{:S(2)}) collective-permute-start(f32[8,128]{1,0:T(8,128)S(1)} %add.110), channel_id=1, source_target_pairs={{0,16},{4,20},{8,24},{12,28},{16,0},{20,4},{24,8},{28,12},{1,17},{... | collective-permute-start | bytes 12296 | tf_op jit(solution)/shard_map/ppermute | solution.py:218
  135.4 30.3 %collective-permute-start.27 = (bf16[2,128,1024]{2,1,0:T(8,128)(2,1)S(1)}, bf16[2,128,1024]{2,1,0:T(8,128)(2,1)S(1)}, u32[]{:S(2)}, u32[]{:S(2)}) collective-permute-start(bf16[2,128,1024]{2,1,0:T(8,128)(2,1)S(1)} %collective-permute-done.22), channel_id=1, source_target_pairs={{0,12},{4,8},{8,4},{12,0},{16,28},{20,24},{24,20},{28,16},{1,13},{... | collective-permute-start | bytes 1572872 | tf_op jit(solution)/shard_map/ppermute | solution.py:360
  138.2 33.0 %collective-permute-start.28 = (bf16[2,128,1024]{2,1,0:T(8,128)(2,1)S(1)}, bf16[2,128,1024]{2,1,0:T(8,128)(2,1)S(1)}, u32[]{:S(2)}, u32[]{:S(2)}) collective-permute-start(bf16[2,128,1024]{2,1,0:T(8,128)(2,1)S(1)} %collective-permute-done.22), channel_id=1, source_target_pairs={{0,8},{4,12},{8,0},{12,4},{16,24},{20,28},{24,16},{28,20},{1,9},{5... | collective-permute-start | bytes 1572872 | tf_op jit(solution)/shard_map/ppermute | solution.py:360
  138.4 32.9 %collective-permute-start.29 = (bf16[2,128,1024]{2,1,0:T(8,128)(2,1)S(1)}, bf16[2,128,1024]{2,1,0:T(8,128)(2,1)S(1)}, u32[]{:S(2)}, u32[]{:S(2)}) collective-permute-start(bf16[2,128,1024]{2,1,0:T(8,128)(2,1)S(1)} %pad_maximum_fusion.4), channel_id=1, source_target_pairs={{0,16},{4,20},{8,24},{12,28},{16,0},{20,4},{24,8},{28,12},{1,17},{... | collective-permute-start | bytes 1572872 | tf_op jit(solution)/shard_map/ppermute | solution.py:218
  140.9 30.4 %copy-start.17 = (f32[2,128,1024]{2,1,0:T(8,128)S(1)}, f32[2,128,1024]{2,1,0:T(8,128)}, u32[]{:S(2)}) copy-start(f32[2,128,1024]{2,1,0:T(8,128)} %param.8) | copy-start | bytes 3145732
  140.9 30.4 %copy-start.20 = (f32[2,128,1024]{2,1,0:T(8,128)S(1)}, f32[2,128,1024]{2,1,0:T(8,128)}, u32[]{:S(2)}) copy-start(f32[2,128,1024]{2,1,0:T(8,128)} %param.7) | copy-start | bytes 3145732
  171.3 2.0 %copy-start.16 = (bf16[2,2,4,128,1024]{4,3,2,1,0:T(8,128)(2,1)}, bf16[2,2,4,128,1024]{4,3,2,1,0:T(8,128)(2,1)S(1)}, u32[]{:S(2)}) copy-start(bf16[2,2,4,128,1024]{4,3,2,1,0:T(8,128)(2,1)S(1)} %fusion.20) | copy-start | bytes 12582916
  171.5 2.1 %copy-start.18 = (f32[2,128,1024]{2,1,0:T(8,128)}, f32[2,128,1024]{2,1,0:T(8,128)S(1)}, u32[]{:S(2)}) copy-start(f32[2,128,1024]{2,1,0:T(8,128)S(1)} %get-tuple-element.70) | copy-start | bytes 3145732
  171.5 2.4 %copy-start.21 = (f32[2,128,1024]{2,1,0:T(8,128)}, f32[2,128,1024]{2,1,0:T(8,128)S(1)}, u32[]{:S(2)}) copy-start(f32[2,128,1024]{2,1,0:T(8,128)S(1)} %get-tuple-element.71) | copy-start | bytes 3145732

commit v3 on v2

--- a/solution.py
+++ b/solution.py
@@ -274,7 +274,8 @@
     reduce_step(0, 0)
     left_partner = swap(after(choose(left_root, 1 - half), terms[0][-1][0], terms[1][-1][0]), top)
     for step in range(1, bits - 1):
-        reduce_step(0, step, right_partner, reduce_step(1, step, right_partner))
+        for part in range(2):
+            reduce_step(part, step, right_partner)
     round_ends = [t[-1][0] for t in terms]
 
     halved = members == 4 and rows % 128 == 0

time: 174 us -> 172 us (0.989)
  waiting for transfers between devices: 96.8 us -> 94.2 us
    ppermute x2, waiting for transfers between devices: 5.26 us -> 2.94 us  [per_device(): lax.ppermute(partner, 'dp', [(i, i ^ k) for i in range(devices)])]
  transfers between devices with their start and end apart: 30 -> 30, of which waited for: 14 -> 13; matrix products, arithmetic and copies ran while one was open for 6% -> 6% of each run, Pallas kernels for 5% -> 5%
where the time goes in v3:
time: 172 us; the launch traced here: 171 us
  waiting for transfers between devices  94.2 us (55%)
  starting transfers between devices  42.7 us (25%)
  Pallas kernels  12.8 us (7%)
  local copies, waits for them, and re-layouts  10.8 us (6%)
  other arithmetic  6.5 us (4%)
  between operations  2.52 us (1%)
    ppermute x23, waiting for transfers between devices, swap(): lax.ppermute(array, 'dp', [(i, i ^ 1 << bit) for i in range(devices)])  89.6 us
    ppermute x23, starting transfers between devices, swap(): lax.ppermute(array, 'dp', [(i, i ^ 1 << bit) for i in range(devices)])  35 us
    pallas_call x9, Pallas kernels, run(): pl.pallas_call(kernel, out_shape=out_shape, in_specs=[SMEM] + [VMEM] * le...  9.64 us
    unnamed x52, local copies, waits for them, and re-layouts  8.98 us
    ppermute x3, starting transfers between devices, gather_direct(): pieces[k] = lax.ppermute(own, 'dp', [(i, i ^ k) for i in range(devices)])  4.05 us
  transfers between devices with their start and end apart: 30, of which 13 were waited for; matrix products, arithmetic and copies ran while one was open for 6% of the time, Pallas kernels for 5%

profile of v3, /device:TPU:0, one launch (start us, length us, event | category | flops | bytes accessed | tf_op | source)
XLA Modules:
  0.0 171.2 jit_solution(2252862200882060524)
XLA Ops:
  0.6 3.0 %cut.2 = (bf16[4,128,1024]{2,1,0:T(8,128)(2,1)}, bf16[4,128,1024]{2,1,0:T(8,128)(2,1)}) custom-call(bf16[2,2,4,128,1024]{4,3,2,1,0:T(8,128)(2,1)} %bitcast.103), custom_call_target="tpu_custom_call" | custom-call | bytes 4194304 | tf_op jit(solution)/shard_map/cut/pallas_call | solution.py:69
  3.6 3.0 %collective-permute-start = (bf16[4,128,1024]{2,1,0:T(8,128)(2,1)}, bf16[4,128,1024]{2,1,0:T(8,128)(2,1)S(1)}, u32[]{:S(2)}, u32[]{:S(2)}) collective-permute-start(bf16[4,128,1024]{2,1,0:T(8,128)(2,1)} %get-tuple-element.34), channel_id=1, source_target_pairs={{0,4},{4,0},{8,12},{12,8},{16,20},{20,16},{24,28},{28,24},{1,5},{5... | collective-permute-start | bytes 3145736 | tf_op jit(solution)/shard_map/ppermute | solution.py:218
  6.6 1.6 collective-permute-start.3
  8.2 0.7 dynamic-slice_bitcast_fusion.1
  8.9 2.6 %collective-permute-start.1 = (bf16[128,1024]{1,0:T(8,128)(2,1)}, bf16[128,1024]{1,0:T(8,128)(2,1)S(1)}, u32[]{:S(2)}, u32[]{:S(2)}) collective-permute-start(bf16[128,1024]{1,0:T(8,128)(2,1)} %dynamic-slice_bitcast_fusion.1), channel_id=1, source_target_pairs={{0,16},{4,20},{8,24},{12,28},{16,0},{20,4},{24,8},{28,12},{1,17},{... | collective-permute-start | bytes 786440 | tf_op jit(solution)/shard_map/ppermute | solution.py:218
  11.5 2.2 %copy-done = bf16[1,2,1024,1024]{3,2,1,0:T(8,128)(2,1)S(1)} copy-done((bf16[1,2,1024,1024]{3,2,1,0:T(8,128)(2,1)S(1)}, bf16[1,2,1024,1024]{3,2,1,0:T(8,128)(2,1)}, u32[]{:S(2)}) %copy-start) | copy-done | bytes 4194328
  14.0 1.0 copy-done.1
  15.0 21.3 %collective-permute-done.1.partner_ref = bf16[128,1024]{1,0:T(8,128)(2,1)S(1)} collective-permute-done((bf16[128,1024]{1,0:T(8,128)(2,1)}, bf16[128,1024]{1,0:T(8,128)(2,1)S(1)}, u32[]{:S(2)}, u32[]{:S(2)}) %collective-permute-start.1) | collective-permute-done | bytes 262176 | tf_op jit(solution)/shard_map/ppermute | solution.py:218
  36.3 0.7 copy-done.14
  37.0 1.2 copy-done.2
  38.2 0.7 sum_pieces.6
  38.9 3.5 %collective-permute-start.2 = (bf16[2,128,1024]{2,1,0:T(8,128)(2,1)S(1)}, bf16[2,128,1024]{2,1,0:T(8,128)(2,1)S(1)}, u32[]{:S(2)}, u32[]{:S(2)}) collective-permute-start(bf16[2,128,1024]{2,1,0:T(8,128)(2,1)S(1)} %sum_pieces.6), channel_id=1, source_target_pairs={{0,8},{4,12},{8,0},{12,4},{16,24},{20,28},{24,16},{28,20},{1,9},{5... | collective-permute-start | bytes 1572872 | tf_op jit(solution)/shard_map/ppermute | solution.py:218
  42.4 0.7 sum_pieces.7
  43.0 0.6 collective-permute-start.4
  43.7 0.7 pack.1
  44.4 13.6 %collective-permute-done.5 = bf16[128,1024]{1,0:T(8,128)(2,1)S(1)} collective-permute-done((bf16[128,1024]{1,0:T(8,128)(2,1)S(1)}, bf16[128,1024]{1,0:T(8,128)(2,1)S(1)}, u32[]{:S(2)}, u32[]{:S(2)}) %collective-permute-start.5) | collective-permute-done | bytes 262176 | tf_op jit(solution)/shard_map/ppermute | solution.py:218
  58.0 0.7 collective-permute-done.2.refs_2_
  58.7 0.6 sum_pieces.8
  59.4 1.7 %collective-permute-start.8 = (bf16[9,128,128]{2,1,0:T(8,128)(2,1)S(1)}, bf16[9,128,128]{2,1,0:T(8,128)(2,1)S(1)}, u32[]{:S(2)}, u32[]{:S(2)}) collective-permute-start(bf16[9,128,128]{2,1,0:T(8,128)(2,1)S(1)} %get-tuple-element.45), channel_id=1, source_target_pairs={{0,8},{4,12},{8,0},{12,4},{16,24},{20,28},{24,16},{28,20},{1,9},{5... | collective-permute-start | bytes 884744 | tf_op jit(solution)/shard_map/ppermute | solution.py:218
  61.1 0.5 collective-permute-start.9
  61.6 1.1 collective-permute-start.6
  62.7 8.5 %collective-permute-done.6 = bf16[128,1024]{1,0:T(8,128)(2,1)S(1)} collective-permute-done((bf16[128,1024]{1,0:T(8,128)(2,1)S(1)}, bf16[128,1024]{1,0:T(8,128)(2,1)S(1)}, u32[]{:S(2)}, u32[]{:S(2)}) %collective-permute-start.6) | collective-permute-done | bytes 262176 | tf_op jit(solution)/shard_map/ppermute | solution.py:218
  71.2 0.7 sum_pieces.9
  71.9 1.3 sum_pieces.10
  73.2 3.2 %collective-permute-start.7 = (bf16[128,1024]{1,0:T(8,128)(2,1)}, bf16[128,1024]{1,0:T(8,128)(2,1)}, u32[]{:S(2)}, u32[]{:S(2)}) collective-permute-start(bf16[128,1024]{1,0:T(8,128)(2,1)} %bitcast.9), channel_id=1, source_target_pairs={{0,16},{4,20},{8,24},{12,28},{16,0},{20,4},{24,8},{28,12},{1,17},{... | collective-permute-start | bytes 786440 | tf_op jit(solution)/shard_map/ppermute | solution.py:218
  76.4 0.7 copy-done.10
  77.2 0.7 copy-done.12
  77.9 1.3 collective-permute-start.11
  79.2 2.4 %collective-permute-start.10 = (bf16[128,1024]{1,0:T(8,128)(2,1)S(1)}, bf16[128,1024]{1,0:T(8,128)(2,1)}, u32[]{:S(2)}, u32[]{:S(2)}) collective-permute-start(bf16[128,1024]{1,0:T(8,128)(2,1)S(1)} %bitcast.106), channel_id=1, source_target_pairs={{0,8},{4,12},{8,0},{12,4},{16,24},{20,28},{24,16},{28,20},{1,9},{5... | collective-permute-start | bytes 786440 | tf_op jit(solution)/shard_map/ppermute | solution.py:218
  81.6 0.6 collective-permute-start.16
  82.2 1.1 fusion.31
  83.3 2.1 %collective-permute-done.7 = bf16[128,1024]{1,0:T(8,128)(2,1)} collective-permute-done((bf16[128,1024]{1,0:T(8,128)(2,1)}, bf16[128,1024]{1,0:T(8,128)(2,1)}, u32[]{:S(2)}, u32[]{:S(2)}) %collective-permute-start.7) | collective-permute-done | bytes 262176 | tf_op jit(solution)/shard_map/ppermute | solution.py:218
  85.4 1.1 sum_pieces.11
  86.5 1.4 collective-permute-done.10.refs_2_
  87.9 2.1 %collective-permute-start.13 = (bf16[128,1024]{1,0:T(8,128)(2,1)S(1)}, bf16[128,1024]{1,0:T(8,128)(2,1)S(1)}, u32[]{:S(2)}, u32[]{:S(2)}) collective-permute-start(bf16[128,1024]{1,0:T(8,128)(2,1)S(1)} %bitcast.108), channel_id=1, source_target_pairs={{0,4},{4,0},{8,12},{12,8},{16,20},{20,16},{24,28},{28,24},{1,5},{5... | collective-permute-start | bytes 786440 | tf_op jit(solution)/shard_map/ppermute | solution.py:234
  90.5 1.5 collective-permute-start.15
  92.0 1.6 collective-permute-start.12
  93.6 0.6 collective-permute-start.17
  94.4 1.1 unfold.1.refs_8_
  95.6 9.8 %collective-permute-done.12.refs_3_ = bf16[128,1024]{1,0:T(8,128)(2,1)S(1)} collective-permute-done((bf16[128,1024]{1,0:T(8,128)(2,1)}, bf16[128,1024]{1,0:T(8,128)(2,1)S(1)}, u32[]{:S(2)}, u32[]{:S(2)}) %collective-permute-start.12) | collective-permute-done | bytes 262176 | tf_op jit(solution)/shard_map/ppermute | solution.py:218
  105.4 2.8 %product.1 = (bf16[256,1024]{1,0:T(8,128)(2,1)S(1)}, bf16[1024,1024]{1,0:T(8,128)(2,1)S(1)}, f32[8,128]{1,0:T(8,128)S(1)}) custom-call(s32[3]{0:T(128)S(1)} %pad_add_fusion.place_ref, bf16[128,1024]{1,0:T(8,128)(2,1)S(1)} %bitcast.107, bf16[128,1024]{1,0:T(8,128)(2,1)} %collective-permute-done.11.refs_1_, bf16[128,1024]{1,0:T(8,128)(2,1)} %collective-permute-done.10.refs_2_, ...), custom_call_target="tpu_custom_call" | custom-call | flops 1073741824 | bytes 4718592 | tf_op jit(solution)/shard_map/product/pallas_call | solution.py:31
  108.2 1.7 collective-permute-start.22
  109.9 2.2 %collective-permute-start.23 = (bf16[2,128,1024]{2,1,0:T(8,128)(2,1)S(1)}, bf16[2,128,1024]{2,1,0:T(8,128)(2,1)S(1)}, u32[]{:S(2)}, u32[]{:S(2)}) collective-permute-start(bf16[2,128,1024]{2,1,0:T(8,128)(2,1)S(1)} %bitcast.114), channel_id=1, source_target_pairs={{0,8},{4,12},{8,0},{12,4},{16,24},{20,28},{24,16},{28,20},{1,9},{5... | collective-permute-start | bytes 1572872 | tf_op jit(solution)/shard_map/ppermute | solution.py:218
  112.1 1.7 collective-permute-start.24
  113.9 2.1 %fusion.4 = (f32[]{:T(128)}, f32[2,128,1024]{2,1,0:T(8,128)}) fusion(bf16[1,128,1024]{2,1,0:T(8,128)(2,1)S(1)} %get-tuple-element.67, bf16[1,128,1024]{2,1,0:T(8,128)(2,1)S(1)} %get-tuple-element.66, f32[2,128,1024]{2,1,0:T(8,128)S(1)} %copy-done.23), kind=kLoop, calls=%fused_computation.21 | loop fusion | flops 2621439 | bytes 2621444 | tf_op jit(solution)/shard_map/reduce_sum | solution.py:330
  116.0 0.6 broadcast_select_fusion
  116.8 0.7 fusion
  117.5 0.5 convolution_bitcast_fusion.1
  118.0 0.7 fusion.42
  118.7 1.6 collective-permute-start.19
  120.2 0.5 convolution_bitcast_fusion
  120.7 1.6 collective-permute-done.19
  123.1 2.9 %collective-permute-done.20 = f32[8,128]{1,0:T(8,128)S(1)} collective-permute-done((f32[8,128]{1,0:T(8,128)S(1)}, f32[8,128]{1,0:T(8,128)S(1)}, u32[]{:S(2)}, u32[]{:S(2)}) %collective-permute-start.20) | collective-permute-done | bytes 4128 | tf_op jit(solution)/shard_map/ppermute | solution.py:218
  126.0 3.8 %collective-permute-done.22 = bf16[2,128,1024]{2,1,0:T(8,128)(2,1)S(1)} collective-permute-done((bf16[2,128,1024]{2,1,0:T(8,128)(2,1)S(1)}, bf16[2,128,1024]{2,1,0:T(8,128)(2,1)S(1)}, u32[]{:S(2)}, u32[]{:S(2)}) %collective-permute-start.22) | collective-permute-done | bytes 524320 | tf_op jit(solution)/shard_map/ppermute | solution.py:218
  130.1 0.6 collective-permute-start.26
  130.8 3.3 %collective-permute-start.25 = (f32[8,128]{1,0:T(8,128)S(1)}, f32[8,128]{1,0:T(8,128)S(1)}, u32[]{:S(2)}, u32[]{:S(2)}) collective-permute-start(f32[8,128]{1,0:T(8,128)S(1)} %add.110), channel_id=1, source_target_pairs={{0,16},{4,20},{8,24},{12,28},{16,0},{20,4},{24,8},{28,12},{1,17},{... | collective-permute-start | bytes 12296 | tf_op jit(solution)/shard_map/ppermute | solution.py:218
  134.2 1.3 collective-permute-start.27
  135.5 0.6 collective-permute-start.28
  136.1 0.8 collective-permute-start.29
  136.9 0.6 fusion.38
  138.8 0.5 broadcast_in_dim.31
  139.7 25.3 %collective-permute-done.26 = bf16[2,2,128,1024]{3,2,1,0:T(8,128)(2,1)S(1)} collective-permute-done((bf16[2,2,128,1024]{3,2,1,0:T(8,128)(2,1)S(1)}, bf16[2,2,128,1024]{3,2,1,0:T(8,128)(2,1)S(1)}, u32[]{:S(2)}, u32[]{:S(2)}) %collective-permute-start.26) | collective-permute-done | bytes 1048608 | tf_op jit(solution)/shard_map/ppermute | solution.py:218
  165.5 2.9 %collective-permute-done.28 = bf16[2,128,1024]{2,1,0:T(8,128)(2,1)S(1)} collective-permute-done((bf16[2,128,1024]{2,1,0:T(8,128)(2,1)S(1)}, bf16[2,128,1024]{2,1,0:T(8,128)(2,1)S(1)}, u32[]{:S(2)}, u32[]{:S(2)}) %collective-permute-start.28) | collective-permute-done | bytes 524320 | tf_op jit(solution)/shard_map/ppermute | solution.py:361
  168.8 1.7 %copy-done.16 = bf16[2,2,4,128,1024]{4,3,2,1,0:T(8,128)(2,1)} copy-done((bf16[2,2,4,128,1024]{4,3,2,1,0:T(8,128)(2,1)}, bf16[2,2,4,128,1024]{4,3,2,1,0:T(8,128)(2,1)S(1)}, u32[]{:S(2)}) %copy-start.16) | copy-done | bytes 4194328
  (93 shorter events, 4.2 us)
Async XLA Ops:
  0.6 7.6 %copy-start.6 = (bf16[2,128,1024]{2,1,0:T(8,128)(2,1)S(1)}, bf16[2,128,1024]{2,1,0:T(8,128)(2,1)}, u32[]{:S(2)}) copy-start(bf16[2,128,1024]{2,1,0:T(8,128)(2,1)} %own_ref.1) | copy-start | bytes 1572868
  3.6 33.4 %collective-permute-start = (bf16[4,128,1024]{2,1,0:T(8,128)(2,1)}, bf16[4,128,1024]{2,1,0:T(8,128)(2,1)S(1)}, u32[]{:S(2)}, u32[]{:S(2)}) collective-permute-start(bf16[4,128,1024]{2,1,0:T(8,128)(2,1)} %get-tuple-element.34), channel_id=1, source_target_pairs={{0,4},{4,0},{8,12},{12,8},{16,20},{20,16},{24,28},{28,24},{1,5},{5... | collective-permute-start | bytes 3145736 | tf_op jit(solution)/shard_map/ppermute | solution.py:218
  6.6 35.7 %collective-permute-start.3 = (bf16[4,128,1024]{2,1,0:T(8,128)(2,1)}, bf16[4,128,1024]{2,1,0:T(8,128)(2,1)S(1)}, u32[]{:S(2)}, u32[]{:S(2)}) collective-permute-start(bf16[4,128,1024]{2,1,0:T(8,128)(2,1)} %get-tuple-element.35), channel_id=1, source_target_pairs={{0,8},{4,12},{8,0},{12,4},{16,24},{20,28},{24,16},{28,20},{1,9},{5... | collective-permute-start | bytes 3145736 | tf_op jit(solution)/shard_map/ppermute | solution.py:218
  8.9 27.3 %collective-permute-start.1 = (bf16[128,1024]{1,0:T(8,128)(2,1)}, bf16[128,1024]{1,0:T(8,128)(2,1)S(1)}, u32[]{:S(2)}, u32[]{:S(2)}) collective-permute-start(bf16[128,1024]{1,0:T(8,128)(2,1)} %dynamic-slice_bitcast_fusion.1), channel_id=1, source_target_pairs={{0,16},{4,20},{8,24},{12,28},{16,0},{20,4},{24,8},{28,12},{1,17},{... | collective-permute-start | bytes 786440 | tf_op jit(solution)/shard_map/ppermute | solution.py:218
  11.5 2.2 %copy-start = (bf16[1,2,1024,1024]{3,2,1,0:T(8,128)(2,1)S(1)}, bf16[1,2,1024,1024]{3,2,1,0:T(8,128)(2,1)}, u32[]{:S(2)}) copy-start(bf16[1,2,1024,1024]{3,2,1,0:T(8,128)(2,1)} %param.6) | copy-start | bytes 12582916
  13.9 1.0 copy-start.1
  36.3 0.7 copy-start.14
  37.0 1.2 copy-start.2
  38.2 5.4 %copy-start.24 = (bf16[2,128,1024]{2,1,0:T(8,128)(2,1)S(1)}, bf16[2,128,1024]{2,1,0:T(8,128)(2,1)}, u32[]{:S(2)}) copy-start(bf16[2,128,1024]{2,1,0:T(8,128)(2,1)} %param.9) | copy-start | bytes 1572868
  38.2 5.5 %copy-start.7 = (bf16[2,128,1024]{2,1,0:T(8,128)(2,1)S(1)}, bf16[2,128,1024]{2,1,0:T(8,128)(2,1)}, u32[]{:S(2)}) copy-start(bf16[2,128,1024]{2,1,0:T(8,128)(2,1)} %own_ref.1) | copy-start | bytes 1572868
  38.2 5.5 %copy-start.15 = (bf16[128,1024]{1,0:T(8,128)(2,1)S(1)}, bf16[128,1024]{1,0:T(8,128)(2,1)}, u32[]{:S(2)}) copy-start(bf16[128,1024]{1,0:T(8,128)(2,1)} %copy-done.14) | copy-start | bytes 786436
  38.2 20.5 %copy-start.3 = (bf16[4,128,1024]{2,1,0:T(8,128)(2,1)S(1)}, bf16[4,128,1024]{2,1,0:T(8,128)(2,1)}, u32[]{:S(2)}) copy-start(bf16[4,128,1024]{2,1,0:T(8,128)(2,1)} %copy-done.1) | copy-start | bytes 3145732
  38.9 19.8 %collective-permute-start.2 = (bf16[2,128,1024]{2,1,0:T(8,128)(2,1)S(1)}, bf16[2,128,1024]{2,1,0:T(8,128)(2,1)S(1)}, u32[]{:S(2)}, u32[]{:S(2)}) collective-permute-start(bf16[2,128,1024]{2,1,0:T(8,128)(2,1)S(1)} %sum_pieces.6), channel_id=1, source_target_pairs={{0,8},{4,12},{8,0},{12,4},{16,24},{20,28},{24,16},{28,20},{1,9},{5... | collective-permute-start | bytes 1572872 | tf_op jit(solution)/shard_map/ppermute | solution.py:218
  43.0 15.7 %collective-permute-start.4 = (bf16[2,128,1024]{2,1,0:T(8,128)(2,1)S(1)}, bf16[2,128,1024]{2,1,0:T(8,128)(2,1)S(1)}, u32[]{:S(2)}, u32[]{:S(2)}) collective-permute-start(bf16[2,128,1024]{2,1,0:T(8,128)(2,1)S(1)} %sum_pieces.7), channel_id=1, source_target_pairs={{0,4},{4,0},{8,12},{12,8},{16,20},{20,16},{24,28},{28,24},{1,5},{5... | collective-permute-start | bytes 1572872 | tf_op jit(solution)/shard_map/ppermute | solution.py:218
  43.6 14.3 %collective-permute-start.5 = (bf16[128,1024]{1,0:T(8,128)(2,1)S(1)}, bf16[128,1024]{1,0:T(8,128)(2,1)S(1)}, u32[]{:S(2)}, u32[]{:S(2)}) collective-permute-start(bf16[128,1024]{1,0:T(8,128)(2,1)S(1)} %dynamic-slice_bitcast_fusion), channel_id=1, source_target_pairs={{0,16},{4,20},{8,24},{12,28},{16,0},{20,4},{24,8},{28,12},{1,17},{... | collective-permute-start | bytes 786440 | tf_op jit(solution)/shard_map/ppermute | solution.py:218
  44.4 28.8 %copy-start.8 = (bf16[2,128,1024]{2,1,0:T(8,128)(2,1)}, bf16[2,128,1024]{2,1,0:T(8,128)(2,1)S(1)}, u32[]{:S(2)}) copy-start(bf16[2,128,1024]{2,1,0:T(8,128)(2,1)S(1)} %get-tuple-element.48.pair_ref) | copy-start | bytes 1572868
  58.0 13.2 %copy-start.25 = (bf16[128,1024]{1,0:T(8,128)(2,1)}, bf16[128,1024]{1,0:T(8,128)(2,1)S(1)}, u32[]{:S(2)}) copy-start(bf16[128,1024]{1,0:T(8,128)(2,1)S(1)} %collective-permute-done.5) | copy-start | bytes 786436
  58.7 14.5 %copy-start.4 = (bf16[2,128,1024]{2,1,0:T(8,128)(2,1)}, bf16[2,128,1024]{2,1,0:T(8,128)(2,1)S(1)}, u32[]{:S(2)}) copy-start(bf16[2,128,1024]{2,1,0:T(8,128)(2,1)S(1)} %collective-permute-done.4.refs_2_) | copy-start | bytes 1572868
  59.4 17.1 %collective-permute-start.8 = (bf16[9,128,128]{2,1,0:T(8,128)(2,1)S(1)}, bf16[9,128,128]{2,1,0:T(8,128)(2,1)S(1)}, u32[]{:S(2)}, u32[]{:S(2)}) collective-permute-start(bf16[9,128,128]{2,1,0:T(8,128)(2,1)S(1)} %get-tuple-element.45), channel_id=1, source_target_pairs={{0,8},{4,12},{8,0},{12,4},{16,24},{20,28},{24,16},{28,20},{1,9},{5... | collective-permute-start | bytes 884744 | tf_op jit(solution)/shard_map/ppermute | solution.py:218
  61.1 15.4 %collective-permute-start.9 = (bf16[9,128,128]{2,1,0:T(8,128)(2,1)S(1)}, bf16[9,128,128]{2,1,0:T(8,128)(2,1)S(1)}, u32[]{:S(2)}, u32[]{:S(2)}) collective-permute-start(bf16[9,128,128]{2,1,0:T(8,128)(2,1)S(1)} %get-tuple-element.45), channel_id=1, source_target_pairs={{0,4},{4,0},{8,12},{12,8},{16,20},{20,16},{24,28},{28,24},{1,5},{5... | collective-permute-start | bytes 884744 | tf_op jit(solution)/shard_map/ppermute | solution.py:218
  61.6 9.6 %collective-permute-start.6 = (bf16[128,1024]{1,0:T(8,128)(2,1)S(1)}, bf16[128,1024]{1,0:T(8,128)(2,1)S(1)}, u32[]{:S(2)}, u32[]{:S(2)}) collective-permute-start(bf16[128,1024]{1,0:T(8,128)(2,1)S(1)} %bitcast.117), channel_id=1, source_target_pairs={{0,16},{4,20},{8,24},{12,28},{16,0},{20,4},{24,8},{28,12},{1,17},{... | collective-permute-start | bytes 786440 | tf_op jit(solution)/shard_map/ppermute | solution.py:218
  73.2 12.2 %copy-start.5 = (bf16[2,128,1024]{2,1,0:T(8,128)(2,1)S(1)}, bf16[2,128,1024]{2,1,0:T(8,128)(2,1)}, u32[]{:S(2)}) copy-start(bf16[2,128,1024]{2,1,0:T(8,128)(2,1)} %copy-done.4) | copy-start | bytes 1572868
  73.2 12.2 %collective-permute-start.7 = (bf16[128,1024]{1,0:T(8,128)(2,1)}, bf16[128,1024]{1,0:T(8,128)(2,1)}, u32[]{:S(2)}, u32[]{:S(2)}) collective-permute-start(bf16[128,1024]{1,0:T(8,128)(2,1)} %bitcast.9), channel_id=1, source_target_pairs={{0,16},{4,20},{8,24},{12,28},{16,0},{20,4},{24,8},{28,12},{1,17},{... | collective-permute-start | bytes 786440 | tf_op jit(solution)/shard_map/ppermute | solution.py:218
  76.4 0.7 copy-start.10
  77.2 0.7 copy-start.12
  77.9 8.6 %collective-permute-start.11 = (bf16[128,1024]{1,0:T(8,128)(2,1)S(1)}, bf16[128,1024]{1,0:T(8,128)(2,1)}, u32[]{:S(2)}, u32[]{:S(2)}) collective-permute-start(bf16[128,1024]{1,0:T(8,128)(2,1)S(1)} %bitcast.105), channel_id=1, source_target_pairs={{0,4},{4,0},{8,12},{12,8},{16,20},{20,16},{24,28},{28,24},{1,5},{5... | collective-permute-start | bytes 786440 | tf_op jit(solution)/shard_map/ppermute | solution.py:218
  79.2 8.8 %collective-permute-start.10 = (bf16[128,1024]{1,0:T(8,128)(2,1)S(1)}, bf16[128,1024]{1,0:T(8,128)(2,1)}, u32[]{:S(2)}, u32[]{:S(2)}) collective-permute-start(bf16[128,1024]{1,0:T(8,128)(2,1)S(1)} %bitcast.106), channel_id=1, source_target_pairs={{0,8},{4,12},{8,0},{12,4},{16,24},{20,28},{24,16},{28,20},{1,9},{5... | collective-permute-start | bytes 786440 | tf_op jit(solution)/shard_map/ppermute | solution.py:218
  81.6 12.8 %copy-start.9 = (bf16[2,128,1024]{2,1,0:T(8,128)(2,1)S(1)}, bf16[2,128,1024]{2,1,0:T(8,128)(2,1)}, u32[]{:S(2)}) copy-start(bf16[2,128,1024]{2,1,0:T(8,128)(2,1)} %copy-done.8) | copy-start | bytes 1572868
  81.6 12.8 %copy-start.11 = (bf16[9,128,128]{2,1,0:T(8,128)(2,1)S(1)}, bf16[9,128,128]{2,1,0:T(8,128)(2,1)}, u32[]{:S(2)}) copy-start(bf16[9,128,128]{2,1,0:T(8,128)(2,1)} %copy-done.10) | copy-start | bytes 884740
  81.6 12.8 %copy-start.13 = (bf16[9,128,128]{2,1,0:T(8,128)(2,1)S(1)}, bf16[9,128,128]{2,1,0:T(8,128)(2,1)}, u32[]{:S(2)}) copy-start(bf16[9,128,128]{2,1,0:T(8,128)(2,1)} %copy-done.12) | copy-start | bytes 884740
  81.6 12.0 %collective-permute-start.16 = (bf16[9,128,128]{2,1,0:T(8,128)(2,1)}, bf16[9,128,128]{2,1,0:T(8,128)(2,1)S(1)}, u32[]{:S(2)}, u32[]{:S(2)}) collective-permute-start(bf16[9,128,128]{2,1,0:T(8,128)(2,1)} %copy-done.10), channel_id=1, source_target_pairs={{0,4},{4,0},{8,12},{12,8},{16,20},{20,16},{24,28},{28,24},{1,5},{5... | collective-permute-start | bytes 884744 | tf_op jit(solution)/shard_map/ppermute | solution.py:218
  87.9 17.5 %collective-permute-start.13 = (bf16[128,1024]{1,0:T(8,128)(2,1)S(1)}, bf16[128,1024]{1,0:T(8,128)(2,1)S(1)}, u32[]{:S(2)}, u32[]{:S(2)}) collective-permute-start(bf16[128,1024]{1,0:T(8,128)(2,1)S(1)} %bitcast.108), channel_id=1, source_target_pairs={{0,4},{4,0},{8,12},{12,8},{16,20},{20,16},{24,28},{28,24},{1,5},{5... | collective-permute-start | bytes 786440 | tf_op jit(solution)/shard_map/ppermute | solution.py:234
  90.0 15.3 %collective-permute-start.14 = (bf16[128,1024]{1,0:T(8,128)(2,1)S(1)}, bf16[128,1024]{1,0:T(8,128)(2,1)S(1)}, u32[]{:S(2)}, u32[]{:S(2)}) collective-permute-start(bf16[128,1024]{1,0:T(8,128)(2,1)S(1)} %bitcast.109), channel_id=1, source_target_pairs={{0,8},{4,12},{8,0},{12,4},{16,24},{20,28},{24,16},{28,20},{1,9},{5... | collective-permute-start | bytes 786440 | tf_op jit(solution)/shard_map/ppermute | solution.py:234
  90.5 14.9 %collective-permute-start.15 = (bf16[128,1024]{1,0:T(8,128)(2,1)S(1)}, bf16[128,1024]{1,0:T(8,128)(2,1)S(1)}, u32[]{:S(2)}, u32[]{:S(2)}) collective-permute-start(bf16[128,1024]{1,0:T(8,128)(2,1)S(1)} %bitcast.110), channel_id=1, source_target_pairs={{0,12},{4,8},{8,4},{12,0},{16,28},{20,24},{24,20},{28,16},{1,13},{... | collective-permute-start | bytes 786440 | tf_op jit(solution)/shard_map/ppermute | solution.py:234
  92.0 13.4 %collective-permute-start.12 = (bf16[128,1024]{1,0:T(8,128)(2,1)}, bf16[128,1024]{1,0:T(8,128)(2,1)S(1)}, u32[]{:S(2)}, u32[]{:S(2)}) collective-permute-start(bf16[128,1024]{1,0:T(8,128)(2,1)} %collective-permute-done.10.refs_2_), channel_id=1, source_target_pairs={{0,4},{4,0},{8,12},{12,8},{16,20},{20,16},{24,28},{28,24},{1,5},{5... | collective-permute-start | bytes 786440 | tf_op jit(solution)/shard_map/ppermute | solution.py:218
  93.6 20.2 %collective-permute-start.17 = (bf16[128,1024]{1,0:T(8,128)(2,1)S(1)}, bf16[128,1024]{1,0:T(8,128)(2,1)S(1)}, u32[]{:S(2)}, u32[]{:S(2)}) collective-permute-start(bf16[128,1024]{1,0:T(8,128)(2,1)S(1)} %fusion.28), channel_id=1, source_target_pairs={{0,16},{4,20},{8,24},{12,28},{16,0},{20,4},{24,8},{28,12},{1,17},{... | collective-permute-start | bytes 786440 | tf_op jit(solution)/shard_map/ppermute | solution.py:218
  94.4 19.4 %copy-start.23 = (f32[2,128,1024]{2,1,0:T(8,128)S(1)}, f32[2,128,1024]{2,1,0:T(8,128)}, u32[]{:S(2)}) copy-start(f32[2,128,1024]{2,1,0:T(8,128)} %param.11) | copy-start | bytes 3145732
  108.2 21.7 %collective-permute-start.22 = (bf16[2,128,1024]{2,1,0:T(8,128)(2,1)S(1)}, bf16[2,128,1024]{2,1,0:T(8,128)(2,1)S(1)}, u32[]{:S(2)}, u32[]{:S(2)}) collective-permute-start(bf16[2,128,1024]{2,1,0:T(8,128)(2,1)S(1)} %bitcast.113), channel_id=1, source_target_pairs={{0,16},{4,20},{8,24},{12,28},{16,0},{20,4},{24,8},{28,12},{1,17},{... | collective-permute-start | bytes 1572872 | tf_op jit(solution)/shard_map/ppermute | solution.py:218
  109.9 20.1 %collective-permute-start.23 = (bf16[2,128,1024]{2,1,0:T(8,128)(2,1)S(1)}, bf16[2,128,1024]{2,1,0:T(8,128)(2,1)S(1)}, u32[]{:S(2)}, u32[]{:S(2)}) collective-permute-start(bf16[2,128,1024]{2,1,0:T(8,128)(2,1)S(1)} %bitcast.114), channel_id=1, source_target_pairs={{0,8},{4,12},{8,0},{12,4},{16,24},{20,28},{24,16},{28,20},{1,9},{5... | collective-permute-start | bytes 1572872 | tf_op jit(solution)/shard_map/ppermute | solution.py:218
  112.1 17.9 %collective-permute-start.24 = (bf16[2,128,1024]{2,1,0:T(8,128)(2,1)S(1)}, bf16[2,128,1024]{2,1,0:T(8,128)(2,1)S(1)}, u32[]{:S(2)}, u32[]{:S(2)}) collective-permute-start(bf16[2,128,1024]{2,1,0:T(8,128)(2,1)S(1)} %bitcast.115), channel_id=1, source_target_pairs={{0,4},{4,0},{8,12},{12,8},{16,20},{20,16},{24,28},{28,24},{1,5},{5... | collective-permute-start | bytes 1572872 | tf_op jit(solution)/shard_map/ppermute | solution.py:218
  116.7 1.3 collective-permute-start.18
  116.7 5.9 %copy-start.19 = (f32[2,128,1024]{2,1,0:T(8,128)S(1)}, f32[2,128,1024]{2,1,0:T(8,128)}, u32[]{:S(2)}) copy-start(f32[2,128,1024]{2,1,0:T(8,128)} %param.8) | copy-start | bytes 3145732
  116.8 5.9 %copy-start.22 = (f32[2,128,1024]{2,1,0:T(8,128)S(1)}, f32[2,128,1024]{2,1,0:T(8,128)}, u32[]{:S(2)}) copy-start(f32[2,128,1024]{2,1,0:T(8,128)} %param.7) | copy-start | bytes 3145732
  118.7 3.7 %collective-permute-start.19 = (f32[8,128]{1,0:T(8,128)S(1)}, f32[8,128]{1,0:T(8,128)S(1)}, u32[]{:S(2)}, u32[]{:S(2)}) collective-permute-start(f32[8,128]{1,0:T(8,128)S(1)} %fusion.42), channel_id=1, source_target_pairs={{0,2},{1,3},{2,0},{3,1},{4,6},{5,7},{6,4},{7,5},{8,10},{9,11},{10,... | collective-permute-start | bytes 12296 | tf_op jit(solution)/shard_map/ppermute | solution.py:335
  122.3 3.6 %collective-permute-start.20 = (f32[8,128]{1,0:T(8,128)S(1)}, f32[8,128]{1,0:T(8,128)S(1)}, u32[]{:S(2)}, u32[]{:S(2)}) collective-permute-start(f32[8,128]{1,0:T(8,128)S(1)} %add.108), channel_id=1, source_target_pairs={{0,4},{4,0},{8,12},{12,8},{16,20},{20,16},{24,28},{28,24},{1,5},{5... | collective-permute-start | bytes 12296 | tf_op jit(solution)/shard_map/ppermute | solution.py:218
  126.0 4.9 %collective-permute-start.21 = (f32[8,128]{1,0:T(8,128)S(1)}, f32[8,128]{1,0:T(8,128)S(1)}, u32[]{:S(2)}, u32[]{:S(2)}) collective-permute-start(f32[8,128]{1,0:T(8,128)S(1)} %add.109), channel_id=1, source_target_pairs={{0,8},{4,12},{8,0},{12,4},{16,24},{20,28},{24,16},{28,20},{1,9},{5... | collective-permute-start | bytes 12296 | tf_op jit(solution)/shard_map/ppermute | solution.py:218
  130.1 35.0 %collective-permute-start.26 = (bf16[2,2,128,1024]{3,2,1,0:T(8,128)(2,1)S(1)}, bf16[2,2,128,1024]{3,2,1,0:T(8,128)(2,1)S(1)}, u32[]{:S(2)}, u32[]{:S(2)}) collective-permute-start(bf16[2,2,128,1024]{3,2,1,0:T(8,128)(2,1)S(1)} %pad_maximum_fusion), channel_id=1, source_target_pairs={{0,4},{4,0},{8,12},{12,8},{16,20},{20,16},{24,28},{28,24},{1,5},{5... | collective-permute-start | bytes 3145736 | tf_op jit(solution)/shard_map/ppermute | solution.py:218
  130.8 6.0 %collective-permute-start.25 = (f32[8,128]{1,0:T(8,128)S(1)}, f32[8,128]{1,0:T(8,128)S(1)}, u32[]{:S(2)}, u32[]{:S(2)}) collective-permute-start(f32[8,128]{1,0:T(8,128)S(1)} %add.110), channel_id=1, source_target_pairs={{0,16},{4,20},{8,24},{12,28},{16,0},{20,4},{24,8},{28,12},{1,17},{... | collective-permute-start | bytes 12296 | tf_op jit(solution)/shard_map/ppermute | solution.py:218
  134.2 31.2 %collective-permute-start.27 = (bf16[2,128,1024]{2,1,0:T(8,128)(2,1)S(1)}, bf16[2,128,1024]{2,1,0:T(8,128)(2,1)S(1)}, u32[]{:S(2)}, u32[]{:S(2)}) collective-permute-start(bf16[2,128,1024]{2,1,0:T(8,128)(2,1)S(1)} %collective-permute-done.22), channel_id=1, source_target_pairs={{0,12},{4,8},{8,4},{12,0},{16,28},{20,24},{24,20},{28,16},{1,13},{... | collective-permute-start | bytes 1572872 | tf_op jit(solution)/shard_map/ppermute | solution.py:361
  135.5 33.0 %collective-permute-start.28 = (bf16[2,128,1024]{2,1,0:T(8,128)(2,1)S(1)}, bf16[2,128,1024]{2,1,0:T(8,128)(2,1)S(1)}, u32[]{:S(2)}, u32[]{:S(2)}) collective-permute-start(bf16[2,128,1024]{2,1,0:T(8,128)(2,1)S(1)} %collective-permute-done.22), channel_id=1, source_target_pairs={{0,8},{4,12},{8,0},{12,4},{16,24},{20,28},{24,16},{28,20},{1,9},{5... | collective-permute-start | bytes 1572872 | tf_op jit(solution)/shard_map/ppermute | solution.py:361
  136.1 32.5 %collective-permute-start.29 = (bf16[2,128,1024]{2,1,0:T(8,128)(2,1)S(1)}, bf16[2,128,1024]{2,1,0:T(8,128)(2,1)S(1)}, u32[]{:S(2)}, u32[]{:S(2)}) collective-permute-start(bf16[2,128,1024]{2,1,0:T(8,128)(2,1)S(1)} %pad_maximum_fusion.4), channel_id=1, source_target_pairs={{0,16},{4,20},{8,24},{12,28},{16,0},{20,4},{24,8},{28,12},{1,17},{... | collective-permute-start | bytes 1572872 | tf_op jit(solution)/shard_map/ppermute | solution.py:218
  139.4 29.2 %copy-start.17 = (f32[2,128,1024]{2,1,0:T(8,128)S(1)}, f32[2,128,1024]{2,1,0:T(8,128)}, u32[]{:S(2)}) copy-start(f32[2,128,1024]{2,1,0:T(8,128)} %param.8) | copy-start | bytes 3145732
  139.4 29.2 %copy-start.20 = (f32[2,128,1024]{2,1,0:T(8,128)S(1)}, f32[2,128,1024]{2,1,0:T(8,128)}, u32[]{:S(2)}) copy-start(f32[2,128,1024]{2,1,0:T(8,128)} %param.7) | copy-start | bytes 3145732
  168.5 2.0 %copy-start.16 = (bf16[2,2,4,128,1024]{4,3,2,1,0:T(8,128)(2,1)}, bf16[2,2,4,128,1024]{4,3,2,1,0:T(8,128)(2,1)S(1)}, u32[]{:S(2)}) copy-start(bf16[2,2,4,128,1024]{4,3,2,1,0:T(8,128)(2,1)S(1)} %fusion.20) | copy-start | bytes 12582916
  168.8 2.1 %copy-start.18 = (f32[2,128,1024]{2,1,0:T(8,128)}, f32[2,128,1024]{2,1,0:T(8,128)S(1)}, u32[]{:S(2)}) copy-start(f32[2,128,1024]{2,1,0:T(8,128)S(1)} %get-tuple-element.70) | copy-start | bytes 3145732
  168.8 2.4 %copy-start.21 = (f32[2,128,1024]{2,1,0:T(8,128)}, f32[2,128,1024]{2,1,0:T(8,128)S(1)}, u32[]{:S(2)}) copy-start(f32[2,128,1024]{2,1,0:T(8,128)S(1)} %get-tuple-element.71) | copy-start | bytes 3145732

commit v4 on v3

--- a/solution.py
+++ b/solution.py
@@ -25,7 +25,7 @@
 SMEM = pl.BlockSpec(memory_space=pltpu.SMEM)
 
 
-def call(kernel, out_shape, name, flops=0):
+def call(kernel, out_shape, name, flops=0, grant=8):
     def run(place, *arrays):
         size = sum(a.size * a.dtype.itemsize for a in arrays)
         return pl.pallas_call(
@@ -33,7 +33,7 @@
             out_shape=out_shape,
             in_specs=[SMEM] + [VMEM] * len(arrays),
             out_specs=jax.tree.map(lambda _: VMEM, out_shape),
-            compiler_params=pltpu.CompilerParams(vmem_limit_bytes=24 * 2**20),
+            compiler_params=pltpu.CompilerParams(vmem_limit_bytes=grant * 2**20),
             cost_estimate=pl.CostEstimate(flops=flops, bytes_accessed=size, transcendentals=0),
             name=name,
         )(place, *arrays)
@@ -72,7 +72,7 @@
         in_specs=[pl.BlockSpec(memory_space=pl.ANY)],
         out_specs=(VMEM, VMEM),
         scratch_shapes=[pltpu.SemaphoreType.DMA((2 * members,))],
-        compiler_params=pltpu.CompilerParams(vmem_limit_bytes=(56 if flip else 24) * 2**20),
+        compiler_params=pltpu.CompilerParams(vmem_limit_bytes=(56 if flip else 16) * 2**20),
         cost_estimate=pl.CostEstimate(flops=0, bytes_accessed=8 * members * rows * width, transcendentals=0),
         name="cut",
     )(grads)
@@ -203,7 +203,7 @@
         jax.ShapeDtypeStruct((8, 128), f32),
     )
     kernel = functools.partial(product_kernel, members, rows)
-    return call(kernel, out_shape, "product", 8 * rows * width * width)(place, *grad_pieces, right_full, left_pair)
+    return call(kernel, out_shape, "product", 8 * rows * width * width, 16)(place, *grad_pieces, right_full, left_pair)
 
 
 def per_device(devices, groups, grad_partial, left_stat, right_stat, left_root, right_root, second_moment):

time: 172 us -> 172 us (level)
  no operation moved by 1% of the time
where the time goes in v4:
time: 172 us; the launch traced here: 171 us
  waiting for transfers between devices  94.2 us (55%)
  starting transfers between devices  42.6 us (25%)
  Pallas kernels  12.8 us (7%)
  local copies, waits for them, and re-layouts  10.8 us (6%)
  other arithmetic  6.51 us (4%)
  between operations  2.52 us (1%)
    ppermute x23, waiting for transfers between devices, swap(): lax.ppermute(array, 'dp', [(i, i ^ 1 << bit) for i in range(devices)])  89.6 us
    ppermute x23, starting transfers between devices, swap(): lax.ppermute(array, 'dp', [(i, i ^ 1 << bit) for i in range(devices)])  35 us
    pallas_call x9, Pallas kernels, run(): pl.pallas_call(kernel, out_shape=out_shape, in_specs=[SMEM] + [VMEM] * le...  9.65 us
    unnamed x52, local copies, waits for them, and re-layouts  8.98 us
    ppermute x3, starting transfers between devices, gather_direct(): pieces[k] = lax.ppermute(own, 'dp', [(i, i ^ k) for i in range(devices)])  4.05 us
  transfers between devices with their start and end apart: 30, of which 13 were waited for; matrix products, arithmetic and copies ran while one was open for 6% of the time, Pallas kernels for 5%

profile of v4, /device:TPU:0, one launch (start us, length us, event | category | flops | bytes accessed | tf_op | source)
XLA Modules:
  0.0 171.2 jit_solution(10911531173567766096)
XLA Ops:
  0.6 3.0 %cut.2 = (bf16[4,128,1024]{2,1,0:T(8,128)(2,1)}, bf16[4,128,1024]{2,1,0:T(8,128)(2,1)}) custom-call(bf16[2,2,4,128,1024]{4,3,2,1,0:T(8,128)(2,1)} %bitcast.103), custom_call_target="tpu_custom_call" | custom-call | bytes 4194304 | tf_op jit(solution)/shard_map/cut/pallas_call | solution.py:69
  3.6 3.0 %collective-permute-start = (bf16[4,128,1024]{2,1,0:T(8,128)(2,1)}, bf16[4,128,1024]{2,1,0:T(8,128)(2,1)S(1)}, u32[]{:S(2)}, u32[]{:S(2)}) collective-permute-start(bf16[4,128,1024]{2,1,0:T(8,128)(2,1)} %get-tuple-element.34), channel_id=1, source_target_pairs={{0,4},{4,0},{8,12},{12,8},{16,20},{20,16},{24,28},{28,24},{1,5},{5... | collective-permute-start | bytes 3145736 | tf_op jit(solution)/shard_map/ppermute | solution.py:218
  6.6 1.6 collective-permute-start.3
  8.2 0.7 dynamic-slice_bitcast_fusion.1
  8.9 2.6 %collective-permute-start.1 = (bf16[128,1024]{1,0:T(8,128)(2,1)}, bf16[128,1024]{1,0:T(8,128)(2,1)S(1)}, u32[]{:S(2)}, u32[]{:S(2)}) collective-permute-start(bf16[128,1024]{1,0:T(8,128)(2,1)} %dynamic-slice_bitcast_fusion.1), channel_id=1, source_target_pairs={{0,16},{4,20},{8,24},{12,28},{16,0},{20,4},{24,8},{28,12},{1,17},{... | collective-permute-start | bytes 786440 | tf_op jit(solution)/shard_map/ppermute | solution.py:218
  11.5 2.2 %copy-done = bf16[1,2,1024,1024]{3,2,1,0:T(8,128)(2,1)S(1)} copy-done((bf16[1,2,1024,1024]{3,2,1,0:T(8,128)(2,1)S(1)}, bf16[1,2,1024,1024]{3,2,1,0:T(8,128)(2,1)}, u32[]{:S(2)}) %copy-start) | copy-done | bytes 4194328
  14.0 1.0 copy-done.1
  15.0 21.3 %collective-permute-done.1.partner_ref = bf16[128,1024]{1,0:T(8,128)(2,1)S(1)} collective-permute-done((bf16[128,1024]{1,0:T(8,128)(2,1)}, bf16[128,1024]{1,0:T(8,128)(2,1)S(1)}, u32[]{:S(2)}, u32[]{:S(2)}) %collective-permute-start.1) | collective-permute-done | bytes 262176 | tf_op jit(solution)/shard_map/ppermute | solution.py:218
  36.3 0.7 copy-done.14
  37.0 1.2 copy-done.2
  38.2 0.7 sum_pieces.6
  38.9 3.5 %collective-permute-start.2 = (bf16[2,128,1024]{2,1,0:T(8,128)(2,1)S(1)}, bf16[2,128,1024]{2,1,0:T(8,128)(2,1)S(1)}, u32[]{:S(2)}, u32[]{:S(2)}) collective-permute-start(bf16[2,128,1024]{2,1,0:T(8,128)(2,1)S(1)} %sum_pieces.6), channel_id=1, source_target_pairs={{0,8},{4,12},{8,0},{12,4},{16,24},{20,28},{24,16},{28,20},{1,9},{5... | collective-permute-start | bytes 1572872 | tf_op jit(solution)/shard_map/ppermute | solution.py:218
  42.4 0.7 sum_pieces.7
  43.0 0.6 collective-permute-start.4
  43.7 0.7 pack.1
  44.4 13.6 %collective-permute-done.5 = bf16[128,1024]{1,0:T(8,128)(2,1)S(1)} collective-permute-done((bf16[128,1024]{1,0:T(8,128)(2,1)S(1)}, bf16[128,1024]{1,0:T(8,128)(2,1)S(1)}, u32[]{:S(2)}, u32[]{:S(2)}) %collective-permute-start.5) | collective-permute-done | bytes 262176 | tf_op jit(solution)/shard_map/ppermute | solution.py:218
  58.0 0.7 collective-permute-done.2.refs_2_
  58.7 0.6 sum_pieces.8
  59.4 1.7 %collective-permute-start.8 = (bf16[9,128,128]{2,1,0:T(8,128)(2,1)S(1)}, bf16[9,128,128]{2,1,0:T(8,128)(2,1)S(1)}, u32[]{:S(2)}, u32[]{:S(2)}) collective-permute-start(bf16[9,128,128]{2,1,0:T(8,128)(2,1)S(1)} %get-tuple-element.45), channel_id=1, source_target_pairs={{0,8},{4,12},{8,0},{12,4},{16,24},{20,28},{24,16},{28,20},{1,9},{5... | collective-permute-start | bytes 884744 | tf_op jit(solution)/shard_map/ppermute | solution.py:218
  61.1 0.5 collective-permute-start.9
  61.6 1.1 collective-permute-start.6
  62.7 8.5 %collective-permute-done.6 = bf16[128,1024]{1,0:T(8,128)(2,1)S(1)} collective-permute-done((bf16[128,1024]{1,0:T(8,128)(2,1)S(1)}, bf16[128,1024]{1,0:T(8,128)(2,1)S(1)}, u32[]{:S(2)}, u32[]{:S(2)}) %collective-permute-start.6) | collective-permute-done | bytes 262176 | tf_op jit(solution)/shard_map/ppermute | solution.py:218
  71.2 0.7 sum_pieces.9
  71.9 1.4 sum_pieces.10
  73.2 3.2 %collective-permute-start.7 = (bf16[128,1024]{1,0:T(8,128)(2,1)}, bf16[128,1024]{1,0:T(8,128)(2,1)}, u32[]{:S(2)}, u32[]{:S(2)}) collective-permute-start(bf16[128,1024]{1,0:T(8,128)(2,1)} %bitcast.9), channel_id=1, source_target_pairs={{0,16},{4,20},{8,24},{12,28},{16,0},{20,4},{24,8},{28,12},{1,17},{... | collective-permute-start | bytes 786440 | tf_op jit(solution)/shard_map/ppermute | solution.py:218
  76.5 0.7 copy-done.10
  77.2 0.7 copy-done.12
  77.9 1.3 collective-permute-start.11
  79.2 2.4 %collective-permute-start.10 = (bf16[128,1024]{1,0:T(8,128)(2,1)S(1)}, bf16[128,1024]{1,0:T(8,128)(2,1)}, u32[]{:S(2)}, u32[]{:S(2)}) collective-permute-start(bf16[128,1024]{1,0:T(8,128)(2,1)S(1)} %bitcast.106), channel_id=1, source_target_pairs={{0,8},{4,12},{8,0},{12,4},{16,24},{20,28},{24,16},{28,20},{1,9},{5... | collective-permute-start | bytes 786440 | tf_op jit(solution)/shard_map/ppermute | solution.py:218
  81.6 0.6 collective-permute-start.16
  82.2 1.1 fusion.31
  83.3 2.1 %collective-permute-done.7 = bf16[128,1024]{1,0:T(8,128)(2,1)} collective-permute-done((bf16[128,1024]{1,0:T(8,128)(2,1)}, bf16[128,1024]{1,0:T(8,128)(2,1)}, u32[]{:S(2)}, u32[]{:S(2)}) %collective-permute-start.7) | collective-permute-done | bytes 262176 | tf_op jit(solution)/shard_map/ppermute | solution.py:218
  85.4 1.1 sum_pieces.11
  86.5 1.4 collective-permute-done.10.refs_2_
  87.9 2.1 %collective-permute-start.13 = (bf16[128,1024]{1,0:T(8,128)(2,1)S(1)}, bf16[128,1024]{1,0:T(8,128)(2,1)S(1)}, u32[]{:S(2)}, u32[]{:S(2)}) collective-permute-start(bf16[128,1024]{1,0:T(8,128)(2,1)S(1)} %bitcast.108), channel_id=1, source_target_pairs={{0,4},{4,0},{8,12},{12,8},{16,20},{20,16},{24,28},{28,24},{1,5},{5... | collective-permute-start | bytes 786440 | tf_op jit(solution)/shard_map/ppermute | solution.py:234
  90.5 1.5 collective-permute-start.15
  92.0 1.6 collective-permute-start.12
  93.6 0.7 collective-permute-start.17
  94.5 1.1 unfold.1.refs_8_
  95.6 9.8 %collective-permute-done.12.refs_3_ = bf16[128,1024]{1,0:T(8,128)(2,1)S(1)} collective-permute-done((bf16[128,1024]{1,0:T(8,128)(2,1)}, bf16[128,1024]{1,0:T(8,128)(2,1)S(1)}, u32[]{:S(2)}, u32[]{:S(2)}) %collective-permute-start.12) | collective-permute-done | bytes 262176 | tf_op jit(solution)/shard_map/ppermute | solution.py:218
  105.4 2.8 %product.1 = (bf16[256,1024]{1,0:T(8,128)(2,1)S(1)}, bf16[1024,1024]{1,0:T(8,128)(2,1)S(1)}, f32[8,128]{1,0:T(8,128)S(1)}) custom-call(s32[3]{0:T(128)S(1)} %pad_add_fusion.place_ref, bf16[128,1024]{1,0:T(8,128)(2,1)S(1)} %bitcast.107, bf16[128,1024]{1,0:T(8,128)(2,1)} %collective-permute-done.11.refs_1_, bf16[128,1024]{1,0:T(8,128)(2,1)} %collective-permute-done.10.refs_2_, ...), custom_call_target="tpu_custom_call" | custom-call | flops 1073741824 | bytes 4718592 | tf_op jit(solution)/shard_map/product/pallas_call | solution.py:31
  108.2 1.7 collective-permute-start.22
  109.9 2.2 %collective-permute-start.23 = (bf16[2,128,1024]{2,1,0:T(8,128)(2,1)S(1)}, bf16[2,128,1024]{2,1,0:T(8,128)(2,1)S(1)}, u32[]{:S(2)}, u32[]{:S(2)}) collective-permute-start(bf16[2,128,1024]{2,1,0:T(8,128)(2,1)S(1)} %bitcast.114), channel_id=1, source_target_pairs={{0,8},{4,12},{8,0},{12,4},{16,24},{20,28},{24,16},{28,20},{1,9},{5... | collective-permute-start | bytes 1572872 | tf_op jit(solution)/shard_map/ppermute | solution.py:218
  112.1 1.7 collective-permute-start.24
  113.9 2.1 %fusion.4 = (f32[]{:T(128)}, f32[2,128,1024]{2,1,0:T(8,128)}) fusion(bf16[1,128,1024]{2,1,0:T(8,128)(2,1)S(1)} %get-tuple-element.67, bf16[1,128,1024]{2,1,0:T(8,128)(2,1)S(1)} %get-tuple-element.66, f32[2,128,1024]{2,1,0:T(8,128)S(1)} %copy-done.23), kind=kLoop, calls=%fused_computation.21 | loop fusion | flops 2621439 | bytes 2621444 | tf_op jit(solution)/shard_map/reduce_sum | solution.py:330
  116.0 0.6 broadcast_select_fusion
  116.8 0.7 fusion
  117.5 0.5 convolution_bitcast_fusion.1
  118.0 0.7 fusion.42
  118.7 1.6 collective-permute-start.19
  120.3 0.5 convolution_bitcast_fusion
  120.7 1.6 collective-permute-done.19
  123.1 2.9 %collective-permute-done.20 = f32[8,128]{1,0:T(8,128)S(1)} collective-permute-done((f32[8,128]{1,0:T(8,128)S(1)}, f32[8,128]{1,0:T(8,128)S(1)}, u32[]{:S(2)}, u32[]{:S(2)}) %collective-permute-start.20) | collective-permute-done | bytes 4128 | tf_op jit(solution)/shard_map/ppermute | solution.py:218
  126.0 3.8 %collective-permute-done.22 = bf16[2,128,1024]{2,1,0:T(8,128)(2,1)S(1)} collective-permute-done((bf16[2,128,1024]{2,1,0:T(8,128)(2,1)S(1)}, bf16[2,128,1024]{2,1,0:T(8,128)(2,1)S(1)}, u32[]{:S(2)}, u32[]{:S(2)}) %collective-permute-start.22) | collective-permute-done | bytes 524320 | tf_op jit(solution)/shard_map/ppermute | solution.py:218
  130.1 0.6 collective-permute-start.26
  130.9 3.3 %collective-permute-start.25 = (f32[8,128]{1,0:T(8,128)S(1)}, f32[8,128]{1,0:T(8,128)S(1)}, u32[]{:S(2)}, u32[]{:S(2)}) collective-permute-start(f32[8,128]{1,0:T(8,128)S(1)} %add.110), channel_id=1, source_target_pairs={{0,16},{4,20},{8,24},{12,28},{16,0},{20,4},{24,8},{28,12},{1,17},{... | collective-permute-start | bytes 12296 | tf_op jit(solution)/shard_map/ppermute | solution.py:218
  134.2 1.3 collective-permute-start.27
  135.5 0.6 collective-permute-start.28
  136.1 0.8 collective-permute-start.29
  136.9 0.6 fusion.38
  138.9 0.5 broadcast_in_dim.31
  139.8 25.3 %collective-permute-done.26 = bf16[2,2,128,1024]{3,2,1,0:T(8,128)(2,1)S(1)} collective-permute-done((bf16[2,2,128,1024]{3,2,1,0:T(8,128)(2,1)S(1)}, bf16[2,2,128,1024]{3,2,1,0:T(8,128)(2,1)S(1)}, u32[]{:S(2)}, u32[]{:S(2)}) %collective-permute-start.26) | collective-permute-done | bytes 1048608 | tf_op jit(solution)/shard_map/ppermute | solution.py:218
  165.5 2.9 %collective-permute-done.28 = bf16[2,128,1024]{2,1,0:T(8,128)(2,1)S(1)} collective-permute-done((bf16[2,128,1024]{2,1,0:T(8,128)(2,1)S(1)}, bf16[2,128,1024]{2,1,0:T(8,128)(2,1)S(1)}, u32[]{:S(2)}, u32[]{:S(2)}) %collective-permute-start.28) | collective-permute-done | bytes 524320 | tf_op jit(solution)/shard_map/ppermute | solution.py:361
  168.8 1.7 %copy-done.16 = bf16[2,2,4,128,1024]{4,3,2,1,0:T(8,128)(2,1)} copy-done((bf16[2,2,4,128,1024]{4,3,2,1,0:T(8,128)(2,1)}, bf16[2,2,4,128,1024]{4,3,2,1,0:T(8,128)(2,1)S(1)}, u32[]{:S(2)}) %copy-start.16) | copy-done | bytes 4194328
  (93 shorter events, 4.2 us)
Async XLA Ops:
  0.6 7.6 %copy-start.6 = (bf16[2,128,1024]{2,1,0:T(8,128)(2,1)S(1)}, bf16[2,128,1024]{2,1,0:T(8,128)(2,1)}, u32[]{:S(2)}) copy-start(bf16[2,128,1024]{2,1,0:T(8,128)(2,1)} %own_ref.1) | copy-start | bytes 1572868
  3.6 33.4 %collective-permute-start = (bf16[4,128,1024]{2,1,0:T(8,128)(2,1)}, bf16[4,128,1024]{2,1,0:T(8,128)(2,1)S(1)}, u32[]{:S(2)}, u32[]{:S(2)}) collective-permute-start(bf16[4,128,1024]{2,1,0:T(8,128)(2,1)} %get-tuple-element.34), channel_id=1, source_target_pairs={{0,4},{4,0},{8,12},{12,8},{16,20},{20,16},{24,28},{28,24},{1,5},{5... | collective-permute-start | bytes 3145736 | tf_op jit(solution)/shard_map/ppermute | solution.py:218
  6.6 35.7 %collective-permute-start.3 = (bf16[4,128,1024]{2,1,0:T(8,128)(2,1)}, bf16[4,128,1024]{2,1,0:T(8,128)(2,1)S(1)}, u32[]{:S(2)}, u32[]{:S(2)}) collective-permute-start(bf16[4,128,1024]{2,1,0:T(8,128)(2,1)} %get-tuple-element.35), channel_id=1, source_target_pairs={{0,8},{4,12},{8,0},{12,4},{16,24},{20,28},{24,16},{28,20},{1,9},{5... | collective-permute-start | bytes 3145736 | tf_op jit(solution)/shard_map/ppermute | solution.py:218
  8.9 27.3 %collective-permute-start.1 = (bf16[128,1024]{1,0:T(8,128)(2,1)}, bf16[128,1024]{1,0:T(8,128)(2,1)S(1)}, u32[]{:S(2)}, u32[]{:S(2)}) collective-permute-start(bf16[128,1024]{1,0:T(8,128)(2,1)} %dynamic-slice_bitcast_fusion.1), channel_id=1, source_target_pairs={{0,16},{4,20},{8,24},{12,28},{16,0},{20,4},{24,8},{28,12},{1,17},{... | collective-permute-start | bytes 786440 | tf_op jit(solution)/shard_map/ppermute | solution.py:218
  11.5 2.2 %copy-start = (bf16[1,2,1024,1024]{3,2,1,0:T(8,128)(2,1)S(1)}, bf16[1,2,1024,1024]{3,2,1,0:T(8,128)(2,1)}, u32[]{:S(2)}) copy-start(bf16[1,2,1024,1024]{3,2,1,0:T(8,128)(2,1)} %param.6) | copy-start | bytes 12582916
  13.9 1.0 copy-start.1
  36.3 0.7 copy-start.14
  37.0 1.2 copy-start.2
  38.2 5.4 %copy-start.24 = (bf16[2,128,1024]{2,1,0:T(8,128)(2,1)S(1)}, bf16[2,128,1024]{2,1,0:T(8,128)(2,1)}, u32[]{:S(2)}) copy-start(bf16[2,128,1024]{2,1,0:T(8,128)(2,1)} %param.9) | copy-start | bytes 1572868
  38.2 5.5 %copy-start.7 = (bf16[2,128,1024]{2,1,0:T(8,128)(2,1)S(1)}, bf16[2,128,1024]{2,1,0:T(8,128)(2,1)}, u32[]{:S(2)}) copy-start(bf16[2,128,1024]{2,1,0:T(8,128)(2,1)} %own_ref.1) | copy-start | bytes 1572868
  38.2 5.5 %copy-start.15 = (bf16[128,1024]{1,0:T(8,128)(2,1)S(1)}, bf16[128,1024]{1,0:T(8,128)(2,1)}, u32[]{:S(2)}) copy-start(bf16[128,1024]{1,0:T(8,128)(2,1)} %copy-done.14) | copy-start | bytes 786436
  38.2 20.5 %copy-start.3 = (bf16[4,128,1024]{2,1,0:T(8,128)(2,1)S(1)}, bf16[4,128,1024]{2,1,0:T(8,128)(2,1)}, u32[]{:S(2)}) copy-start(bf16[4,128,1024]{2,1,0:T(8,128)(2,1)} %copy-done.1) | copy-start | bytes 3145732
  38.9 19.8 %collective-permute-start.2 = (bf16[2,128,1024]{2,1,0:T(8,128)(2,1)S(1)}, bf16[2,128,1024]{2,1,0:T(8,128)(2,1)S(1)}, u32[]{:S(2)}, u32[]{:S(2)}) collective-permute-start(bf16[2,128,1024]{2,1,0:T(8,128)(2,1)S(1)} %sum_pieces.6), channel_id=1, source_target_pairs={{0,8},{4,12},{8,0},{12,4},{16,24},{20,28},{24,16},{28,20},{1,9},{5... | collective-permute-start | bytes 1572872 | tf_op jit(solution)/shard_map/ppermute | solution.py:218
  43.0 15.7 %collective-permute-start.4 = (bf16[2,128,1024]{2,1,0:T(8,128)(2,1)S(1)}, bf16[2,128,1024]{2,1,0:T(8,128)(2,1)S(1)}, u32[]{:S(2)}, u32[]{:S(2)}) collective-permute-start(bf16[2,128,1024]{2,1,0:T(8,128)(2,1)S(1)} %sum_pieces.7), channel_id=1, source_target_pairs={{0,4},{4,0},{8,12},{12,8},{16,20},{20,16},{24,28},{28,24},{1,5},{5... | collective-permute-start | bytes 1572872 | tf_op jit(solution)/shard_map/ppermute | solution.py:218
  43.6 14.3 %collective-permute-start.5 = (bf16[128,1024]{1,0:T(8,128)(2,1)S(1)}, bf16[128,1024]{1,0:T(8,128)(2,1)S(1)}, u32[]{:S(2)}, u32[]{:S(2)}) collective-permute-start(bf16[128,1024]{1,0:T(8,128)(2,1)S(1)} %dynamic-slice_bitcast_fusion), channel_id=1, source_target_pairs={{0,16},{4,20},{8,24},{12,28},{16,0},{20,4},{24,8},{28,12},{1,17},{... | collective-permute-start | bytes 786440 | tf_op jit(solution)/shard_map/ppermute | solution.py:218
  44.4 28.8 %copy-start.8 = (bf16[2,128,1024]{2,1,0:T(8,128)(2,1)}, bf16[2,128,1024]{2,1,0:T(8,128)(2,1)S(1)}, u32[]{:S(2)}) copy-start(bf16[2,128,1024]{2,1,0:T(8,128)(2,1)S(1)} %get-tuple-element.48.pair_ref) | copy-start | bytes 1572868
  58.0 13.2 %copy-start.25 = (bf16[128,1024]{1,0:T(8,128)(2,1)}, bf16[128,1024]{1,0:T(8,128)(2,1)S(1)}, u32[]{:S(2)}) copy-start(bf16[128,1024]{1,0:T(8,128)(2,1)S(1)} %collective-permute-done.5) | copy-start | bytes 786436
  58.7 14.5 %copy-start.4 = (bf16[2,128,1024]{2,1,0:T(8,128)(2,1)}, bf16[2,128,1024]{2,1,0:T(8,128)(2,1)S(1)}, u32[]{:S(2)}) copy-start(bf16[2,128,1024]{2,1,0:T(8,128)(2,1)S(1)} %collective-permute-done.4.refs_2_) | copy-start | bytes 1572868
  59.4 17.1 %collective-permute-start.8 = (bf16[9,128,128]{2,1,0:T(8,128)(2,1)S(1)}, bf16[9,128,128]{2,1,0:T(8,128)(2,1)S(1)}, u32[]{:S(2)}, u32[]{:S(2)}) collective-permute-start(bf16[9,128,128]{2,1,0:T(8,128)(2,1)S(1)} %get-tuple-element.45), channel_id=1, source_target_pairs={{0,8},{4,12},{8,0},{12,4},{16,24},{20,28},{24,16},{28,20},{1,9},{5... | collective-permute-start | bytes 884744 | tf_op jit(solution)/shard_map/ppermute | solution.py:218
  61.1 15.4 %collective-permute-start.9 = (bf16[9,128,128]{2,1,0:T(8,128)(2,1)S(1)}, bf16[9,128,128]{2,1,0:T(8,128)(2,1)S(1)}, u32[]{:S(2)}, u32[]{:S(2)}) collective-permute-start(bf16[9,128,128]{2,1,0:T(8,128)(2,1)S(1)} %get-tuple-element.45), channel_id=1, source_target_pairs={{0,4},{4,0},{8,12},{12,8},{16,20},{20,16},{24,28},{28,24},{1,5},{5... | collective-permute-start | bytes 884744 | tf_op jit(solution)/shard_map/ppermute | solution.py:218
  61.6 9.6 %collective-permute-start.6 = (bf16[128,1024]{1,0:T(8,128)(2,1)S(1)}, bf16[128,1024]{1,0:T(8,128)(2,1)S(1)}, u32[]{:S(2)}, u32[]{:S(2)}) collective-permute-start(bf16[128,1024]{1,0:T(8,128)(2,1)S(1)} %bitcast.117), channel_id=1, source_target_pairs={{0,16},{4,20},{8,24},{12,28},{16,0},{20,4},{24,8},{28,12},{1,17},{... | collective-permute-start | bytes 786440 | tf_op jit(solution)/shard_map/ppermute | solution.py:218
  73.2 12.2 %copy-start.5 = (bf16[2,128,1024]{2,1,0:T(8,128)(2,1)S(1)}, bf16[2,128,1024]{2,1,0:T(8,128)(2,1)}, u32[]{:S(2)}) copy-start(bf16[2,128,1024]{2,1,0:T(8,128)(2,1)} %copy-done.4) | copy-start | bytes 1572868
  73.2 12.2 %collective-permute-start.7 = (bf16[128,1024]{1,0:T(8,128)(2,1)}, bf16[128,1024]{1,0:T(8,128)(2,1)}, u32[]{:S(2)}, u32[]{:S(2)}) collective-permute-start(bf16[128,1024]{1,0:T(8,128)(2,1)} %bitcast.9), channel_id=1, source_target_pairs={{0,16},{4,20},{8,24},{12,28},{16,0},{20,4},{24,8},{28,12},{1,17},{... | collective-permute-start | bytes 786440 | tf_op jit(solution)/shard_map/ppermute | solution.py:218
  76.4 0.7 copy-start.10
  77.2 0.7 copy-start.12
  77.9 8.6 %collective-permute-start.11 = (bf16[128,1024]{1,0:T(8,128)(2,1)S(1)}, bf16[128,1024]{1,0:T(8,128)(2,1)}, u32[]{:S(2)}, u32[]{:S(2)}) collective-permute-start(bf16[128,1024]{1,0:T(8,128)(2,1)S(1)} %bitcast.105), channel_id=1, source_target_pairs={{0,4},{4,0},{8,12},{12,8},{16,20},{20,16},{24,28},{28,24},{1,5},{5... | collective-permute-start | bytes 786440 | tf_op jit(solution)/shard_map/ppermute | solution.py:218
  79.2 8.8 %collective-permute-start.10 = (bf16[128,1024]{1,0:T(8,128)(2,1)S(1)}, bf16[128,1024]{1,0:T(8,128)(2,1)}, u32[]{:S(2)}, u32[]{:S(2)}) collective-permute-start(bf16[128,1024]{1,0:T(8,128)(2,1)S(1)} %bitcast.106), channel_id=1, source_target_pairs={{0,8},{4,12},{8,0},{12,4},{16,24},{20,28},{24,16},{28,20},{1,9},{5... | collective-permute-start | bytes 786440 | tf_op jit(solution)/shard_map/ppermute | solution.py:218
  81.6 12.8 %copy-start.9 = (bf16[2,128,1024]{2,1,0:T(8,128)(2,1)S(1)}, bf16[2,128,1024]{2,1,0:T(8,128)(2,1)}, u32[]{:S(2)}) copy-start(bf16[2,128,1024]{2,1,0:T(8,128)(2,1)} %copy-done.8) | copy-start | bytes 1572868
  81.6 12.8 %copy-start.11 = (bf16[9,128,128]{2,1,0:T(8,128)(2,1)S(1)}, bf16[9,128,128]{2,1,0:T(8,128)(2,1)}, u32[]{:S(2)}) copy-start(bf16[9,128,128]{2,1,0:T(8,128)(2,1)} %copy-done.10) | copy-start | bytes 884740
  81.6 12.8 %copy-start.13 = (bf16[9,128,128]{2,1,0:T(8,128)(2,1)S(1)}, bf16[9,128,128]{2,1,0:T(8,128)(2,1)}, u32[]{:S(2)}) copy-start(bf16[9,128,128]{2,1,0:T(8,128)(2,1)} %copy-done.12) | copy-start | bytes 884740
  81.6 12.0 %collective-permute-start.16 = (bf16[9,128,128]{2,1,0:T(8,128)(2,1)}, bf16[9,128,128]{2,1,0:T(8,128)(2,1)S(1)}, u32[]{:S(2)}, u32[]{:S(2)}) collective-permute-start(bf16[9,128,128]{2,1,0:T(8,128)(2,1)} %copy-done.10), channel_id=1, source_target_pairs={{0,4},{4,0},{8,12},{12,8},{16,20},{20,16},{24,28},{28,24},{1,5},{5... | collective-permute-start | bytes 884744 | tf_op jit(solution)/shard_map/ppermute | solution.py:218
  87.9 17.5 %collective-permute-start.13 = (bf16[128,1024]{1,0:T(8,128)(2,1)S(1)}, bf16[128,1024]{1,0:T(8,128)(2,1)S(1)}, u32[]{:S(2)}, u32[]{:S(2)}) collective-permute-start(bf16[128,1024]{1,0:T(8,128)(2,1)S(1)} %bitcast.108), channel_id=1, source_target_pairs={{0,4},{4,0},{8,12},{12,8},{16,20},{20,16},{24,28},{28,24},{1,5},{5... | collective-permute-start | bytes 786440 | tf_op jit(solution)/shard_map/ppermute | solution.py:234
  90.0 15.3 %collective-permute-start.14 = (bf16[128,1024]{1,0:T(8,128)(2,1)S(1)}, bf16[128,1024]{1,0:T(8,128)(2,1)S(1)}, u32[]{:S(2)}, u32[]{:S(2)}) collective-permute-start(bf16[128,1024]{1,0:T(8,128)(2,1)S(1)} %bitcast.109), channel_id=1, source_target_pairs={{0,8},{4,12},{8,0},{12,4},{16,24},{20,28},{24,16},{28,20},{1,9},{5... | collective-permute-start | bytes 786440 | tf_op jit(solution)/shard_map/ppermute | solution.py:234
  90.5 14.9 %collective-permute-start.15 = (bf16[128,1024]{1,0:T(8,128)(2,1)S(1)}, bf16[128,1024]{1,0:T(8,128)(2,1)S(1)}, u32[]{:S(2)}, u32[]{:S(2)}) collective-permute-start(bf16[128,1024]{1,0:T(8,128)(2,1)S(1)} %bitcast.110), channel_id=1, source_target_pairs={{0,12},{4,8},{8,4},{12,0},{16,28},{20,24},{24,20},{28,16},{1,13},{... | collective-permute-start | bytes 786440 | tf_op jit(solution)/shard_map/ppermute | solution.py:234
  92.0 13.4 %collective-permute-start.12 = (bf16[128,1024]{1,0:T(8,128)(2,1)}, bf16[128,1024]{1,0:T(8,128)(2,1)S(1)}, u32[]{:S(2)}, u32[]{:S(2)}) collective-permute-start(bf16[128,1024]{1,0:T(8,128)(2,1)} %collective-permute-done.10.refs_2_), channel_id=1, source_target_pairs={{0,4},{4,0},{8,12},{12,8},{16,20},{20,16},{24,28},{28,24},{1,5},{5... | collective-permute-start | bytes 786440 | tf_op jit(solution)/shard_map/ppermute | solution.py:218
  93.6 20.2 %collective-permute-start.17 = (bf16[128,1024]{1,0:T(8,128)(2,1)S(1)}, bf16[128,1024]{1,0:T(8,128)(2,1)S(1)}, u32[]{:S(2)}, u32[]{:S(2)}) collective-permute-start(bf16[128,1024]{1,0:T(8,128)(2,1)S(1)} %fusion.28), channel_id=1, source_target_pairs={{0,16},{4,20},{8,24},{12,28},{16,0},{20,4},{24,8},{28,12},{1,17},{... | collective-permute-start | bytes 786440 | tf_op jit(solution)/shard_map/ppermute | solution.py:218
  94.4 19.4 %copy-start.23 = (f32[2,128,1024]{2,1,0:T(8,128)S(1)}, f32[2,128,1024]{2,1,0:T(8,128)}, u32[]{:S(2)}) copy-start(f32[2,128,1024]{2,1,0:T(8,128)} %param.11) | copy-start | bytes 3145732
  108.2 21.7 %collective-permute-start.22 = (bf16[2,128,1024]{2,1,0:T(8,128)(2,1)S(1)}, bf16[2,128,1024]{2,1,0:T(8,128)(2,1)S(1)}, u32[]{:S(2)}, u32[]{:S(2)}) collective-permute-start(bf16[2,128,1024]{2,1,0:T(8,128)(2,1)S(1)} %bitcast.113), channel_id=1, source_target_pairs={{0,16},{4,20},{8,24},{12,28},{16,0},{20,4},{24,8},{28,12},{1,17},{... | collective-permute-start | bytes 1572872 | tf_op jit(solution)/shard_map/ppermute | solution.py:218
  109.9 20.1 %collective-permute-start.23 = (bf16[2,128,1024]{2,1,0:T(8,128)(2,1)S(1)}, bf16[2,128,1024]{2,1,0:T(8,128)(2,1)S(1)}, u32[]{:S(2)}, u32[]{:S(2)}) collective-permute-start(bf16[2,128,1024]{2,1,0:T(8,128)(2,1)S(1)} %bitcast.114), channel_id=1, source_target_pairs={{0,8},{4,12},{8,0},{12,4},{16,24},{20,28},{24,16},{28,20},{1,9},{5... | collective-permute-start | bytes 1572872 | tf_op jit(solution)/shard_map/ppermute | solution.py:218
  112.1 17.9 %collective-permute-start.24 = (bf16[2,128,1024]{2,1,0:T(8,128)(2,1)S(1)}, bf16[2,128,1024]{2,1,0:T(8,128)(2,1)S(1)}, u32[]{:S(2)}, u32[]{:S(2)}) collective-permute-start(bf16[2,128,1024]{2,1,0:T(8,128)(2,1)S(1)} %bitcast.115), channel_id=1, source_target_pairs={{0,4},{4,0},{8,12},{12,8},{16,20},{20,16},{24,28},{28,24},{1,5},{5... | collective-permute-start | bytes 1572872 | tf_op jit(solution)/shard_map/ppermute | solution.py:218
  116.7 1.4 collective-permute-start.18
  116.8 5.9 %copy-start.19 = (f32[2,128,1024]{2,1,0:T(8,128)S(1)}, f32[2,128,1024]{2,1,0:T(8,128)}, u32[]{:S(2)}) copy-start(f32[2,128,1024]{2,1,0:T(8,128)} %param.8) | copy-start | bytes 3145732
  116.8 5.9 %copy-start.22 = (f32[2,128,1024]{2,1,0:T(8,128)S(1)}, f32[2,128,1024]{2,1,0:T(8,128)}, u32[]{:S(2)}) copy-start(f32[2,128,1024]{2,1,0:T(8,128)} %param.7) | copy-start | bytes 3145732
  118.7 3.7 %collective-permute-start.19 = (f32[8,128]{1,0:T(8,128)S(1)}, f32[8,128]{1,0:T(8,128)S(1)}, u32[]{:S(2)}, u32[]{:S(2)}) collective-permute-start(f32[8,128]{1,0:T(8,128)S(1)} %fusion.42), channel_id=1, source_target_pairs={{0,2},{1,3},{2,0},{3,1},{4,6},{5,7},{6,4},{7,5},{8,10},{9,11},{10,... | collective-permute-start | bytes 12296 | tf_op jit(solution)/shard_map/ppermute | solution.py:335
  122.4 3.6 %collective-permute-start.20 = (f32[8,128]{1,0:T(8,128)S(1)}, f32[8,128]{1,0:T(8,128)S(1)}, u32[]{:S(2)}, u32[]{:S(2)}) collective-permute-start(f32[8,128]{1,0:T(8,128)S(1)} %add.108), channel_id=1, source_target_pairs={{0,4},{4,0},{8,12},{12,8},{16,20},{20,16},{24,28},{28,24},{1,5},{5... | collective-permute-start | bytes 12296 | tf_op jit(solution)/shard_map/ppermute | solution.py:218
  126.0 4.8 %collective-permute-start.21 = (f32[8,128]{1,0:T(8,128)S(1)}, f32[8,128]{1,0:T(8,128)S(1)}, u32[]{:S(2)}, u32[]{:S(2)}) collective-permute-start(f32[8,128]{1,0:T(8,128)S(1)} %add.109), channel_id=1, source_target_pairs={{0,8},{4,12},{8,0},{12,4},{16,24},{20,28},{24,16},{28,20},{1,9},{5... | collective-permute-start | bytes 12296 | tf_op jit(solution)/shard_map/ppermute | solution.py:218
  130.1 35.0 %collective-permute-start.26 = (bf16[2,2,128,1024]{3,2,1,0:T(8,128)(2,1)S(1)}, bf16[2,2,128,1024]{3,2,1,0:T(8,128)(2,1)S(1)}, u32[]{:S(2)}, u32[]{:S(2)}) collective-permute-start(bf16[2,2,128,1024]{3,2,1,0:T(8,128)(2,1)S(1)} %pad_maximum_fusion), channel_id=1, source_target_pairs={{0,4},{4,0},{8,12},{12,8},{16,20},{20,16},{24,28},{28,24},{1,5},{5... | collective-permute-start | bytes 3145736 | tf_op jit(solution)/shard_map/ppermute | solution.py:218
  130.9 6.0 %collective-permute-start.25 = (f32[8,128]{1,0:T(8,128)S(1)}, f32[8,128]{1,0:T(8,128)S(1)}, u32[]{:S(2)}, u32[]{:S(2)}) collective-permute-start(f32[8,128]{1,0:T(8,128)S(1)} %add.110), channel_id=1, source_target_pairs={{0,16},{4,20},{8,24},{12,28},{16,0},{20,4},{24,8},{28,12},{1,17},{... | collective-permute-start | bytes 12296 | tf_op jit(solution)/shard_map/ppermute | solution.py:218
  134.2 31.2 %collective-permute-start.27 = (bf16[2,128,1024]{2,1,0:T(8,128)(2,1)S(1)}, bf16[2,128,1024]{2,1,0:T(8,128)(2,1)S(1)}, u32[]{:S(2)}, u32[]{:S(2)}) collective-permute-start(bf16[2,128,1024]{2,1,0:T(8,128)(2,1)S(1)} %collective-permute-done.22), channel_id=1, source_target_pairs={{0,12},{4,8},{8,4},{12,0},{16,28},{20,24},{24,20},{28,16},{1,13},{... | collective-permute-start | bytes 1572872 | tf_op jit(solution)/shard_map/ppermute | solution.py:361
  135.5 32.9 %collective-permute-start.28 = (bf16[2,128,1024]{2,1,0:T(8,128)(2,1)S(1)}, bf16[2,128,1024]{2,1,0:T(8,128)(2,1)S(1)}, u32[]{:S(2)}, u32[]{:S(2)}) collective-permute-start(bf16[2,128,1024]{2,1,0:T(8,128)(2,1)S(1)} %collective-permute-done.22), channel_id=1, source_target_pairs={{0,8},{4,12},{8,0},{12,4},{16,24},{20,28},{24,16},{28,20},{1,9},{5... | collective-permute-start | bytes 1572872 | tf_op jit(solution)/shard_map/ppermute | solution.py:361
  136.1 32.5 %collective-permute-start.29 = (bf16[2,128,1024]{2,1,0:T(8,128)(2,1)S(1)}, bf16[2,128,1024]{2,1,0:T(8,128)(2,1)S(1)}, u32[]{:S(2)}, u32[]{:S(2)}) collective-permute-start(bf16[2,128,1024]{2,1,0:T(8,128)(2,1)S(1)} %pad_maximum_fusion.4), channel_id=1, source_target_pairs={{0,16},{4,20},{8,24},{12,28},{16,0},{20,4},{24,8},{28,12},{1,17},{... | collective-permute-start | bytes 1572872 | tf_op jit(solution)/shard_map/ppermute | solution.py:218
  139.4 29.2 %copy-start.17 = (f32[2,128,1024]{2,1,0:T(8,128)S(1)}, f32[2,128,1024]{2,1,0:T(8,128)}, u32[]{:S(2)}) copy-start(f32[2,128,1024]{2,1,0:T(8,128)} %param.8) | copy-start | bytes 3145732
  139.4 29.2 %copy-start.20 = (f32[2,128,1024]{2,1,0:T(8,128)S(1)}, f32[2,128,1024]{2,1,0:T(8,128)}, u32[]{:S(2)}) copy-start(f32[2,128,1024]{2,1,0:T(8,128)} %param.7) | copy-start | bytes 3145732
  168.5 2.0 %copy-start.16 = (bf16[2,2,4,128,1024]{4,3,2,1,0:T(8,128)(2,1)}, bf16[2,2,4,128,1024]{4,3,2,1,0:T(8,128)(2,1)S(1)}, u32[]{:S(2)}) copy-start(bf16[2,2,4,128,1024]{4,3,2,1,0:T(8,128)(2,1)S(1)} %fusion.20) | copy-start | bytes 12582916
  168.8 2.1 %copy-start.18 = (f32[2,128,1024]{2,1,0:T(8,128)}, f32[2,128,1024]{2,1,0:T(8,128)S(1)}, u32[]{:S(2)}) copy-start(f32[2,128,1024]{2,1,0:T(8,128)S(1)} %get-tuple-element.70) | copy-start | bytes 3145732
  168.8 2.4 %copy-start.21 = (f32[2,128,1024]{2,1,0:T(8,128)}, f32[2,128,1024]{2,1,0:T(8,128)S(1)}, u32[]{:S(2)}) copy-start(f32[2,128,1024]{2,1,0:T(8,128)S(1)} %get-tuple-element.71) | copy-start | bytes 3145732

commit v5 on v2

--- a/solution.py
+++ b/solution.py
@@ -101,7 +101,8 @@
     free = [axis for axis in axes_lists[0] if axis not in places]
     shape = arrays[0].shape[-2:]
     kernel = functools.partial(sum_kernel, axes_lists, places, free)
-    out = call(kernel, jax.ShapeDtypeStruct((1 << len(free),) + shape, bf16), "sum_pieces")(place, *arrays)
+    out_shape = jax.ShapeDtypeStruct((1 << len(free),) + shape, bf16)
+    out = call(kernel, out_shape, "sum_pieces", 1 << 30)(place, *arrays)
     return out.reshape([2] * len(free) + list(shape))
 
 
@@ -270,13 +271,6 @@
     def reduced(part):
         return sum_pieces(place, terms[part], places[part])
 
-    reduce_step(1, 0)
-    reduce_step(0, 0)
-    left_partner = swap(after(choose(left_root, 1 - half), terms[0][-1][0], terms[1][-1][0]), top)
-    for step in range(1, bits - 1):
-        reduce_step(0, step, right_partner, reduce_step(1, step, right_partner))
-    round_ends = [t[-1][0] for t in terms]
-
     halved = members == 4 and rows % 128 == 0
 
     def pair_rows(own, partner):
@@ -293,8 +287,16 @@
     def exchanged(pieces):
         return [pieces[1 << bit] for bit in member_axes]
 
+    right_pair, right_message = pair_rows(right_root, right_partner)
+    reduce_step(1, 0)
+    reduce_step(0, 0)
+    left_partner = swap(after(choose(left_root, 1 - half), terms[0][-1][0], terms[1][-1][0]), top)
+    for step in range(1, bits - 1):
+        for part in range(2):
+            reduce_step(part, step, right_message)
+    round_ends = [t[-1][0] for t in terms]
+
     last_send = reduce_step(0, bits - 1, *round_ends, left_partner)
-    right_pair, right_message = pair_rows(right_root, right_partner)
     right_pieces = gather_pieces(after(right_message, last_send))
     low = [reduced(0)]
     reduce_step(1, bits - 1, low[0])

time: 174 us -> 176 us (1.011)
  waiting for transfers between devices: 96.8 us -> 104 us
  starting transfers between devices: 42.8 us -> 36.1 us
    ppermute x23, starting transfers between devices: 34.7 us -> 28.2 us  [swap(): lax.ppermute(array, 'dp', [(i, i ^ 1 << bit) for i in range(devices)])]
    ppermute x23, waiting for transfers between devices: 89.9 us -> 95.7 us  [swap(): lax.ppermute(array, 'dp', [(i, i ^ 1 << bit) for i in range(devices)])]
    ppermute x3, waiting for transfers between devices: 0.01 us -> 5.21 us  [gather_direct(): pieces[k] = lax.ppermute(own, 'dp', [(i, i ^ k) for i in range(devices)])]
    ppermute x2, waiting for transfers between devices: 5.26 us -> 1.2 us  [per_device(): lax.ppermute(partner, 'dp', [(i, i ^ k) for i in range(devices)])]
    unnamed x52 -> x38, local copies, waits for them, and re-layouts: 8.96 us -> 9.02 us
  transfers between devices with their start and end apart: 30 -> 30, of which waited for: 14 -> 14; matrix products, arithmetic and copies ran while one was open for 6% -> 5% of each run, Pallas kernels for 5% -> 6%
where the time goes in v5:
time: 176 us; the launch traced here: 175 us
  waiting for transfers between devices  104 us (59%)
  starting transfers between devices  36.1 us (21%)
  Pallas kernels  14.5 us (8%)
  local copies, waits for them, and re-layouts  10.2 us (6%)
  other arithmetic  6.5 us (4%)
  between operations  2.54 us (1%)
    ppermute x23, waiting for transfers between devices, swap(): lax.ppermute(array, 'dp', [(i, i ^ 1 << bit) for i in range(devices)])  95.7 us
    ppermute x23, starting transfers between devices, swap(): lax.ppermute(array, 'dp', [(i, i ^ 1 << bit) for i in range(devices)])  28.2 us
    pallas_call x9, Pallas kernels, run(): pl.pallas_call(kernel, out_shape=out_shape, in_specs=[SMEM] + [VMEM] * le...  11.3 us
    unnamed x38, local copies, waits for them, and re-layouts  9.02 us
    ppermute x3, waiting for transfers between devices, gather_direct(): pieces[k] = lax.ppermute(own, 'dp', [(i, i ^ k) for i in range(devices)])  5.21 us
    ppermute x3, starting transfers between devices, gather_direct(): pieces[k] = lax.ppermute(own, 'dp', [(i, i ^ k) for i in range(devices)])  3.55 us
  transfers between devices with their start and end apart: 30, of which 14 were waited for; matrix products, arithmetic and copies ran while one was open for 5% of the time, Pallas kernels for 6%

profile of v5, /device:TPU:0, one launch (start us, length us, event | category | flops | bytes accessed | tf_op | source)
XLA Modules:
  0.0 175.2 jit_solution(5737770963012592461)
XLA Ops:
  0.6 3.0 %cut.2 = (bf16[4,128,1024]{2,1,0:T(8,128)(2,1)}, bf16[4,128,1024]{2,1,0:T(8,128)(2,1)}) custom-call(bf16[2,2,4,128,1024]{4,3,2,1,0:T(8,128)(2,1)} %bitcast.103), custom_call_target="tpu_custom_call" | custom-call | bytes 4194304 | tf_op jit(solution)/shard_map/cut/pallas_call | solution.py:69
  3.6 3.0 %collective-permute-start = (bf16[4,128,1024]{2,1,0:T(8,128)(2,1)}, bf16[4,128,1024]{2,1,0:T(8,128)(2,1)}, u32[]{:S(2)}, u32[]{:S(2)}) collective-permute-start(bf16[4,128,1024]{2,1,0:T(8,128)(2,1)} %get-tuple-element.34), channel_id=1, source_target_pairs={{0,4},{4,0},{8,12},{12,8},{16,20},{20,16},{24,28},{28,24},{1,5},{5... | collective-permute-start | bytes 3145736 | tf_op jit(solution)/shard_map/ppermute | solution.py:219
  6.6 1.6 collective-permute-start.3
  8.2 2.7 %collective-permute-start.1 = (bf16[128,1024]{1,0:T(8,128)(2,1)S(1)}, bf16[128,1024]{1,0:T(8,128)(2,1)S(1)}, u32[]{:S(2)}, u32[]{:S(2)}) collective-permute-start(bf16[128,1024]{1,0:T(8,128)(2,1)S(1)} %dynamic-slice_bitcast_fusion.1), channel_id=1, source_target_pairs={{0,16},{4,20},{8,24},{12,28},{16,0},{20,4},{24,8},{28,12},{1,17},{... | collective-permute-start | bytes 786440 | tf_op jit(solution)/shard_map/ppermute | solution.py:219
  10.9 2.2 %copy-done = bf16[1,2,1024,1024]{3,2,1,0:T(8,128)(2,1)S(1)} copy-done((bf16[1,2,1024,1024]{3,2,1,0:T(8,128)(2,1)S(1)}, bf16[1,2,1024,1024]{3,2,1,0:T(8,128)(2,1)}, u32[]{:S(2)}) %copy-start) | copy-done | bytes 4194328
  13.1 0.2 cut.3
  13.3 1.0 copy-done.2
  14.3 1.0 copy-done.5
  15.3 20.8 %collective-permute-done.1.partner_ref = bf16[128,1024]{1,0:T(8,128)(2,1)S(1)} collective-permute-done((bf16[128,1024]{1,0:T(8,128)(2,1)S(1)}, bf16[128,1024]{1,0:T(8,128)(2,1)S(1)}, u32[]{:S(2)}, u32[]{:S(2)}) %collective-permute-start.1) | collective-permute-done | bytes 262176 | tf_op jit(solution)/shard_map/ppermute | solution.py:219
  36.2 0.7 pack.1
  36.9 1.2 copy-done.6
  38.1 1.4 sum_pieces.6
  39.5 3.6 %collective-permute-start.2 = (bf16[2,128,1024]{2,1,0:T(8,128)(2,1)S(1)}, bf16[2,128,1024]{2,1,0:T(8,128)(2,1)S(1)}, u32[]{:S(2)}, u32[]{:S(2)}) collective-permute-start(bf16[2,128,1024]{2,1,0:T(8,128)(2,1)S(1)} %sum_pieces.6), channel_id=1, source_target_pairs={{0,8},{4,12},{8,0},{12,4},{16,24},{20,28},{24,16},{28,20},{1,9},{5... | collective-permute-start | bytes 1572872 | tf_op jit(solution)/shard_map/ppermute | solution.py:219
  43.1 0.7 sum_pieces.7
  43.7 0.6 collective-permute-start.4
  44.4 14.3 %collective-permute-done.5 = bf16[128,1024]{1,0:T(8,128)(2,1)S(1)} collective-permute-done((bf16[128,1024]{1,0:T(8,128)(2,1)S(1)}, bf16[128,1024]{1,0:T(8,128)(2,1)S(1)}, u32[]{:S(2)}, u32[]{:S(2)}) %collective-permute-start.5) | collective-permute-done | bytes 262176 | tf_op jit(solution)/shard_map/ppermute | solution.py:219
  58.7 0.7 collective-permute-done.2.refs_2_
  59.4 1.3 sum_pieces.8
  60.8 3.4 %collective-permute-start.6 = (bf16[128,1024]{1,0:T(8,128)(2,1)S(1)}, bf16[128,1024]{1,0:T(8,128)(2,1)S(1)}, u32[]{:S(2)}, u32[]{:S(2)}) collective-permute-start(bf16[128,1024]{1,0:T(8,128)(2,1)S(1)} %bitcast.118), channel_id=1, source_target_pairs={{0,16},{4,20},{8,24},{12,28},{16,0},{20,4},{24,8},{28,12},{1,17},{... | collective-permute-start | bytes 786440 | tf_op jit(solution)/shard_map/ppermute | solution.py:219
  64.2 0.5 collective-permute-start.9
  64.7 9.4 %collective-permute-done.6 = bf16[128,1024]{1,0:T(8,128)(2,1)S(1)} collective-permute-done((bf16[128,1024]{1,0:T(8,128)(2,1)S(1)}, bf16[128,1024]{1,0:T(8,128)(2,1)S(1)}, u32[]{:S(2)}, u32[]{:S(2)}) %collective-permute-start.6) | collective-permute-done | bytes 262176 | tf_op jit(solution)/shard_map/ppermute | solution.py:219
  74.0 1.4 sum_pieces.9
  75.4 1.3 sum_pieces.10
  77.0 0.6 collective-permute-start.11
  77.5 1.7 collective-permute-start.10
  79.2 1.5 collective-permute-start.16
  80.7 1.1 fusion.31
  81.8 6.1 %collective-permute-done.7 = bf16[128,1024]{1,0:T(8,128)(2,1)} collective-permute-done((bf16[128,1024]{1,0:T(8,128)(2,1)}, bf16[128,1024]{1,0:T(8,128)(2,1)}, u32[]{:S(2)}, u32[]{:S(2)}) %collective-permute-start.7) | collective-permute-done | bytes 262176 | tf_op jit(solution)/shard_map/ppermute | solution.py:219
  87.9 1.2 copy-done.4
  89.2 1.1 sum_pieces.11
  90.3 0.8 collective-permute-start.13
  91.0 2.8 %collective-permute-start.15 = (bf16[128,1024]{1,0:T(8,128)(2,1)S(1)}, bf16[128,1024]{1,0:T(8,128)(2,1)S(1)}, u32[]{:S(2)}, u32[]{:S(2)}) collective-permute-start(bf16[128,1024]{1,0:T(8,128)(2,1)S(1)} %bitcast.110), channel_id=1, source_target_pairs={{0,12},{4,8},{8,4},{12,0},{16,28},{20,24},{24,20},{28,16},{1,13},{... | collective-permute-start | bytes 786440 | tf_op jit(solution)/shard_map/ppermute | solution.py:235
  93.8 0.7 collective-permute-start.12
  94.9 1.1 unfold.1.refs_8_
  96.0 8.6 %collective-permute-done.12.refs_3_ = bf16[128,1024]{1,0:T(8,128)(2,1)S(1)} collective-permute-done((bf16[128,1024]{1,0:T(8,128)(2,1)S(1)}, bf16[128,1024]{1,0:T(8,128)(2,1)S(1)}, u32[]{:S(2)}, u32[]{:S(2)}) %collective-permute-start.12) | collective-permute-done | bytes 262176 | tf_op jit(solution)/shard_map/ppermute | solution.py:219
  104.6 1.3 collective-permute-done.14.refs_6_
  105.9 3.9 %collective-permute-done.15.refs_7_ = bf16[128,1024]{1,0:T(8,128)(2,1)S(1)} collective-permute-done((bf16[128,1024]{1,0:T(8,128)(2,1)S(1)}, bf16[128,1024]{1,0:T(8,128)(2,1)S(1)}, u32[]{:S(2)}, u32[]{:S(2)}) %collective-permute-start.15) | collective-permute-done | bytes 262176 | tf_op jit(solution)/shard_map/ppermute | solution.py:235
  109.8 2.3 %product.1 = (bf16[256,1024]{1,0:T(8,128)(2,1)S(1)}, bf16[1024,1024]{1,0:T(8,128)(2,1)S(1)}, f32[8,128]{1,0:T(8,128)S(1)}) custom-call(s32[3]{0:T(128)S(1)} %pad_add_fusion.place_ref, bf16[128,1024]{1,0:T(8,128)(2,1)S(1)} %bitcast.107, bf16[128,1024]{1,0:T(8,128)(2,1)S(1)} %collective-permute-done.11.refs_1_, ...), custom_call_target="tpu_custom_call" | custom-call | flops 1073741824 | bytes 4718592 | tf_op jit(solution)/shard_map/product/pallas_call | solution.py:31
  112.2 0.9 collective-permute-start.24
  113.2 2.1 %fusion.4 = (f32[]{:T(128)}, f32[2,128,1024]{2,1,0:T(8,128)}) fusion(bf16[1,128,1024]{2,1,0:T(8,128)(2,1)S(1)} %get-tuple-element.67, bf16[1,128,1024]{2,1,0:T(8,128)(2,1)S(1)} %get-tuple-element.66, f32[2,128,1024]{2,1,0:T(8,128)S(1)} %copy-done.16), kind=kLoop, calls=%fused_computation.21 | loop fusion | flops 2621439 | bytes 2621444 | tf_op jit(solution)/shard_map/reduce_sum | solution.py:331
  115.3 0.6 broadcast_select_fusion
  116.1 0.7 fusion
  116.8 0.5 convolution_bitcast_fusion.1
  117.3 0.7 fusion.42
  118.0 1.6 collective-permute-start.19
  119.5 0.5 convolution_bitcast_fusion
  120.0 1.6 collective-permute-done.19
  121.7 1.2 collective-permute-start.20
  122.8 0.4 fusion.26
  123.2 2.0 %collective-permute-done.20 = f32[8,128]{1,0:T(8,128)S(1)} collective-permute-done((f32[8,128]{1,0:T(8,128)S(1)}, f32[8,128]{1,0:T(8,128)S(1)}, u32[]{:S(2)}, u32[]{:S(2)}) %collective-permute-start.20) | collective-permute-done | bytes 4128 | tf_op jit(solution)/shard_map/ppermute | solution.py:219
  125.3 2.0 %collective-permute-start.21 = (f32[8,128]{1,0:T(8,128)S(1)}, f32[8,128]{1,0:T(8,128)S(1)}, u32[]{:S(2)}, u32[]{:S(2)}) collective-permute-start(f32[8,128]{1,0:T(8,128)S(1)} %add.109), channel_id=1, source_target_pairs={{0,8},{4,12},{8,0},{12,4},{16,24},{20,28},{24,16},{28,20},{1,9},{5... | collective-permute-start | bytes 12296 | tf_op jit(solution)/shard_map/ppermute | solution.py:219
  127.2 7.1 %collective-permute-done.22 = bf16[2,128,1024]{2,1,0:T(8,128)(2,1)S(1)} collective-permute-done((bf16[2,128,1024]{2,1,0:T(8,128)(2,1)S(1)}, bf16[2,128,1024]{2,1,0:T(8,128)(2,1)S(1)}, u32[]{:S(2)}, u32[]{:S(2)}) %collective-permute-start.22) | collective-permute-done | bytes 524320 | tf_op jit(solution)/shard_map/ppermute | solution.py:219
  134.3 1.2 collective-permute-done.23
  135.6 0.9 collective-permute-start.26
  136.8 1.0 collective-permute-start.27
  137.8 1.7 collective-permute-start.28
  139.5 2.9 %collective-permute-start.29 = (bf16[2,128,1024]{2,1,0:T(8,128)(2,1)S(1)}, bf16[2,128,1024]{2,1,0:T(8,128)(2,1)S(1)}, u32[]{:S(2)}, u32[]{:S(2)}) collective-permute-start(bf16[2,128,1024]{2,1,0:T(8,128)(2,1)S(1)} %pad_maximum_fusion.4), channel_id=1, source_target_pairs={{0,16},{4,20},{8,24},{12,28},{16,0},{20,4},{24,8},{28,12},{1,17},{... | collective-permute-start | bytes 1572872 | tf_op jit(solution)/shard_map/ppermute | solution.py:219
  142.4 0.6 fusion.38
  144.4 0.5 broadcast_in_dim.31
  145.3 25.5 %collective-permute-done.26 = bf16[2,2,128,1024]{3,2,1,0:T(8,128)(2,1)S(1)} collective-permute-done((bf16[2,2,128,1024]{3,2,1,0:T(8,128)(2,1)S(1)}, bf16[2,2,128,1024]{3,2,1,0:T(8,128)(2,1)S(1)}, u32[]{:S(2)}, u32[]{:S(2)}) %collective-permute-start.26) | collective-permute-done | bytes 1048608 | tf_op jit(solution)/shard_map/ppermute | solution.py:219
  171.2 1.2 collective-permute-done.28
  172.8 1.7 copy-done.7
  174.5 0.3 copy-done.9
  174.9 0.3 copy-done.14
  (79 shorter events, 2.4 us)
Async XLA Ops:
  0.6 7.6 %copy-start.1 = (bf16[2,128,1024]{2,1,0:T(8,128)(2,1)S(1)}, bf16[2,128,1024]{2,1,0:T(8,128)(2,1)}, u32[]{:S(2)}) copy-start(bf16[2,128,1024]{2,1,0:T(8,128)(2,1)} %own_ref.1) | copy-start | bytes 1572868
  3.6 33.2 %collective-permute-start = (bf16[4,128,1024]{2,1,0:T(8,128)(2,1)}, bf16[4,128,1024]{2,1,0:T(8,128)(2,1)}, u32[]{:S(2)}, u32[]{:S(2)}) collective-permute-start(bf16[4,128,1024]{2,1,0:T(8,128)(2,1)} %get-tuple-element.34), channel_id=1, source_target_pairs={{0,4},{4,0},{8,12},{12,8},{16,20},{20,16},{24,28},{28,24},{1,5},{5... | collective-permute-start | bytes 3145736 | tf_op jit(solution)/shard_map/ppermute | solution.py:219
  6.6 36.4 %collective-permute-start.3 = (bf16[4,128,1024]{2,1,0:T(8,128)(2,1)}, bf16[4,128,1024]{2,1,0:T(8,128)(2,1)S(1)}, u32[]{:S(2)}, u32[]{:S(2)}) collective-permute-start(bf16[4,128,1024]{2,1,0:T(8,128)(2,1)} %get-tuple-element.35), channel_id=1, source_target_pairs={{0,8},{4,12},{8,0},{12,4},{16,24},{20,28},{24,16},{28,20},{1,9},{5... | collective-permute-start | bytes 3145736 | tf_op jit(solution)/shard_map/ppermute | solution.py:219
  8.2 27.9 %collective-permute-start.1 = (bf16[128,1024]{1,0:T(8,128)(2,1)S(1)}, bf16[128,1024]{1,0:T(8,128)(2,1)S(1)}, u32[]{:S(2)}, u32[]{:S(2)}) collective-permute-start(bf16[128,1024]{1,0:T(8,128)(2,1)S(1)} %dynamic-slice_bitcast_fusion.1), channel_id=1, source_target_pairs={{0,16},{4,20},{8,24},{12,28},{16,0},{20,4},{24,8},{28,12},{1,17},{... | collective-permute-start | bytes 786440 | tf_op jit(solution)/shard_map/ppermute | solution.py:219
  10.9 2.2 %copy-start = (bf16[1,2,1024,1024]{3,2,1,0:T(8,128)(2,1)S(1)}, bf16[1,2,1024,1024]{3,2,1,0:T(8,128)(2,1)}, u32[]{:S(2)}) copy-start(bf16[1,2,1024,1024]{3,2,1,0:T(8,128)(2,1)} %param.6) | copy-start | bytes 12582916
  13.3 1.0 copy-start.2
  14.3 1.0 copy-start.5
  15.3 27.8 %copy-start.3 = (bf16[4,128,1024]{2,1,0:T(8,128)(2,1)S(1)}, bf16[4,128,1024]{2,1,0:T(8,128)(2,1)}, u32[]{:S(2)}) copy-start(bf16[4,128,1024]{2,1,0:T(8,128)(2,1)} %copy-done.2) | copy-start | bytes 3145732
  36.9 1.2 copy-start.6
  38.1 6.2 %copy-start.17 = (bf16[2,128,1024]{2,1,0:T(8,128)(2,1)S(1)}, bf16[2,128,1024]{2,1,0:T(8,128)(2,1)}, u32[]{:S(2)}) copy-start(bf16[2,128,1024]{2,1,0:T(8,128)(2,1)} %param.9) | copy-start | bytes 1572868
  39.5 19.9 %collective-permute-start.2 = (bf16[2,128,1024]{2,1,0:T(8,128)(2,1)S(1)}, bf16[2,128,1024]{2,1,0:T(8,128)(2,1)S(1)}, u32[]{:S(2)}, u32[]{:S(2)}) collective-permute-start(bf16[2,128,1024]{2,1,0:T(8,128)(2,1)S(1)} %sum_pieces.6), channel_id=1, source_target_pairs={{0,8},{4,12},{8,0},{12,4},{16,24},{20,28},{24,16},{28,20},{1,9},{5... | collective-permute-start | bytes 1572872 | tf_op jit(solution)/shard_map/ppermute | solution.py:219
  43.7 15.7 %collective-permute-start.4 = (bf16[2,128,1024]{2,1,0:T(8,128)(2,1)S(1)}, bf16[2,128,1024]{2,1,0:T(8,128)(2,1)S(1)}, u32[]{:S(2)}, u32[]{:S(2)}) collective-permute-start(bf16[2,128,1024]{2,1,0:T(8,128)(2,1)S(1)} %sum_pieces.7), channel_id=1, source_target_pairs={{0,4},{4,0},{8,12},{12,8},{16,20},{20,16},{24,28},{28,24},{1,5},{5... | collective-permute-start | bytes 1572872 | tf_op jit(solution)/shard_map/ppermute | solution.py:219
  44.3 14.3 %collective-permute-start.5 = (bf16[128,1024]{1,0:T(8,128)(2,1)S(1)}, bf16[128,1024]{1,0:T(8,128)(2,1)S(1)}, u32[]{:S(2)}, u32[]{:S(2)}) collective-permute-start(bf16[128,1024]{1,0:T(8,128)(2,1)S(1)} %dynamic-slice_bitcast_fusion), channel_id=1, source_target_pairs={{0,16},{4,20},{8,24},{12,28},{16,0},{20,4},{24,8},{28,12},{1,17},{... | collective-permute-start | bytes 786440 | tf_op jit(solution)/shard_map/ppermute | solution.py:219
  58.7 0.7 copy-start.18
  60.8 13.3 %collective-permute-start.6 = (bf16[128,1024]{1,0:T(8,128)(2,1)S(1)}, bf16[128,1024]{1,0:T(8,128)(2,1)S(1)}, u32[]{:S(2)}, u32[]{:S(2)}) collective-permute-start(bf16[128,1024]{1,0:T(8,128)(2,1)S(1)} %bitcast.118), channel_id=1, source_target_pairs={{0,16},{4,20},{8,24},{12,28},{16,0},{20,4},{24,8},{28,12},{1,17},{... | collective-permute-start | bytes 786440 | tf_op jit(solution)/shard_map/ppermute | solution.py:219
  64.2 12.8 %collective-permute-start.8 = (bf16[9,128,128]{2,1,0:T(8,128)(2,1)S(1)}, bf16[9,128,128]{2,1,0:T(8,128)(2,1)S(1)}, u32[]{:S(2)}, u32[]{:S(2)}) collective-permute-start(bf16[9,128,128]{2,1,0:T(8,128)(2,1)S(1)} %get-tuple-element.45), channel_id=1, source_target_pairs={{0,8},{4,12},{8,0},{12,4},{16,24},{20,28},{24,16},{28,20},{1,9},{5... | collective-permute-start | bytes 884744 | tf_op jit(solution)/shard_map/ppermute | solution.py:219
  64.2 12.8 %collective-permute-start.9 = (bf16[9,128,128]{2,1,0:T(8,128)(2,1)S(1)}, bf16[9,128,128]{2,1,0:T(8,128)(2,1)S(1)}, u32[]{:S(2)}, u32[]{:S(2)}) collective-permute-start(bf16[9,128,128]{2,1,0:T(8,128)(2,1)S(1)} %get-tuple-element.45), channel_id=1, source_target_pairs={{0,4},{4,0},{8,12},{12,8},{16,20},{20,16},{24,28},{28,24},{1,5},{5... | collective-permute-start | bytes 884744 | tf_op jit(solution)/shard_map/ppermute | solution.py:219
  76.8 11.2 %collective-permute-start.7 = (bf16[128,1024]{1,0:T(8,128)(2,1)}, bf16[128,1024]{1,0:T(8,128)(2,1)}, u32[]{:S(2)}, u32[]{:S(2)}) collective-permute-start(bf16[128,1024]{1,0:T(8,128)(2,1)} %bitcast.9), channel_id=1, source_target_pairs={{0,16},{4,20},{8,24},{12,28},{16,0},{20,4},{24,8},{28,12},{1,17},{... | collective-permute-start | bytes 786440 | tf_op jit(solution)/shard_map/ppermute | solution.py:219
  77.0 13.3 %collective-permute-start.11 = (bf16[128,1024]{1,0:T(8,128)(2,1)S(1)}, bf16[128,1024]{1,0:T(8,128)(2,1)S(1)}, u32[]{:S(2)}, u32[]{:S(2)}) collective-permute-start(bf16[128,1024]{1,0:T(8,128)(2,1)S(1)} %bitcast.105), channel_id=1, source_target_pairs={{0,4},{4,0},{8,12},{12,8},{16,20},{20,16},{24,28},{28,24},{1,5},{5... | collective-permute-start | bytes 786440 | tf_op jit(solution)/shard_map/ppermute | solution.py:219
  77.5 12.8 %collective-permute-start.10 = (bf16[128,1024]{1,0:T(8,128)(2,1)S(1)}, bf16[128,1024]{1,0:T(8,128)(2,1)S(1)}, u32[]{:S(2)}, u32[]{:S(2)}) collective-permute-start(bf16[128,1024]{1,0:T(8,128)(2,1)S(1)} %bitcast.106), channel_id=1, source_target_pairs={{0,8},{4,12},{8,0},{12,4},{16,24},{20,28},{24,16},{28,20},{1,9},{5... | collective-permute-start | bytes 786440 | tf_op jit(solution)/shard_map/ppermute | solution.py:219
  79.2 15.4 %collective-permute-start.16 = (bf16[9,128,128]{2,1,0:T(8,128)(2,1)S(1)}, bf16[9,128,128]{2,1,0:T(8,128)(2,1)S(1)}, u32[]{:S(2)}, u32[]{:S(2)}) collective-permute-start(bf16[9,128,128]{2,1,0:T(8,128)(2,1)S(1)} %collective-permute-done.8.refs_1_), channel_id=1, source_target_pairs={{0,4},{4,0},{8,12},{12,8},{16,20},{20,16},{24,28},{28,24},{1,5},{5... | collective-permute-start | bytes 884744 | tf_op jit(solution)/shard_map/ppermute | solution.py:219
  87.9 1.2 copy-start.4
  90.3 14.3 %collective-permute-start.13 = (bf16[128,1024]{1,0:T(8,128)(2,1)S(1)}, bf16[128,1024]{1,0:T(8,128)(2,1)S(1)}, u32[]{:S(2)}, u32[]{:S(2)}) collective-permute-start(bf16[128,1024]{1,0:T(8,128)(2,1)S(1)} %bitcast.108), channel_id=1, source_target_pairs={{0,4},{4,0},{8,12},{12,8},{16,20},{20,16},{24,28},{28,24},{1,5},{5... | collective-permute-start | bytes 786440 | tf_op jit(solution)/shard_map/ppermute | solution.py:235
  91.0 14.9 %collective-permute-start.14 = (bf16[128,1024]{1,0:T(8,128)(2,1)S(1)}, bf16[128,1024]{1,0:T(8,128)(2,1)S(1)}, u32[]{:S(2)}, u32[]{:S(2)}) collective-permute-start(bf16[128,1024]{1,0:T(8,128)(2,1)S(1)} %bitcast.109), channel_id=1, source_target_pairs={{0,8},{4,12},{8,0},{12,4},{16,24},{20,28},{24,16},{28,20},{1,9},{5... | collective-permute-start | bytes 786440 | tf_op jit(solution)/shard_map/ppermute | solution.py:235
  91.0 18.7 %collective-permute-start.15 = (bf16[128,1024]{1,0:T(8,128)(2,1)S(1)}, bf16[128,1024]{1,0:T(8,128)(2,1)S(1)}, u32[]{:S(2)}, u32[]{:S(2)}) collective-permute-start(bf16[128,1024]{1,0:T(8,128)(2,1)S(1)} %bitcast.110), channel_id=1, source_target_pairs={{0,12},{4,8},{8,4},{12,0},{16,28},{20,24},{24,20},{28,16},{1,13},{... | collective-permute-start | bytes 786440 | tf_op jit(solution)/shard_map/ppermute | solution.py:235
  93.8 10.7 %collective-permute-start.12 = (bf16[128,1024]{1,0:T(8,128)(2,1)S(1)}, bf16[128,1024]{1,0:T(8,128)(2,1)S(1)}, u32[]{:S(2)}, u32[]{:S(2)}) collective-permute-start(bf16[128,1024]{1,0:T(8,128)(2,1)S(1)} %collective-permute-done.10.refs_2_), channel_id=1, source_target_pairs={{0,4},{4,0},{8,12},{12,8},{16,20},{20,16},{24,28},{28,24},{1,5},{5... | collective-permute-start | bytes 786440 | tf_op jit(solution)/shard_map/ppermute | solution.py:219
  94.6 18.5 %collective-permute-start.17 = (bf16[128,1024]{1,0:T(8,128)(2,1)S(1)}, bf16[128,1024]{1,0:T(8,128)(2,1)S(1)}, u32[]{:S(2)}, u32[]{:S(2)}) collective-permute-start(bf16[128,1024]{1,0:T(8,128)(2,1)S(1)} %fusion.28), channel_id=1, source_target_pairs={{0,16},{4,20},{8,24},{12,28},{16,0},{20,4},{24,8},{28,12},{1,17},{... | collective-permute-start | bytes 786440 | tf_op jit(solution)/shard_map/ppermute | solution.py:219
  94.8 18.3 %copy-start.16 = (f32[2,128,1024]{2,1,0:T(8,128)S(1)}, f32[2,128,1024]{2,1,0:T(8,128)}, u32[]{:S(2)}) copy-start(f32[2,128,1024]{2,1,0:T(8,128)} %param.11) | copy-start | bytes 3145732
  112.0 22.3 %collective-permute-start.22 = (bf16[2,128,1024]{2,1,0:T(8,128)(2,1)S(1)}, bf16[2,128,1024]{2,1,0:T(8,128)(2,1)S(1)}, u32[]{:S(2)}, u32[]{:S(2)}) collective-permute-start(bf16[2,128,1024]{2,1,0:T(8,128)(2,1)S(1)} %bitcast.113), channel_id=1, source_target_pairs={{0,16},{4,20},{8,24},{12,28},{16,0},{20,4},{24,8},{28,12},{1,17},{... | collective-permute-start | bytes 1572872 | tf_op jit(solution)/shard_map/ppermute | solution.py:219
  112.1 23.4 %collective-permute-start.23 = (bf16[2,128,1024]{2,1,0:T(8,128)(2,1)S(1)}, bf16[2,128,1024]{2,1,0:T(8,128)(2,1)S(1)}, u32[]{:S(2)}, u32[]{:S(2)}) collective-permute-start(bf16[2,128,1024]{2,1,0:T(8,128)(2,1)S(1)} %bitcast.114), channel_id=1, source_target_pairs={{0,8},{4,12},{8,0},{12,4},{16,24},{20,28},{24,16},{28,20},{1,9},{5... | collective-permute-start | bytes 1572872 | tf_op jit(solution)/shard_map/ppermute | solution.py:219
  112.2 23.3 %collective-permute-start.24 = (bf16[2,128,1024]{2,1,0:T(8,128)(2,1)S(1)}, bf16[2,128,1024]{2,1,0:T(8,128)(2,1)S(1)}, u32[]{:S(2)}, u32[]{:S(2)}) collective-permute-start(bf16[2,128,1024]{2,1,0:T(8,128)(2,1)S(1)} %bitcast.115), channel_id=1, source_target_pairs={{0,4},{4,0},{8,12},{12,8},{16,20},{20,16},{24,28},{28,24},{1,5},{5... | collective-permute-start | bytes 1572872 | tf_op jit(solution)/shard_map/ppermute | solution.py:219
  116.0 1.3 collective-permute-start.18
  116.1 6.8 %copy-start.10 = (f32[2,128,1024]{2,1,0:T(8,128)S(1)}, f32[2,128,1024]{2,1,0:T(8,128)}, u32[]{:S(2)}) copy-start(f32[2,128,1024]{2,1,0:T(8,128)} %param.8) | copy-start | bytes 3145732
  116.1 6.8 %copy-start.15 = (f32[2,128,1024]{2,1,0:T(8,128)S(1)}, f32[2,128,1024]{2,1,0:T(8,128)}, u32[]{:S(2)}) copy-start(f32[2,128,1024]{2,1,0:T(8,128)} %param.7) | copy-start | bytes 3145732
  118.0 3.7 %collective-permute-start.19 = (f32[8,128]{1,0:T(8,128)S(1)}, f32[8,128]{1,0:T(8,128)S(1)}, u32[]{:S(2)}, u32[]{:S(2)}) collective-permute-start(f32[8,128]{1,0:T(8,128)S(1)} %fusion.42), channel_id=1, source_target_pairs={{0,2},{1,3},{2,0},{3,1},{4,6},{5,7},{6,4},{7,5},{8,10},{9,11},{10,... | collective-permute-start | bytes 12296 | tf_op jit(solution)/shard_map/ppermute | solution.py:336
  121.7 3.6 %collective-permute-start.20 = (f32[8,128]{1,0:T(8,128)S(1)}, f32[8,128]{1,0:T(8,128)S(1)}, u32[]{:S(2)}, u32[]{:S(2)}) collective-permute-start(f32[8,128]{1,0:T(8,128)S(1)} %add.108), channel_id=1, source_target_pairs={{0,4},{4,0},{8,12},{12,8},{16,20},{20,16},{24,28},{28,24},{1,5},{5... | collective-permute-start | bytes 12296 | tf_op jit(solution)/shard_map/ppermute | solution.py:219
  123.2 21.2 %copy-start.12 = (f32[2,128,1024]{2,1,0:T(8,128)}, f32[2,128,1024]{2,1,0:T(8,128)S(1)}, u32[]{:S(2)}) copy-start(f32[2,128,1024]{2,1,0:T(8,128)S(1)} %get-tuple-element.60) | copy-start | bytes 3145732
  125.3 11.4 %collective-permute-start.21 = (f32[8,128]{1,0:T(8,128)S(1)}, f32[8,128]{1,0:T(8,128)S(1)}, u32[]{:S(2)}, u32[]{:S(2)}) collective-permute-start(f32[8,128]{1,0:T(8,128)S(1)} %add.109), channel_id=1, source_target_pairs={{0,8},{4,12},{8,0},{12,4},{16,24},{20,28},{24,16},{28,20},{1,9},{5... | collective-permute-start | bytes 12296 | tf_op jit(solution)/shard_map/ppermute | solution.py:219
  135.6 35.2 %collective-permute-start.26 = (bf16[2,2,128,1024]{3,2,1,0:T(8,128)(2,1)S(1)}, bf16[2,2,128,1024]{3,2,1,0:T(8,128)(2,1)S(1)}, u32[]{:S(2)}, u32[]{:S(2)}) collective-permute-start(bf16[2,2,128,1024]{3,2,1,0:T(8,128)(2,1)S(1)} %pad_maximum_fusion), channel_id=1, source_target_pairs={{0,4},{4,0},{8,12},{12,8},{16,20},{20,16},{24,28},{28,24},{1,5},{5... | collective-permute-start | bytes 3145736 | tf_op jit(solution)/shard_map/ppermute | solution.py:219
  136.7 5.7 %collective-permute-start.25 = (f32[8,128]{1,0:T(8,128)S(1)}, f32[8,128]{1,0:T(8,128)S(1)}, u32[]{:S(2)}, u32[]{:S(2)}) collective-permute-start(f32[8,128]{1,0:T(8,128)S(1)} %add.110), channel_id=1, source_target_pairs={{0,16},{4,20},{8,24},{12,28},{16,0},{20,4},{24,8},{28,12},{1,17},{... | collective-permute-start | bytes 12296 | tf_op jit(solution)/shard_map/ppermute | solution.py:219
  136.8 34.3 %collective-permute-start.27 = (bf16[2,128,1024]{2,1,0:T(8,128)(2,1)S(1)}, bf16[2,128,1024]{2,1,0:T(8,128)(2,1)S(1)}, u32[]{:S(2)}, u32[]{:S(2)}) collective-permute-start(bf16[2,128,1024]{2,1,0:T(8,128)(2,1)S(1)} %collective-permute-done.22), channel_id=1, source_target_pairs={{0,12},{4,8},{8,4},{12,0},{16,28},{20,24},{24,20},{28,16},{1,13},{... | collective-permute-start | bytes 1572872 | tf_op jit(solution)/shard_map/ppermute | solution.py:362
  137.8 34.6 %collective-permute-start.28 = (bf16[2,128,1024]{2,1,0:T(8,128)(2,1)S(1)}, bf16[2,128,1024]{2,1,0:T(8,128)(2,1)S(1)}, u32[]{:S(2)}, u32[]{:S(2)}) collective-permute-start(bf16[2,128,1024]{2,1,0:T(8,128)(2,1)S(1)} %collective-permute-done.22), channel_id=1, source_target_pairs={{0,8},{4,12},{8,0},{12,4},{16,24},{20,28},{24,16},{28,20},{1,9},{5... | collective-permute-start | bytes 1572872 | tf_op jit(solution)/shard_map/ppermute | solution.py:362
  139.5 33.0 %collective-permute-start.29 = (bf16[2,128,1024]{2,1,0:T(8,128)(2,1)S(1)}, bf16[2,128,1024]{2,1,0:T(8,128)(2,1)S(1)}, u32[]{:S(2)}, u32[]{:S(2)}) collective-permute-start(bf16[2,128,1024]{2,1,0:T(8,128)(2,1)S(1)} %pad_maximum_fusion.4), channel_id=1, source_target_pairs={{0,16},{4,20},{8,24},{12,28},{16,0},{20,4},{24,8},{28,12},{1,17},{... | collective-permute-start | bytes 1572872 | tf_op jit(solution)/shard_map/ppermute | solution.py:219
  144.9 27.6 %copy-start.8 = (f32[2,128,1024]{2,1,0:T(8,128)S(1)}, f32[2,128,1024]{2,1,0:T(8,128)}, u32[]{:S(2)}) copy-start(f32[2,128,1024]{2,1,0:T(8,128)} %param.8) | copy-start | bytes 3145732
  144.9 27.6 %copy-start.11 = (f32[2,128,1024]{2,1,0:T(8,128)S(1)}, f32[2,128,1024]{2,1,0:T(8,128)}, u32[]{:S(2)}) copy-start(f32[2,128,1024]{2,1,0:T(8,128)} %param.7) | copy-start | bytes 3145732
  144.9 27.6 %copy-start.13 = (f32[2,128,1024]{2,1,0:T(8,128)S(1)}, f32[2,128,1024]{2,1,0:T(8,128)}, u32[]{:S(2)}) copy-start(f32[2,128,1024]{2,1,0:T(8,128)} %copy-done.12) | copy-start | bytes 3145732
  172.5 2.0 %copy-start.7 = (bf16[2,2,4,128,1024]{4,3,2,1,0:T(8,128)(2,1)}, bf16[2,2,4,128,1024]{4,3,2,1,0:T(8,128)(2,1)S(1)}, u32[]{:S(2)}) copy-start(bf16[2,2,4,128,1024]{4,3,2,1,0:T(8,128)(2,1)S(1)} %fusion.20) | copy-start | bytes 12582916
  172.8 2.1 %copy-start.9 = (f32[2,128,1024]{2,1,0:T(8,128)}, f32[2,128,1024]{2,1,0:T(8,128)S(1)}, u32[]{:S(2)}) copy-start(f32[2,128,1024]{2,1,0:T(8,128)S(1)} %get-tuple-element.70) | copy-start | bytes 3145732
  172.8 2.4 %copy-start.14 = (f32[2,128,1024]{2,1,0:T(8,128)}, f32[2,128,1024]{2,1,0:T(8,128)S(1)}, u32[]{:S(2)}) copy-start(f32[2,128,1024]{2,1,0:T(8,128)S(1)} %get-tuple-element.71) | copy-start | bytes 3145732

commit v6 on v3

--- a/solution.py
+++ b/solution.py
@@ -333,10 +333,10 @@
     sums = jnp.where(lane == 0, adam_part, precond_part)
     for bit in range(bits_of(groups)):
         sums = sums + lax.ppermute(sums, "blk", [(i, i ^ (1 << bit)) for i in range(groups)])
-    for bit in range(bits):
-        if bit == top:
-            sums = after(sums, partner, *first_pieces.values())
+    for bit in (*range(top - 1), top):
         sums = sums + swap(sums, bit)
+    sums = after(sums, partner, *first_pieces.values())
+    sums = sums + swap(sums, top - 1)
 
     def columns(part):
         return lax.dynamic_slice_in_dim(grad_low, part * members * rows + member * rows, rows, 1)

time: 172 us -> 170 us (0.988)
  waiting for transfers between devices: 94.2 us -> 91.8 us
    ppermute x2, waiting for transfers between devices: 2.94 us -> 1.2 us  [per_device(): lax.ppermute(partner, 'dp', [(i, i ^ k) for i in range(devices)])]
where the time goes in v6:
time: 170 us
  waiting for transfers between devices  91.8 us (54%)
  starting transfers between devices  43.4 us (26%)
  Pallas kernels  12.8 us (8%)
  local copies, waits for them, and re-layouts  10.8 us (6%)
  other arithmetic  6.5 us (4%)
  between operations  2.52 us (1%)
    ppermute x23, waiting for transfers between devices, swap(): lax.ppermute(array, 'dp', [(i, i ^ 1 << bit) for i in range(devices)])  88.9 us
    ppermute x23, starting transfers between devices, swap(): lax.ppermute(array, 'dp', [(i, i ^ 1 << bit) for i in range(devices)])  34.5 us
    pallas_call x9, Pallas kernels, run(): pl.pallas_call(kernel, out_shape=out_shape, in_specs=[SMEM] + [VMEM] * le...  9.64 us
    unnamed x52, local copies, waits for them, and re-layouts  8.98 us
    ppermute x3, starting transfers between devices, gather_direct(): pieces[k] = lax.ppermute(own, 'dp', [(i, i ^ k) for i in range(devices)])  4.05 us
  transfers between devices with their start and end apart: 30, of which 13 were waited for; matrix products, arithmetic and copies ran while one was open for 6% of the time, Pallas kernels for 5%

profile of v6, /device:TPU:0, one launch (start us, length us, event | category | flops | bytes accessed | tf_op | source)
XLA Modules:
  0.0 169.5 jit_solution(6845310828608915459)
XLA Ops:
  0.6 3.0 %cut.2 = (bf16[4,128,1024]{2,1,0:T(8,128)(2,1)}, bf16[4,128,1024]{2,1,0:T(8,128)(2,1)}) custom-call(bf16[2,2,4,128,1024]{4,3,2,1,0:T(8,128)(2,1)} %bitcast.103), custom_call_target="tpu_custom_call" | custom-call | bytes 4194304 | tf_op jit(solution)/shard_map/cut/pallas_call | solution.py:69
  3.6 3.0 %collective-permute-start = (bf16[4,128,1024]{2,1,0:T(8,128)(2,1)}, bf16[4,128,1024]{2,1,0:T(8,128)(2,1)S(1)}, u32[]{:S(2)}, u32[]{:S(2)}) collective-permute-start(bf16[4,128,1024]{2,1,0:T(8,128)(2,1)} %get-tuple-element.34), channel_id=1, source_target_pairs={{0,4},{4,0},{8,12},{12,8},{16,20},{20,16},{24,28},{28,24},{1,5},{5... | collective-permute-start | bytes 3145736 | tf_op jit(solution)/shard_map/ppermute | solution.py:218
  6.6 1.6 collective-permute-start.3
  8.2 0.7 dynamic-slice_bitcast_fusion.1
  8.9 2.6 %collective-permute-start.1 = (bf16[128,1024]{1,0:T(8,128)(2,1)}, bf16[128,1024]{1,0:T(8,128)(2,1)S(1)}, u32[]{:S(2)}, u32[]{:S(2)}) collective-permute-start(bf16[128,1024]{1,0:T(8,128)(2,1)} %dynamic-slice_bitcast_fusion.1), channel_id=1, source_target_pairs={{0,16},{4,20},{8,24},{12,28},{16,0},{20,4},{24,8},{28,12},{1,17},{... | collective-permute-start | bytes 786440 | tf_op jit(solution)/shard_map/ppermute | solution.py:218
  11.5 2.2 %copy-done = bf16[1,2,1024,1024]{3,2,1,0:T(8,128)(2,1)S(1)} copy-done((bf16[1,2,1024,1024]{3,2,1,0:T(8,128)(2,1)S(1)}, bf16[1,2,1024,1024]{3,2,1,0:T(8,128)(2,1)}, u32[]{:S(2)}) %copy-start) | copy-done | bytes 4194328
  14.0 1.0 copy-done.1
  15.0 21.3 %collective-permute-done.1.partner_ref = bf16[128,1024]{1,0:T(8,128)(2,1)S(1)} collective-permute-done((bf16[128,1024]{1,0:T(8,128)(2,1)}, bf16[128,1024]{1,0:T(8,128)(2,1)S(1)}, u32[]{:S(2)}, u32[]{:S(2)}) %collective-permute-start.1) | collective-permute-done | bytes 262176 | tf_op jit(solution)/shard_map/ppermute | solution.py:218
  36.3 0.7 copy-done.14
  37.0 1.2 copy-done.2
  38.2 0.7 sum_pieces.6
  38.9 3.5 %collective-permute-start.2 = (bf16[2,128,1024]{2,1,0:T(8,128)(2,1)S(1)}, bf16[2,128,1024]{2,1,0:T(8,128)(2,1)S(1)}, u32[]{:S(2)}, u32[]{:S(2)}) collective-permute-start(bf16[2,128,1024]{2,1,0:T(8,128)(2,1)S(1)} %sum_pieces.6), channel_id=1, source_target_pairs={{0,8},{4,12},{8,0},{12,4},{16,24},{20,28},{24,16},{28,20},{1,9},{5... | collective-permute-start | bytes 1572872 | tf_op jit(solution)/shard_map/ppermute | solution.py:218
  42.4 0.7 sum_pieces.7
  43.0 0.6 collective-permute-start.4
  43.7 0.7 pack.1
  44.4 13.6 %collective-permute-done.5 = bf16[128,1024]{1,0:T(8,128)(2,1)S(1)} collective-permute-done((bf16[128,1024]{1,0:T(8,128)(2,1)S(1)}, bf16[128,1024]{1,0:T(8,128)(2,1)S(1)}, u32[]{:S(2)}, u32[]{:S(2)}) %collective-permute-start.5) | collective-permute-done | bytes 262176 | tf_op jit(solution)/shard_map/ppermute | solution.py:218
  58.0 0.7 collective-permute-done.2.refs_2_
  58.7 0.6 sum_pieces.8
  59.4 1.7 %collective-permute-start.8 = (bf16[9,128,128]{2,1,0:T(8,128)(2,1)S(1)}, bf16[9,128,128]{2,1,0:T(8,128)(2,1)S(1)}, u32[]{:S(2)}, u32[]{:S(2)}) collective-permute-start(bf16[9,128,128]{2,1,0:T(8,128)(2,1)S(1)} %get-tuple-element.45), channel_id=1, source_target_pairs={{0,8},{4,12},{8,0},{12,4},{16,24},{20,28},{24,16},{28,20},{1,9},{5... | collective-permute-start | bytes 884744 | tf_op jit(solution)/shard_map/ppermute | solution.py:218
  61.1 0.5 collective-permute-start.9
  61.6 1.1 collective-permute-start.6
  62.7 8.5 %collective-permute-done.6 = bf16[128,1024]{1,0:T(8,128)(2,1)S(1)} collective-permute-done((bf16[128,1024]{1,0:T(8,128)(2,1)S(1)}, bf16[128,1024]{1,0:T(8,128)(2,1)S(1)}, u32[]{:S(2)}, u32[]{:S(2)}) %collective-permute-start.6) | collective-permute-done | bytes 262176 | tf_op jit(solution)/shard_map/ppermute | solution.py:218
  71.2 0.7 sum_pieces.9
  71.9 1.3 sum_pieces.10
  73.2 3.2 %collective-permute-start.7 = (bf16[128,1024]{1,0:T(8,128)(2,1)}, bf16[128,1024]{1,0:T(8,128)(2,1)}, u32[]{:S(2)}, u32[]{:S(2)}) collective-permute-start(bf16[128,1024]{1,0:T(8,128)(2,1)} %bitcast.9), channel_id=1, source_target_pairs={{0,16},{4,20},{8,24},{12,28},{16,0},{20,4},{24,8},{28,12},{1,17},{... | collective-permute-start | bytes 786440 | tf_op jit(solution)/shard_map/ppermute | solution.py:218
  76.4 0.7 copy-done.10
  77.2 0.7 copy-done.12
  77.9 1.3 collective-permute-start.11
  79.2 2.4 %collective-permute-start.10 = (bf16[128,1024]{1,0:T(8,128)(2,1)S(1)}, bf16[128,1024]{1,0:T(8,128)(2,1)}, u32[]{:S(2)}, u32[]{:S(2)}) collective-permute-start(bf16[128,1024]{1,0:T(8,128)(2,1)S(1)} %bitcast.106), channel_id=1, source_target_pairs={{0,8},{4,12},{8,0},{12,4},{16,24},{20,28},{24,16},{28,20},{1,9},{5... | collective-permute-start | bytes 786440 | tf_op jit(solution)/shard_map/ppermute | solution.py:218
  81.6 0.6 collective-permute-start.16
  82.2 1.1 fusion.31
  83.3 2.1 %collective-permute-done.7 = bf16[128,1024]{1,0:T(8,128)(2,1)} collective-permute-done((bf16[128,1024]{1,0:T(8,128)(2,1)}, bf16[128,1024]{1,0:T(8,128)(2,1)}, u32[]{:S(2)}, u32[]{:S(2)}) %collective-permute-start.7) | collective-permute-done | bytes 262176 | tf_op jit(solution)/shard_map/ppermute | solution.py:218
  85.4 1.1 sum_pieces.11
  86.5 1.4 collective-permute-done.10.refs_2_
  87.9 2.1 %collective-permute-start.13 = (bf16[128,1024]{1,0:T(8,128)(2,1)S(1)}, bf16[128,1024]{1,0:T(8,128)(2,1)S(1)}, u32[]{:S(2)}, u32[]{:S(2)}) collective-permute-start(bf16[128,1024]{1,0:T(8,128)(2,1)S(1)} %bitcast.108), channel_id=1, source_target_pairs={{0,4},{4,0},{8,12},{12,8},{16,20},{20,16},{24,28},{28,24},{1,5},{5... | collective-permute-start | bytes 786440 | tf_op jit(solution)/shard_map/ppermute | solution.py:234
  90.5 1.5 collective-permute-start.15
  92.0 1.6 collective-permute-start.12
  93.6 0.6 collective-permute-start.17
  94.4 1.1 unfold.1.refs_8_
  95.6 9.8 %collective-permute-done.12.refs_3_ = bf16[128,1024]{1,0:T(8,128)(2,1)S(1)} collective-permute-done((bf16[128,1024]{1,0:T(8,128)(2,1)}, bf16[128,1024]{1,0:T(8,128)(2,1)S(1)}, u32[]{:S(2)}, u32[]{:S(2)}) %collective-permute-start.12) | collective-permute-done | bytes 262176 | tf_op jit(solution)/shard_map/ppermute | solution.py:218
  105.4 2.8 %product.1 = (bf16[256,1024]{1,0:T(8,128)(2,1)S(1)}, bf16[1024,1024]{1,0:T(8,128)(2,1)S(1)}, f32[8,128]{1,0:T(8,128)S(1)}) custom-call(s32[3]{0:T(128)S(1)} %pad_add_fusion.place_ref, bf16[128,1024]{1,0:T(8,128)(2,1)S(1)} %bitcast.107, bf16[128,1024]{1,0:T(8,128)(2,1)} %collective-permute-done.11.refs_1_, bf16[128,1024]{1,0:T(8,128)(2,1)} %collective-permute-done.10.refs_2_, ...), custom_call_target="tpu_custom_call" | custom-call | flops 1073741824 | bytes 4718592 | tf_op jit(solution)/shard_map/product/pallas_call | solution.py:31
  108.2 1.7 %collective-permute-start.22 = (bf16[2,128,1024]{2,1,0:T(8,128)(2,1)S(1)}, bf16[2,128,1024]{2,1,0:T(8,128)(2,1)S(1)}, u32[]{:S(2)}, u32[]{:S(2)}) collective-permute-start(bf16[2,128,1024]{2,1,0:T(8,128)(2,1)S(1)} %bitcast.113), channel_id=1, source_target_pairs={{0,16},{4,20},{8,24},{12,28},{16,0},{20,4},{24,8},{28,12},{1,17},{... | collective-permute-start | bytes 1572872 | tf_op jit(solution)/shard_map/ppermute | solution.py:218
  109.9 2.2 %collective-permute-start.23 = (bf16[2,128,1024]{2,1,0:T(8,128)(2,1)S(1)}, bf16[2,128,1024]{2,1,0:T(8,128)(2,1)S(1)}, u32[]{:S(2)}, u32[]{:S(2)}) collective-permute-start(bf16[2,128,1024]{2,1,0:T(8,128)(2,1)S(1)} %bitcast.114), channel_id=1, source_target_pairs={{0,8},{4,12},{8,0},{12,4},{16,24},{20,28},{24,16},{28,20},{1,9},{5... | collective-permute-start | bytes 1572872 | tf_op jit(solution)/shard_map/ppermute | solution.py:218
  112.1 1.7 %collective-permute-start.24 = (bf16[2,128,1024]{2,1,0:T(8,128)(2,1)S(1)}, bf16[2,128,1024]{2,1,0:T(8,128)(2,1)S(1)}, u32[]{:S(2)}, u32[]{:S(2)}) collective-permute-start(bf16[2,128,1024]{2,1,0:T(8,128)(2,1)S(1)} %bitcast.115), channel_id=1, source_target_pairs={{0,4},{4,0},{8,12},{12,8},{16,20},{20,16},{24,28},{28,24},{1,5},{5... | collective-permute-start | bytes 1572872 | tf_op jit(solution)/shard_map/ppermute | solution.py:218
  113.9 2.1 %fusion.4 = (f32[]{:T(128)}, f32[2,128,1024]{2,1,0:T(8,128)}) fusion(bf16[1,128,1024]{2,1,0:T(8,128)(2,1)S(1)} %get-tuple-element.67, bf16[1,128,1024]{2,1,0:T(8,128)(2,1)S(1)} %get-tuple-element.66, f32[2,128,1024]{2,1,0:T(8,128)S(1)} %copy-done.23), kind=kLoop, calls=%fused_computation.21 | loop fusion | flops 2621439 | bytes 2621444 | tf_op jit(solution)/shard_map/reduce_sum | solution.py:330
  116.0 0.6 broadcast_select_fusion
  116.8 0.7 fusion
  117.5 0.5 convolution_bitcast_fusion.1
  118.0 0.7 fusion.42
  118.7 1.6 collective-permute-start.19
  120.2 0.5 convolution_bitcast_fusion
  120.7 1.6 collective-permute-done.19
  123.1 2.9 %collective-permute-done.20 = f32[8,128]{1,0:T(8,128)S(1)} collective-permute-done((f32[8,128]{1,0:T(8,128)S(1)}, f32[8,128]{1,0:T(8,128)S(1)}, u32[]{:S(2)}, u32[]{:S(2)}) %collective-permute-start.20) | collective-permute-done | bytes 4128 | tf_op jit(solution)/shard_map/ppermute | solution.py:218
  126.0 3.9 %collective-permute-done.22 = bf16[2,128,1024]{2,1,0:T(8,128)(2,1)S(1)} collective-permute-done((bf16[2,128,1024]{2,1,0:T(8,128)(2,1)S(1)}, bf16[2,128,1024]{2,1,0:T(8,128)(2,1)S(1)}, u32[]{:S(2)}, u32[]{:S(2)}) %collective-permute-start.22) | collective-permute-done | bytes 524320 | tf_op jit(solution)/shard_map/ppermute | solution.py:218
  130.1 0.7 collective-permute-start.26
  130.9 1.4 collective-permute-start.25
  132.3 1.6 collective-permute-start.27
  133.9 1.6 collective-permute-start.28
  135.5 2.0 %collective-permute-start.29 = (bf16[2,128,1024]{2,1,0:T(8,128)(2,1)S(1)}, bf16[2,128,1024]{2,1,0:T(8,128)(2,1)S(1)}, u32[]{:S(2)}, u32[]{:S(2)}) collective-permute-start(bf16[2,128,1024]{2,1,0:T(8,128)(2,1)S(1)} %pad_maximum_fusion.4), channel_id=1, source_target_pairs={{0,16},{4,20},{8,24},{12,28},{16,0},{20,4},{24,8},{28,12},{1,17},{... | collective-permute-start | bytes 1572872 | tf_op jit(solution)/shard_map/ppermute | solution.py:218
  137.6 0.6 fusion.38
  139.5 0.5 broadcast_in_dim.31
  140.4 24.7 %collective-permute-done.26 = bf16[2,2,128,1024]{3,2,1,0:T(8,128)(2,1)S(1)} collective-permute-done((bf16[2,2,128,1024]{3,2,1,0:T(8,128)(2,1)S(1)}, bf16[2,2,128,1024]{3,2,1,0:T(8,128)(2,1)S(1)}, u32[]{:S(2)}, u32[]{:S(2)}) %collective-permute-start.26) | collective-permute-done | bytes 1048608 | tf_op jit(solution)/shard_map/ppermute | solution.py:218
  165.5 1.2 collective-permute-done.28
  167.1 1.7 %copy-done.16 = bf16[2,2,4,128,1024]{4,3,2,1,0:T(8,128)(2,1)} copy-done((bf16[2,2,4,128,1024]{4,3,2,1,0:T(8,128)(2,1)}, bf16[2,2,4,128,1024]{4,3,2,1,0:T(8,128)(2,1)S(1)}, u32[]{:S(2)}) %copy-start.16) | copy-done | bytes 4194328
  (93 shorter events, 4.2 us)
Async XLA Ops:
  0.6 7.6 %copy-start.6 = (bf16[2,128,1024]{2,1,0:T(8,128)(2,1)S(1)}, bf16[2,128,1024]{2,1,0:T(8,128)(2,1)}, u32[]{:S(2)}) copy-start(bf16[2,128,1024]{2,1,0:T(8,128)(2,1)} %own_ref.1) | copy-start | bytes 1572868
  3.6 33.4 %collective-permute-start = (bf16[4,128,1024]{2,1,0:T(8,128)(2,1)}, bf16[4,128,1024]{2,1,0:T(8,128)(2,1)S(1)}, u32[]{:S(2)}, u32[]{:S(2)}) collective-permute-start(bf16[4,128,1024]{2,1,0:T(8,128)(2,1)} %get-tuple-element.34), channel_id=1, source_target_pairs={{0,4},{4,0},{8,12},{12,8},{16,20},{20,16},{24,28},{28,24},{1,5},{5... | collective-permute-start | bytes 3145736 | tf_op jit(solution)/shard_map/ppermute | solution.py:218
  6.6 35.7 %collective-permute-start.3 = (bf16[4,128,1024]{2,1,0:T(8,128)(2,1)}, bf16[4,128,1024]{2,1,0:T(8,128)(2,1)S(1)}, u32[]{:S(2)}, u32[]{:S(2)}) collective-permute-start(bf16[4,128,1024]{2,1,0:T(8,128)(2,1)} %get-tuple-element.35), channel_id=1, source_target_pairs={{0,8},{4,12},{8,0},{12,4},{16,24},{20,28},{24,16},{28,20},{1,9},{5... | collective-permute-start | bytes 3145736 | tf_op jit(solution)/shard_map/ppermute | solution.py:218
  8.9 27.3 %collective-permute-start.1 = (bf16[128,1024]{1,0:T(8,128)(2,1)}, bf16[128,1024]{1,0:T(8,128)(2,1)S(1)}, u32[]{:S(2)}, u32[]{:S(2)}) collective-permute-start(bf16[128,1024]{1,0:T(8,128)(2,1)} %dynamic-slice_bitcast_fusion.1), channel_id=1, source_target_pairs={{0,16},{4,20},{8,24},{12,28},{16,0},{20,4},{24,8},{28,12},{1,17},{... | collective-permute-start | bytes 786440 | tf_op jit(solution)/shard_map/ppermute | solution.py:218
  11.5 2.2 %copy-start = (bf16[1,2,1024,1024]{3,2,1,0:T(8,128)(2,1)S(1)}, bf16[1,2,1024,1024]{3,2,1,0:T(8,128)(2,1)}, u32[]{:S(2)}) copy-start(bf16[1,2,1024,1024]{3,2,1,0:T(8,128)(2,1)} %param.6) | copy-start | bytes 12582916
  13.9 1.0 copy-start.1
  36.3 0.7 copy-start.14
  37.0 1.2 copy-start.2
  38.2 5.4 %copy-start.24 = (bf16[2,128,1024]{2,1,0:T(8,128)(2,1)S(1)}, bf16[2,128,1024]{2,1,0:T(8,128)(2,1)}, u32[]{:S(2)}) copy-start(bf16[2,128,1024]{2,1,0:T(8,128)(2,1)} %param.9) | copy-start | bytes 1572868
  38.2 5.5 %copy-start.7 = (bf16[2,128,1024]{2,1,0:T(8,128)(2,1)S(1)}, bf16[2,128,1024]{2,1,0:T(8,128)(2,1)}, u32[]{:S(2)}) copy-start(bf16[2,128,1024]{2,1,0:T(8,128)(2,1)} %own_ref.1) | copy-start | bytes 1572868
  38.2 5.5 %copy-start.15 = (bf16[128,1024]{1,0:T(8,128)(2,1)S(1)}, bf16[128,1024]{1,0:T(8,128)(2,1)}, u32[]{:S(2)}) copy-start(bf16[128,1024]{1,0:T(8,128)(2,1)} %copy-done.14) | copy-start | bytes 786436
  38.2 20.5 %copy-start.3 = (bf16[4,128,1024]{2,1,0:T(8,128)(2,1)S(1)}, bf16[4,128,1024]{2,1,0:T(8,128)(2,1)}, u32[]{:S(2)}) copy-start(bf16[4,128,1024]{2,1,0:T(8,128)(2,1)} %copy-done.1) | copy-start | bytes 3145732
  38.9 19.8 %collective-permute-start.2 = (bf16[2,128,1024]{2,1,0:T(8,128)(2,1)S(1)}, bf16[2,128,1024]{2,1,0:T(8,128)(2,1)S(1)}, u32[]{:S(2)}, u32[]{:S(2)}) collective-permute-start(bf16[2,128,1024]{2,1,0:T(8,128)(2,1)S(1)} %sum_pieces.6), channel_id=1, source_target_pairs={{0,8},{4,12},{8,0},{12,4},{16,24},{20,28},{24,16},{28,20},{1,9},{5... | collective-permute-start | bytes 1572872 | tf_op jit(solution)/shard_map/ppermute | solution.py:218
  43.0 15.7 %collective-permute-start.4 = (bf16[2,128,1024]{2,1,0:T(8,128)(2,1)S(1)}, bf16[2,128,1024]{2,1,0:T(8,128)(2,1)S(1)}, u32[]{:S(2)}, u32[]{:S(2)}) collective-permute-start(bf16[2,128,1024]{2,1,0:T(8,128)(2,1)S(1)} %sum_pieces.7), channel_id=1, source_target_pairs={{0,4},{4,0},{8,12},{12,8},{16,20},{20,16},{24,28},{28,24},{1,5},{5... | collective-permute-start | bytes 1572872 | tf_op jit(solution)/shard_map/ppermute | solution.py:218
  43.6 14.3 %collective-permute-start.5 = (bf16[128,1024]{1,0:T(8,128)(2,1)S(1)}, bf16[128,1024]{1,0:T(8,128)(2,1)S(1)}, u32[]{:S(2)}, u32[]{:S(2)}) collective-permute-start(bf16[128,1024]{1,0:T(8,128)(2,1)S(1)} %dynamic-slice_bitcast_fusion), channel_id=1, source_target_pairs={{0,16},{4,20},{8,24},{12,28},{16,0},{20,4},{24,8},{28,12},{1,17},{... | collective-permute-start | bytes 786440 | tf_op jit(solution)/shard_map/ppermute | solution.py:218
  44.4 28.8 %copy-start.8 = (bf16[2,128,1024]{2,1,0:T(8,128)(2,1)}, bf16[2,128,1024]{2,1,0:T(8,128)(2,1)S(1)}, u32[]{:S(2)}) copy-start(bf16[2,128,1024]{2,1,0:T(8,128)(2,1)S(1)} %get-tuple-element.48.pair_ref) | copy-start | bytes 1572868
  58.0 13.2 %copy-start.25 = (bf16[128,1024]{1,0:T(8,128)(2,1)}, bf16[128,1024]{1,0:T(8,128)(2,1)S(1)}, u32[]{:S(2)}) copy-start(bf16[128,1024]{1,0:T(8,128)(2,1)S(1)} %collective-permute-done.5) | copy-start | bytes 786436
  58.7 14.5 %copy-start.4 = (bf16[2,128,1024]{2,1,0:T(8,128)(2,1)}, bf16[2,128,1024]{2,1,0:T(8,128)(2,1)S(1)}, u32[]{:S(2)}) copy-start(bf16[2,128,1024]{2,1,0:T(8,128)(2,1)S(1)} %collective-permute-done.4.refs_2_) | copy-start | bytes 1572868
  59.4 17.1 %collective-permute-start.8 = (bf16[9,128,128]{2,1,0:T(8,128)(2,1)S(1)}, bf16[9,128,128]{2,1,0:T(8,128)(2,1)S(1)}, u32[]{:S(2)}, u32[]{:S(2)}) collective-permute-start(bf16[9,128,128]{2,1,0:T(8,128)(2,1)S(1)} %get-tuple-element.45), channel_id=1, source_target_pairs={{0,8},{4,12},{8,0},{12,4},{16,24},{20,28},{24,16},{28,20},{1,9},{5... | collective-permute-start | bytes 884744 | tf_op jit(solution)/shard_map/ppermute | solution.py:218
  61.1 15.4 %collective-permute-start.9 = (bf16[9,128,128]{2,1,0:T(8,128)(2,1)S(1)}, bf16[9,128,128]{2,1,0:T(8,128)(2,1)S(1)}, u32[]{:S(2)}, u32[]{:S(2)}) collective-permute-start(bf16[9,128,128]{2,1,0:T(8,128)(2,1)S(1)} %get-tuple-element.45), channel_id=1, source_target_pairs={{0,4},{4,0},{8,12},{12,8},{16,20},{20,16},{24,28},{28,24},{1,5},{5... | collective-permute-start | bytes 884744 | tf_op jit(solution)/shard_map/ppermute | solution.py:218
  61.6 9.6 %collective-permute-start.6 = (bf16[128,1024]{1,0:T(8,128)(2,1)S(1)}, bf16[128,1024]{1,0:T(8,128)(2,1)S(1)}, u32[]{:S(2)}, u32[]{:S(2)}) collective-permute-start(bf16[128,1024]{1,0:T(8,128)(2,1)S(1)} %bitcast.117), channel_id=1, source_target_pairs={{0,16},{4,20},{8,24},{12,28},{16,0},{20,4},{24,8},{28,12},{1,17},{... | collective-permute-start | bytes 786440 | tf_op jit(solution)/shard_map/ppermute | solution.py:218
  73.2 12.2 %copy-start.5 = (bf16[2,128,1024]{2,1,0:T(8,128)(2,1)S(1)}, bf16[2,128,1024]{2,1,0:T(8,128)(2,1)}, u32[]{:S(2)}) copy-start(bf16[2,128,1024]{2,1,0:T(8,128)(2,1)} %copy-done.4) | copy-start | bytes 1572868
  73.2 12.2 %collective-permute-start.7 = (bf16[128,1024]{1,0:T(8,128)(2,1)}, bf16[128,1024]{1,0:T(8,128)(2,1)}, u32[]{:S(2)}, u32[]{:S(2)}) collective-permute-start(bf16[128,1024]{1,0:T(8,128)(2,1)} %bitcast.9), channel_id=1, source_target_pairs={{0,16},{4,20},{8,24},{12,28},{16,0},{20,4},{24,8},{28,12},{1,17},{... | collective-permute-start | bytes 786440 | tf_op jit(solution)/shard_map/ppermute | solution.py:218
  76.4 0.7 copy-start.10
  77.2 0.7 copy-start.12
  77.9 8.6 %collective-permute-start.11 = (bf16[128,1024]{1,0:T(8,128)(2,1)S(1)}, bf16[128,1024]{1,0:T(8,128)(2,1)}, u32[]{:S(2)}, u32[]{:S(2)}) collective-permute-start(bf16[128,1024]{1,0:T(8,128)(2,1)S(1)} %bitcast.105), channel_id=1, source_target_pairs={{0,4},{4,0},{8,12},{12,8},{16,20},{20,16},{24,28},{28,24},{1,5},{5... | collective-permute-start | bytes 786440 | tf_op jit(solution)/shard_map/ppermute | solution.py:218
  79.2 8.8 %collective-permute-start.10 = (bf16[128,1024]{1,0:T(8,128)(2,1)S(1)}, bf16[128,1024]{1,0:T(8,128)(2,1)}, u32[]{:S(2)}, u32[]{:S(2)}) collective-permute-start(bf16[128,1024]{1,0:T(8,128)(2,1)S(1)} %bitcast.106), channel_id=1, source_target_pairs={{0,8},{4,12},{8,0},{12,4},{16,24},{20,28},{24,16},{28,20},{1,9},{5... | collective-permute-start | bytes 786440 | tf_op jit(solution)/shard_map/ppermute | solution.py:218
  81.6 12.8 %copy-start.9 = (bf16[2,128,1024]{2,1,0:T(8,128)(2,1)S(1)}, bf16[2,128,1024]{2,1,0:T(8,128)(2,1)}, u32[]{:S(2)}) copy-start(bf16[2,128,1024]{2,1,0:T(8,128)(2,1)} %copy-done.8) | copy-start | bytes 1572868
  81.6 12.8 %copy-start.11 = (bf16[9,128,128]{2,1,0:T(8,128)(2,1)S(1)}, bf16[9,128,128]{2,1,0:T(8,128)(2,1)}, u32[]{:S(2)}) copy-start(bf16[9,128,128]{2,1,0:T(8,128)(2,1)} %copy-done.10) | copy-start | bytes 884740
  81.6 12.8 %copy-start.13 = (bf16[9,128,128]{2,1,0:T(8,128)(2,1)S(1)}, bf16[9,128,128]{2,1,0:T(8,128)(2,1)}, u32[]{:S(2)}) copy-start(bf16[9,128,128]{2,1,0:T(8,128)(2,1)} %copy-done.12) | copy-start | bytes 884740
  81.6 12.0 %collective-permute-start.16 = (bf16[9,128,128]{2,1,0:T(8,128)(2,1)}, bf16[9,128,128]{2,1,0:T(8,128)(2,1)S(1)}, u32[]{:S(2)}, u32[]{:S(2)}) collective-permute-start(bf16[9,128,128]{2,1,0:T(8,128)(2,1)} %copy-done.10), channel_id=1, source_target_pairs={{0,4},{4,0},{8,12},{12,8},{16,20},{20,16},{24,28},{28,24},{1,5},{5... | collective-permute-start | bytes 884744 | tf_op jit(solution)/shard_map/ppermute | solution.py:218
  87.9 17.5 %collective-permute-start.13 = (bf16[128,1024]{1,0:T(8,128)(2,1)S(1)}, bf16[128,1024]{1,0:T(8,128)(2,1)S(1)}, u32[]{:S(2)}, u32[]{:S(2)}) collective-permute-start(bf16[128,1024]{1,0:T(8,128)(2,1)S(1)} %bitcast.108), channel_id=1, source_target_pairs={{0,4},{4,0},{8,12},{12,8},{16,20},{20,16},{24,28},{28,24},{1,5},{5... | collective-permute-start | bytes 786440 | tf_op jit(solution)/shard_map/ppermute | solution.py:234
  90.0 15.3 %collective-permute-start.14 = (bf16[128,1024]{1,0:T(8,128)(2,1)S(1)}, bf16[128,1024]{1,0:T(8,128)(2,1)S(1)}, u32[]{:S(2)}, u32[]{:S(2)}) collective-permute-start(bf16[128,1024]{1,0:T(8,128)(2,1)S(1)} %bitcast.109), channel_id=1, source_target_pairs={{0,8},{4,12},{8,0},{12,4},{16,24},{20,28},{24,16},{28,20},{1,9},{5... | collective-permute-start | bytes 786440 | tf_op jit(solution)/shard_map/ppermute | solution.py:234
  90.5 14.9 %collective-permute-start.15 = (bf16[128,1024]{1,0:T(8,128)(2,1)S(1)}, bf16[128,1024]{1,0:T(8,128)(2,1)S(1)}, u32[]{:S(2)}, u32[]{:S(2)}) collective-permute-start(bf16[128,1024]{1,0:T(8,128)(2,1)S(1)} %bitcast.110), channel_id=1, source_target_pairs={{0,12},{4,8},{8,4},{12,0},{16,28},{20,24},{24,20},{28,16},{1,13},{... | collective-permute-start | bytes 786440 | tf_op jit(solution)/shard_map/ppermute | solution.py:234
  92.0 13.4 %collective-permute-start.12 = (bf16[128,1024]{1,0:T(8,128)(2,1)}, bf16[128,1024]{1,0:T(8,128)(2,1)S(1)}, u32[]{:S(2)}, u32[]{:S(2)}) collective-permute-start(bf16[128,1024]{1,0:T(8,128)(2,1)} %collective-permute-done.10.refs_2_), channel_id=1, source_target_pairs={{0,4},{4,0},{8,12},{12,8},{16,20},{20,16},{24,28},{28,24},{1,5},{5... | collective-permute-start | bytes 786440 | tf_op jit(solution)/shard_map/ppermute | solution.py:218
  93.6 20.2 %collective-permute-start.17 = (bf16[128,1024]{1,0:T(8,128)(2,1)S(1)}, bf16[128,1024]{1,0:T(8,128)(2,1)S(1)}, u32[]{:S(2)}, u32[]{:S(2)}) collective-permute-start(bf16[128,1024]{1,0:T(8,128)(2,1)S(1)} %fusion.28), channel_id=1, source_target_pairs={{0,16},{4,20},{8,24},{12,28},{16,0},{20,4},{24,8},{28,12},{1,17},{... | collective-permute-start | bytes 786440 | tf_op jit(solution)/shard_map/ppermute | solution.py:218
  94.4 19.4 %copy-start.23 = (f32[2,128,1024]{2,1,0:T(8,128)S(1)}, f32[2,128,1024]{2,1,0:T(8,128)}, u32[]{:S(2)}) copy-start(f32[2,128,1024]{2,1,0:T(8,128)} %param.11) | copy-start | bytes 3145732
  108.2 21.7 %collective-permute-start.22 = (bf16[2,128,1024]{2,1,0:T(8,128)(2,1)S(1)}, bf16[2,128,1024]{2,1,0:T(8,128)(2,1)S(1)}, u32[]{:S(2)}, u32[]{:S(2)}) collective-permute-start(bf16[2,128,1024]{2,1,0:T(8,128)(2,1)S(1)} %bitcast.113), channel_id=1, source_target_pairs={{0,16},{4,20},{8,24},{12,28},{16,0},{20,4},{24,8},{28,12},{1,17},{... | collective-permute-start | bytes 1572872 | tf_op jit(solution)/shard_map/ppermute | solution.py:218
  109.9 20.1 %collective-permute-start.23 = (bf16[2,128,1024]{2,1,0:T(8,128)(2,1)S(1)}, bf16[2,128,1024]{2,1,0:T(8,128)(2,1)S(1)}, u32[]{:S(2)}, u32[]{:S(2)}) collective-permute-start(bf16[2,128,1024]{2,1,0:T(8,128)(2,1)S(1)} %bitcast.114), channel_id=1, source_target_pairs={{0,8},{4,12},{8,0},{12,4},{16,24},{20,28},{24,16},{28,20},{1,9},{5... | collective-permute-start | bytes 1572872 | tf_op jit(solution)/shard_map/ppermute | solution.py:218
  112.1 17.9 %collective-permute-start.24 = (bf16[2,128,1024]{2,1,0:T(8,128)(2,1)S(1)}, bf16[2,128,1024]{2,1,0:T(8,128)(2,1)S(1)}, u32[]{:S(2)}, u32[]{:S(2)}) collective-permute-start(bf16[2,128,1024]{2,1,0:T(8,128)(2,1)S(1)} %bitcast.115), channel_id=1, source_target_pairs={{0,4},{4,0},{8,12},{12,8},{16,20},{20,16},{24,28},{28,24},{1,5},{5... | collective-permute-start | bytes 1572872 | tf_op jit(solution)/shard_map/ppermute | solution.py:218
  116.7 1.3 collective-permute-start.18
  116.7 5.9 %copy-start.19 = (f32[2,128,1024]{2,1,0:T(8,128)S(1)}, f32[2,128,1024]{2,1,0:T(8,128)}, u32[]{:S(2)}) copy-start(f32[2,128,1024]{2,1,0:T(8,128)} %param.8) | copy-start | bytes 3145732
  116.8 5.9 %copy-start.22 = (f32[2,128,1024]{2,1,0:T(8,128)S(1)}, f32[2,128,1024]{2,1,0:T(8,128)}, u32[]{:S(2)}) copy-start(f32[2,128,1024]{2,1,0:T(8,128)} %param.7) | copy-start | bytes 3145732
  118.7 3.7 %collective-permute-start.19 = (f32[8,128]{1,0:T(8,128)S(1)}, f32[8,128]{1,0:T(8,128)S(1)}, u32[]{:S(2)}, u32[]{:S(2)}) collective-permute-start(f32[8,128]{1,0:T(8,128)S(1)} %fusion.42), channel_id=1, source_target_pairs={{0,2},{1,3},{2,0},{3,1},{4,6},{5,7},{6,4},{7,5},{8,10},{9,11},{10,... | collective-permute-start | bytes 12296 | tf_op jit(solution)/shard_map/ppermute | solution.py:335
  122.3 3.6 %collective-permute-start.20 = (f32[8,128]{1,0:T(8,128)S(1)}, f32[8,128]{1,0:T(8,128)S(1)}, u32[]{:S(2)}, u32[]{:S(2)}) collective-permute-start(f32[8,128]{1,0:T(8,128)S(1)} %add.108), channel_id=1, source_target_pairs={{0,4},{4,0},{8,12},{12,8},{16,20},{20,16},{24,28},{28,24},{1,5},{5... | collective-permute-start | bytes 12296 | tf_op jit(solution)/shard_map/ppermute | solution.py:218
  126.0 4.9 %collective-permute-start.21 = (f32[8,128]{1,0:T(8,128)S(1)}, f32[8,128]{1,0:T(8,128)S(1)}, u32[]{:S(2)}, u32[]{:S(2)}) collective-permute-start(f32[8,128]{1,0:T(8,128)S(1)} %add.109), channel_id=1, source_target_pairs={{0,16},{4,20},{8,24},{12,28},{16,0},{20,4},{24,8},{28,12},{1,17},{... | collective-permute-start | bytes 12296 | tf_op jit(solution)/shard_map/ppermute | solution.py:218
  130.1 35.0 %collective-permute-start.26 = (bf16[2,2,128,1024]{3,2,1,0:T(8,128)(2,1)S(1)}, bf16[2,2,128,1024]{3,2,1,0:T(8,128)(2,1)S(1)}, u32[]{:S(2)}, u32[]{:S(2)}) collective-permute-start(bf16[2,2,128,1024]{3,2,1,0:T(8,128)(2,1)S(1)} %pad_maximum_fusion), channel_id=1, source_target_pairs={{0,4},{4,0},{8,12},{12,8},{16,20},{20,16},{24,28},{28,24},{1,5},{5... | collective-permute-start | bytes 3145736 | tf_op jit(solution)/shard_map/ppermute | solution.py:218
  130.9 6.7 %collective-permute-start.25 = (f32[8,128]{1,0:T(8,128)S(1)}, f32[8,128]{1,0:T(8,128)S(1)}, u32[]{:S(2)}, u32[]{:S(2)}) collective-permute-start(f32[8,128]{1,0:T(8,128)S(1)} %add.110), channel_id=1, source_target_pairs={{0,8},{4,12},{8,0},{12,4},{16,24},{20,28},{24,16},{28,20},{1,9},{5... | collective-permute-start | bytes 12296 | tf_op jit(solution)/shard_map/ppermute | solution.py:218
  132.3 33.1 %collective-permute-start.27 = (bf16[2,128,1024]{2,1,0:T(8,128)(2,1)S(1)}, bf16[2,128,1024]{2,1,0:T(8,128)(2,1)S(1)}, u32[]{:S(2)}, u32[]{:S(2)}) collective-permute-start(bf16[2,128,1024]{2,1,0:T(8,128)(2,1)S(1)} %collective-permute-done.22), channel_id=1, source_target_pairs={{0,12},{4,8},{8,4},{12,0},{16,28},{20,24},{24,20},{28,16},{1,13},{... | collective-permute-start | bytes 1572872 | tf_op jit(solution)/shard_map/ppermute | solution.py:361
  133.9 32.8 %collective-permute-start.28 = (bf16[2,128,1024]{2,1,0:T(8,128)(2,1)S(1)}, bf16[2,128,1024]{2,1,0:T(8,128)(2,1)S(1)}, u32[]{:S(2)}, u32[]{:S(2)}) collective-permute-start(bf16[2,128,1024]{2,1,0:T(8,128)(2,1)S(1)} %collective-permute-done.22), channel_id=1, source_target_pairs={{0,8},{4,12},{8,0},{12,4},{16,24},{20,28},{24,16},{28,20},{1,9},{5... | collective-permute-start | bytes 1572872 | tf_op jit(solution)/shard_map/ppermute | solution.py:361
  135.5 31.3 %collective-permute-start.29 = (bf16[2,128,1024]{2,1,0:T(8,128)(2,1)S(1)}, bf16[2,128,1024]{2,1,0:T(8,128)(2,1)S(1)}, u32[]{:S(2)}, u32[]{:S(2)}) collective-permute-start(bf16[2,128,1024]{2,1,0:T(8,128)(2,1)S(1)} %pad_maximum_fusion.4), channel_id=1, source_target_pairs={{0,16},{4,20},{8,24},{12,28},{16,0},{20,4},{24,8},{28,12},{1,17},{... | collective-permute-start | bytes 1572872 | tf_op jit(solution)/shard_map/ppermute | solution.py:218
  140.0 26.8 %copy-start.17 = (f32[2,128,1024]{2,1,0:T(8,128)S(1)}, f32[2,128,1024]{2,1,0:T(8,128)}, u32[]{:S(2)}) copy-start(f32[2,128,1024]{2,1,0:T(8,128)} %param.8) | copy-start | bytes 3145732
  140.1 26.8 %copy-start.20 = (f32[2,128,1024]{2,1,0:T(8,128)S(1)}, f32[2,128,1024]{2,1,0:T(8,128)}, u32[]{:S(2)}) copy-start(f32[2,128,1024]{2,1,0:T(8,128)} %param.7) | copy-start | bytes 3145732
  166.8 2.0 %copy-start.16 = (bf16[2,2,4,128,1024]{4,3,2,1,0:T(8,128)(2,1)}, bf16[2,2,4,128,1024]{4,3,2,1,0:T(8,128)(2,1)S(1)}, u32[]{:S(2)}) copy-start(bf16[2,2,4,128,1024]{4,3,2,1,0:T(8,128)(2,1)S(1)} %fusion.20) | copy-start | bytes 12582916
  167.1 2.1 %copy-start.18 = (f32[2,128,1024]{2,1,0:T(8,128)}, f32[2,128,1024]{2,1,0:T(8,128)S(1)}, u32[]{:S(2)}) copy-start(f32[2,128,1024]{2,1,0:T(8,128)S(1)} %get-tuple-element.70) | copy-start | bytes 3145732
  167.1 2.4 %copy-start.21 = (f32[2,128,1024]{2,1,0:T(8,128)}, f32[2,128,1024]{2,1,0:T(8,128)S(1)}, u32[]{:S(2)}) copy-start(f32[2,128,1024]{2,1,0:T(8,128)S(1)} %get-tuple-element.71) | copy-start | bytes 3145732

commit v7 on v6

--- a/solution.py
+++ b/solution.py
@@ -247,7 +247,8 @@
     first_sends = cut(grads, bits, [order[0] for order in orders], True)
     first_own = cut(after(grads, *first_sends), bits, [order[0] for order in orders], False)
     terms, places = [[], []], [{}, {}]
-    right_partner = swap(choose(right_root, 1 - half), top)
+    roots_away = jnp.stack([choose(right_root, 1 - half), choose(left_root, 1 - half)])
+    right_partner, left_partner = swap(roots_away, top)
 
     place = jnp.stack([member, half, index])
 
@@ -272,7 +273,6 @@
 
     reduce_step(1, 0)
     reduce_step(0, 0)
-    left_partner = swap(after(choose(left_root, 1 - half), terms[0][-1][0], terms[1][-1][0]), top)
     for step in range(1, bits - 1):
         for part in range(2):
             reduce_step(part, step, right_partner)

time: 170 us -> 174 us (1.024)
  waiting for transfers between devices: 91.8 us -> 97.7 us
  starting transfers between devices: 43.4 us -> 39.1 us
  other arithmetic: 6.5 us -> 9.28 us
    ppermute x23 -> x22, waiting for transfers between devices: 88.9 us -> 94.9 us  [swap(): lax.ppermute(array, 'dp', [(i, i ^ 1 << bit) for i in range(devices)])]
    ppermute x23 -> x22, starting transfers between devices: 34.5 us -> 31.2 us  [swap(): lax.ppermute(array, 'dp', [(i, i ^ 1 << bit) for i in range(devices)])]
    select_n x0 -> x1, other arithmetic: none -> 1.96 us  [by_half(): jnp.where(half == 0, own, partner)]
    unnamed x52 -> x40, local copies, waits for them, and re-layouts: 8.98 us -> 7.56 us
  transfers between devices with their start and end apart: 30 -> 29, of which waited for: 13 -> 12; matrix products, arithmetic and copies ran while one was open for 6% -> 7% of each run, Pallas kernels for 5% -> 6%
where the time goes in v7:
time: 174 us; the launch traced here: 173 us
  waiting for transfers between devices  97.7 us (56%)
  starting transfers between devices  39.1 us (22%)
  Pallas kernels  13.4 us (8%)
  local copies, waits for them, and re-layouts  9.66 us (6%)
  other arithmetic  9.28 us (5%)
  between operations  2.5 us (1%)
    ppermute x22, waiting for transfers between devices, swap(): lax.ppermute(array, 'dp', [(i, i ^ 1 << bit) for i in range(devices)])  94.9 us
    ppermute x22, starting transfers between devices, swap(): lax.ppermute(array, 'dp', [(i, i ^ 1 << bit) for i in range(devices)])  31.2 us
    pallas_call x9, Pallas kernels, run(): pl.pallas_call(kernel, out_shape=out_shape, in_specs=[SMEM] + [VMEM] * le...  10.2 us
    unnamed x40, local copies, waits for them, and re-layouts  7.56 us
    ppermute x3, starting transfers between devices, gather_direct(): pieces[k] = lax.ppermute(own, 'dp', [(i, i ^ k) for i in range(devices)])  3.49 us
  transfers between devices with their start and end apart: 29, of which 12 were waited for; matrix products, arithmetic and copies ran while one was open for 7% of the time, Pallas kernels for 6%

profile of v7, /device:TPU:0, one launch (start us, length us, event | category | flops | bytes accessed | tf_op | source)
XLA Modules:
  0.0 173.3 jit_solution(7042432988472393889)
XLA Ops:
  0.6 3.0 %cut.2 = (bf16[4,128,1024]{2,1,0:T(8,128)(2,1)}, bf16[4,128,1024]{2,1,0:T(8,128)(2,1)}) custom-call(bf16[2,2,4,128,1024]{4,3,2,1,0:T(8,128)(2,1)} %bitcast.90), custom_call_target="tpu_custom_call" | custom-call | bytes 4194304 | tf_op jit(solution)/shard_map/cut/pallas_call | solution.py:69
  3.6 3.0 %collective-permute-start = (bf16[4,128,1024]{2,1,0:T(8,128)(2,1)}, bf16[4,128,1024]{2,1,0:T(8,128)(2,1)S(1)}, u32[]{:S(2)}, u32[]{:S(2)}) collective-permute-start(bf16[4,128,1024]{2,1,0:T(8,128)(2,1)} %get-tuple-element.33), channel_id=1, source_target_pairs={{0,4},{4,0},{8,12},{12,8},{16,20},{20,16},{24,28},{28,24},{1,5},{5... | collective-permute-start | bytes 3145736 | tf_op jit(solution)/shard_map/ppermute | solution.py:218
  6.6 1.6 collective-permute-start.3
  8.2 1.0 constant_dynamic-slice_fusion
  9.2 0.8 pad_maximum_fusion.2
  10.1 2.6 %collective-permute-start.1 = (bf16[2,128,1024]{2,1,0:T(8,128)(2,1)}, bf16[2,128,1024]{2,1,0:T(8,128)(2,1)}, u32[]{:S(2)}, u32[]{:S(2)}) collective-permute-start(bf16[2,128,1024]{2,1,0:T(8,128)(2,1)} %pad_maximum_fusion.2), channel_id=1, source_target_pairs={{0,16},{4,20},{8,24},{12,28},{16,0},{20,4},{24,8},{28,12},{1,17},{... | collective-permute-start | bytes 1572872 | tf_op jit(solution)/shard_map/ppermute | solution.py:218
  12.7 2.2 %copy-done = bf16[1,2,1024,1024]{3,2,1,0:T(8,128)(2,1)S(1)} copy-done((bf16[1,2,1024,1024]{3,2,1,0:T(8,128)(2,1)S(1)}, bf16[1,2,1024,1024]{3,2,1,0:T(8,128)(2,1)}, u32[]{:S(2)}) %copy-start) | copy-done | bytes 4194328
  15.1 1.0 copy-done.1
  16.1 25.8 %collective-permute-done.1 = bf16[2,128,1024]{2,1,0:T(8,128)(2,1)} collective-permute-done((bf16[2,128,1024]{2,1,0:T(8,128)(2,1)}, bf16[2,128,1024]{2,1,0:T(8,128)(2,1)}, u32[]{:S(2)}, u32[]{:S(2)}) %collective-permute-start.1) | collective-permute-done | bytes 524320 | tf_op jit(solution)/shard_map/ppermute | solution.py:218
  41.9 2.0 %broadcast_select_fusion.1 = (bf16[1,128,1024]{2,1,0:T(8,128)(2,1)}, bf16[1,128,1024]{2,1,0:T(8,128)(2,1)}, bf16[128,1024]{1,0:T(8,128)(2,1)S(1)}) fusion(pred[]{:T(512)S(6)} %eq.17, bf16[2,128,1024]{2,1,0:T(8,128)(2,1)} %collective-permute-done.1, bf16[2,128,1024]{2,1,0:T(8,128)(2,1)} %param.9, s32[]{:T(128)S(6)} %select_n.97), kind=kLoop, calls=%fused_computation.65 | loop fusion | flops 262144 | bytes 1572869 | tf_op jit(solution)/shard_map/jit(_where)/select_n | solution.py:238
  43.9 1.2 copy-done.2
  45.1 0.7 sum_pieces.6
  45.8 3.6 %collective-permute-start.2 = (bf16[2,128,1024]{2,1,0:T(8,128)(2,1)S(1)}, bf16[2,128,1024]{2,1,0:T(8,128)(2,1)S(1)}, u32[]{:S(2)}, u32[]{:S(2)}) collective-permute-start(bf16[2,128,1024]{2,1,0:T(8,128)(2,1)S(1)} %sum_pieces.6), channel_id=1, source_target_pairs={{0,8},{4,12},{8,0},{12,4},{16,24},{20,28},{24,16},{28,20},{1,9},{5... | collective-permute-start | bytes 1572872 | tf_op jit(solution)/shard_map/ppermute | solution.py:218
  49.3 0.7 sum_pieces.7
  50.0 0.6 collective-permute-start.4
  50.6 0.7 pack.1
  51.3 8.8 %collective-permute-done.2.refs_2_ = bf16[2,128,1024]{2,1,0:T(8,128)(2,1)S(1)} collective-permute-done((bf16[2,128,1024]{2,1,0:T(8,128)(2,1)S(1)}, bf16[2,128,1024]{2,1,0:T(8,128)(2,1)S(1)}, u32[]{:S(2)}, u32[]{:S(2)}) %collective-permute-start.2) | collective-permute-done | bytes 524320 | tf_op jit(solution)/shard_map/ppermute | solution.py:218
  60.1 2.2 %collective-permute-done.4.refs_2_ = bf16[2,128,1024]{2,1,0:T(8,128)(2,1)S(1)} collective-permute-done((bf16[2,128,1024]{2,1,0:T(8,128)(2,1)S(1)}, bf16[2,128,1024]{2,1,0:T(8,128)(2,1)S(1)}, u32[]{:S(2)}, u32[]{:S(2)}) %collective-permute-start.4) | collective-permute-done | bytes 524320 | tf_op jit(solution)/shard_map/ppermute | solution.py:218
  62.3 0.6 sum_pieces.8
  62.9 0.4 collective-permute-start.7
  63.3 0.5 collective-permute-start.8
  63.8 1.6 collective-permute-start.5
  65.4 10.3 %collective-permute-done.5 = bf16[128,1024]{1,0:T(8,128)(2,1)S(1)} collective-permute-done((bf16[128,1024]{1,0:T(8,128)(2,1)S(1)}, bf16[128,1024]{1,0:T(8,128)(2,1)S(1)}, u32[]{:S(2)}, u32[]{:S(2)}) %collective-permute-start.5) | collective-permute-done | bytes 262176 | tf_op jit(solution)/shard_map/ppermute | solution.py:218
  75.7 0.7 sum_pieces.9
  76.4 1.4 sum_pieces.10
  77.8 0.9 collective-permute-start.6
  78.6 0.7 copy-done.10
  79.4 0.7 collective-permute-start.10
  80.1 2.1 %collective-permute-start.9 = (bf16[128,1024]{1,0:T(8,128)(2,1)S(1)}, bf16[128,1024]{1,0:T(8,128)(2,1)}, u32[]{:S(2)}, u32[]{:S(2)}) collective-permute-start(bf16[128,1024]{1,0:T(8,128)(2,1)S(1)} %bitcast.93), channel_id=1, source_target_pairs={{0,8},{4,12},{8,0},{12,4},{16,24},{20,28},{24,16},{28,20},{1,9},{5... | collective-permute-start | bytes 786440 | tf_op jit(solution)/shard_map/ppermute | solution.py:218
  82.1 5.8 %collective-permute-done.6 = bf16[128,1024]{1,0:T(8,128)(2,1)} collective-permute-done((bf16[128,1024]{1,0:T(8,128)(2,1)}, bf16[128,1024]{1,0:T(8,128)(2,1)}, u32[]{:S(2)}, u32[]{:S(2)}) %collective-permute-start.6) | collective-permute-done | bytes 262176 | tf_op jit(solution)/shard_map/ppermute | solution.py:218
  88.0 1.1 sum_pieces.11
  89.1 0.5 collective-permute-done.9.refs_2_
  89.6 2.0 %collective-permute-start.12 = (bf16[128,1024]{1,0:T(8,128)(2,1)S(1)}, bf16[128,1024]{1,0:T(8,128)(2,1)S(1)}, u32[]{:S(2)}, u32[]{:S(2)}) collective-permute-start(bf16[128,1024]{1,0:T(8,128)(2,1)S(1)} %bitcast.95), channel_id=1, source_target_pairs={{0,4},{4,0},{8,12},{12,8},{16,20},{20,16},{24,28},{28,24},{1,5},{5... | collective-permute-start | bytes 786440 | tf_op jit(solution)/shard_map/ppermute | solution.py:234
  91.6 1.5 collective-permute-start.14
  93.1 2.0 %collective-permute-start.11 = (bf16[128,1024]{1,0:T(8,128)(2,1)}, bf16[128,1024]{1,0:T(8,128)(2,1)S(1)}, u32[]{:S(2)}, u32[]{:S(2)}) collective-permute-start(bf16[128,1024]{1,0:T(8,128)(2,1)} %collective-permute-done.9.refs_2_), channel_id=1, source_target_pairs={{0,4},{4,0},{8,12},{12,8},{16,20},{20,16},{24,28},{28,24},{1,5},{5... | collective-permute-start | bytes 786440 | tf_op jit(solution)/shard_map/ppermute | solution.py:218
  95.2 2.5 %collective-permute-start.16 = (bf16[128,1024]{1,0:T(8,128)(2,1)S(1)}, bf16[128,1024]{1,0:T(8,128)(2,1)S(1)}, u32[]{:S(2)}, u32[]{:S(2)}) collective-permute-start(bf16[128,1024]{1,0:T(8,128)(2,1)S(1)} %fusion.28), channel_id=1, source_target_pairs={{0,16},{4,20},{8,24},{12,28},{16,0},{20,4},{24,8},{28,12},{1,17},{... | collective-permute-start | bytes 786440 | tf_op jit(solution)/shard_map/ppermute | solution.py:218
  97.6 1.1 pad_maximum_fusion.3
  98.8 1.7 unfold.1.refs_8_
  100.5 6.3 %collective-permute-done.11.refs_3_ = bf16[128,1024]{1,0:T(8,128)(2,1)S(1)} collective-permute-done((bf16[128,1024]{1,0:T(8,128)(2,1)}, bf16[128,1024]{1,0:T(8,128)(2,1)S(1)}, u32[]{:S(2)}, u32[]{:S(2)}) %collective-permute-start.11) | collective-permute-done | bytes 262176 | tf_op jit(solution)/shard_map/ppermute | solution.py:218
  106.9 2.8 %product.1 = (bf16[256,1024]{1,0:T(8,128)(2,1)S(1)}, bf16[1024,1024]{1,0:T(8,128)(2,1)S(1)}, f32[8,128]{1,0:T(8,128)S(1)}) custom-call(s32[3]{0:T(128)S(1)} %pad_add_fusion.place_ref, bf16[128,1024]{1,0:T(8,128)(2,1)S(1)} %bitcast.94, bf16[128,1024]{1,0:T(8,128)(2,1)} %collective-permute-done.10.refs_1_, bf16[128,1024]{1,0:T(8,128)(2,1)} %collective-permute-done.9.refs_2_, ...), custom_call_target="tpu_custom_call" | custom-call | flops 1073741824 | bytes 4718592 | tf_op jit(solution)/shard_map/product/pallas_call | solution.py:31
  109.7 1.1 collective-permute-start.21
  110.7 0.9 collective-permute-start.22
  111.6 0.9 collective-permute-start.23
  112.6 2.1 %fusion.4 = (f32[]{:T(128)}, f32[2,128,1024]{2,1,0:T(8,128)}) fusion(bf16[1,128,1024]{2,1,0:T(8,128)(2,1)S(1)} %get-tuple-element.67, bf16[1,128,1024]{2,1,0:T(8,128)(2,1)S(1)} %get-tuple-element.66, f32[2,128,1024]{2,1,0:T(8,128)S(1)} %copy-done.19), kind=kLoop, calls=%fused_computation.21 | loop fusion | flops 2621439 | bytes 2621444 | tf_op jit(solution)/shard_map/reduce_sum | solution.py:330
  114.8 0.6 broadcast_select_fusion.2
  115.5 0.7 fusion
  116.3 0.5 convolution_bitcast_fusion.1
  116.8 0.7 fusion.40
  117.4 1.6 collective-permute-start.18
  119.0 0.5 convolution_bitcast_fusion
  119.5 1.6 collective-permute-done.18
  121.1 1.1 collective-permute-start.19
  122.2 0.4 fusion.26
  122.6 2.1 %collective-permute-done.19 = f32[8,128]{1,0:T(8,128)S(1)} collective-permute-done((f32[8,128]{1,0:T(8,128)S(1)}, f32[8,128]{1,0:T(8,128)S(1)}, u32[]{:S(2)}, u32[]{:S(2)}) %collective-permute-start.19) | collective-permute-done | bytes 4128 | tf_op jit(solution)/shard_map/ppermute | solution.py:218
  124.7 1.7 collective-permute-start.20
  126.4 6.0 %collective-permute-done.21 = bf16[2,128,1024]{2,1,0:T(8,128)(2,1)S(1)} collective-permute-done((bf16[2,128,1024]{2,1,0:T(8,128)(2,1)S(1)}, bf16[2,128,1024]{2,1,0:T(8,128)(2,1)S(1)}, u32[]{:S(2)}, u32[]{:S(2)}) %collective-permute-start.21) | collective-permute-done | bytes 524320 | tf_op jit(solution)/shard_map/ppermute | solution.py:218
  132.8 0.8 collective-permute-start.24
  133.7 2.8 %collective-permute-start.26 = (bf16[2,128,1024]{2,1,0:T(8,128)(2,1)S(1)}, bf16[2,128,1024]{2,1,0:T(8,128)(2,1)S(1)}, u32[]{:S(2)}, u32[]{:S(2)}) collective-permute-start(bf16[2,128,1024]{2,1,0:T(8,128)(2,1)S(1)} %collective-permute-done.21), channel_id=1, source_target_pairs={{0,12},{4,8},{8,4},{12,0},{16,28},{20,24},{24,20},{28,16},{1,13},{... | collective-permute-start | bytes 1572872 | tf_op jit(solution)/shard_map/ppermute | solution.py:361
  136.5 2.6 %collective-permute-start.28 = (bf16[2,128,1024]{2,1,0:T(8,128)(2,1)S(1)}, bf16[2,128,1024]{2,1,0:T(8,128)(2,1)S(1)}, u32[]{:S(2)}, u32[]{:S(2)}) collective-permute-start(bf16[2,128,1024]{2,1,0:T(8,128)(2,1)S(1)} %pad_maximum_fusion.5), channel_id=1, source_target_pairs={{0,16},{4,20},{8,24},{12,28},{16,0},{20,4},{24,8},{28,12},{1,17},{... | collective-permute-start | bytes 1572872 | tf_op jit(solution)/shard_map/ppermute | solution.py:218
  139.1 0.6 fusion.36
  141.1 0.5 broadcast_in_dim.31
  142.0 26.9 %collective-permute-done.25 = bf16[2,2,128,1024]{3,2,1,0:T(8,128)(2,1)S(1)} collective-permute-done((bf16[2,2,128,1024]{3,2,1,0:T(8,128)(2,1)S(1)}, bf16[2,2,128,1024]{3,2,1,0:T(8,128)(2,1)S(1)}, u32[]{:S(2)}, u32[]{:S(2)}) %collective-permute-start.25) | collective-permute-done | bytes 1048608 | tf_op jit(solution)/shard_map/ppermute | solution.py:218
  169.4 1.2 collective-permute-done.27
  170.9 1.7 %copy-done.12 = bf16[2,2,4,128,1024]{4,3,2,1,0:T(8,128)(2,1)} copy-done((bf16[2,2,4,128,1024]{4,3,2,1,0:T(8,128)(2,1)}, bf16[2,2,4,128,1024]{4,3,2,1,0:T(8,128)(2,1)S(1)}, u32[]{:S(2)}) %copy-start.12) | copy-done | bytes 4194328
  (80 shorter events, 2.8 us)
Async XLA Ops:
  0.6 8.6 %copy-start.6 = (bf16[2,128,1024]{2,1,0:T(8,128)(2,1)S(1)}, bf16[2,128,1024]{2,1,0:T(8,128)(2,1)}, u32[]{:S(2)}) copy-start(bf16[2,128,1024]{2,1,0:T(8,128)(2,1)} %own_ref.1) | copy-start | bytes 1572868
  3.6 40.3 %collective-permute-start = (bf16[4,128,1024]{2,1,0:T(8,128)(2,1)}, bf16[4,128,1024]{2,1,0:T(8,128)(2,1)S(1)}, u32[]{:S(2)}, u32[]{:S(2)}) collective-permute-start(bf16[4,128,1024]{2,1,0:T(8,128)(2,1)} %get-tuple-element.33), channel_id=1, source_target_pairs={{0,4},{4,0},{8,12},{12,8},{16,20},{20,16},{24,28},{28,24},{1,5},{5... | collective-permute-start | bytes 3145736 | tf_op jit(solution)/shard_map/ppermute | solution.py:218
  6.6 42.7 %collective-permute-start.3 = (bf16[4,128,1024]{2,1,0:T(8,128)(2,1)}, bf16[4,128,1024]{2,1,0:T(8,128)(2,1)S(1)}, u32[]{:S(2)}, u32[]{:S(2)}) collective-permute-start(bf16[4,128,1024]{2,1,0:T(8,128)(2,1)} %get-tuple-element.34), channel_id=1, source_target_pairs={{0,8},{4,12},{8,0},{12,4},{16,24},{20,28},{24,16},{28,20},{1,9},{5... | collective-permute-start | bytes 3145736 | tf_op jit(solution)/shard_map/ppermute | solution.py:218
  10.1 31.8 %collective-permute-start.1 = (bf16[2,128,1024]{2,1,0:T(8,128)(2,1)}, bf16[2,128,1024]{2,1,0:T(8,128)(2,1)}, u32[]{:S(2)}, u32[]{:S(2)}) collective-permute-start(bf16[2,128,1024]{2,1,0:T(8,128)(2,1)} %pad_maximum_fusion.2), channel_id=1, source_target_pairs={{0,16},{4,20},{8,24},{12,28},{16,0},{20,4},{24,8},{28,12},{1,17},{... | collective-permute-start | bytes 1572872 | tf_op jit(solution)/shard_map/ppermute | solution.py:218
  12.7 2.2 %copy-start = (bf16[1,2,1024,1024]{3,2,1,0:T(8,128)(2,1)S(1)}, bf16[1,2,1024,1024]{3,2,1,0:T(8,128)(2,1)}, u32[]{:S(2)}) copy-start(bf16[1,2,1024,1024]{3,2,1,0:T(8,128)(2,1)} %param.6) | copy-start | bytes 12582916
  15.1 1.0 copy-start.1
  16.1 34.5 %copy-start.7 = (bf16[2,128,1024]{2,1,0:T(8,128)(2,1)S(1)}, bf16[2,128,1024]{2,1,0:T(8,128)(2,1)}, u32[]{:S(2)}) copy-start(bf16[2,128,1024]{2,1,0:T(8,128)(2,1)} %own_ref.1) | copy-start | bytes 1572868
  16.1 46.2 %copy-start.3 = (bf16[4,128,1024]{2,1,0:T(8,128)(2,1)S(1)}, bf16[4,128,1024]{2,1,0:T(8,128)(2,1)}, u32[]{:S(2)}) copy-start(bf16[4,128,1024]{2,1,0:T(8,128)(2,1)} %copy-done.1) | copy-start | bytes 3145732
  43.9 1.2 copy-start.2
  45.8 14.3 %collective-permute-start.2 = (bf16[2,128,1024]{2,1,0:T(8,128)(2,1)S(1)}, bf16[2,128,1024]{2,1,0:T(8,128)(2,1)S(1)}, u32[]{:S(2)}, u32[]{:S(2)}) collective-permute-start(bf16[2,128,1024]{2,1,0:T(8,128)(2,1)S(1)} %sum_pieces.6), channel_id=1, source_target_pairs={{0,8},{4,12},{8,0},{12,4},{16,24},{20,28},{24,16},{28,20},{1,9},{5... | collective-permute-start | bytes 1572872 | tf_op jit(solution)/shard_map/ppermute | solution.py:218
  50.0 12.3 %collective-permute-start.4 = (bf16[2,128,1024]{2,1,0:T(8,128)(2,1)S(1)}, bf16[2,128,1024]{2,1,0:T(8,128)(2,1)S(1)}, u32[]{:S(2)}, u32[]{:S(2)}) collective-permute-start(bf16[2,128,1024]{2,1,0:T(8,128)(2,1)S(1)} %sum_pieces.7), channel_id=1, source_target_pairs={{0,4},{4,0},{8,12},{12,8},{16,20},{20,16},{24,28},{28,24},{1,5},{5... | collective-permute-start | bytes 1572872 | tf_op jit(solution)/shard_map/ppermute | solution.py:218
  51.2 26.5 %copy-start.8 = (bf16[2,128,1024]{2,1,0:T(8,128)(2,1)}, bf16[2,128,1024]{2,1,0:T(8,128)(2,1)S(1)}, u32[]{:S(2)}) copy-start(bf16[2,128,1024]{2,1,0:T(8,128)(2,1)S(1)} %get-tuple-element.46.pair_ref) | copy-start | bytes 1572868
  62.3 15.5 %copy-start.4 = (bf16[2,128,1024]{2,1,0:T(8,128)(2,1)}, bf16[2,128,1024]{2,1,0:T(8,128)(2,1)S(1)}, u32[]{:S(2)}) copy-start(bf16[2,128,1024]{2,1,0:T(8,128)(2,1)S(1)} %collective-permute-done.4.refs_2_) | copy-start | bytes 1572868
  62.9 15.7 %collective-permute-start.7 = (bf16[9,128,128]{2,1,0:T(8,128)(2,1)S(1)}, bf16[9,128,128]{2,1,0:T(8,128)(2,1)}, u32[]{:S(2)}, u32[]{:S(2)}) collective-permute-start(bf16[9,128,128]{2,1,0:T(8,128)(2,1)S(1)} %get-tuple-element.43), channel_id=1, source_target_pairs={{0,8},{4,12},{8,0},{12,4},{16,24},{20,28},{24,16},{28,20},{1,9},{5... | collective-permute-start | bytes 884744 | tf_op jit(solution)/shard_map/ppermute | solution.py:218
  63.3 15.4 %collective-permute-start.8 = (bf16[9,128,128]{2,1,0:T(8,128)(2,1)S(1)}, bf16[9,128,128]{2,1,0:T(8,128)(2,1)S(1)}, u32[]{:S(2)}, u32[]{:S(2)}) collective-permute-start(bf16[9,128,128]{2,1,0:T(8,128)(2,1)S(1)} %get-tuple-element.43), channel_id=1, source_target_pairs={{0,4},{4,0},{8,12},{12,8},{16,20},{20,16},{24,28},{28,24},{1,5},{5... | collective-permute-start | bytes 884744 | tf_op jit(solution)/shard_map/ppermute | solution.py:218
  63.8 11.9 %collective-permute-start.5 = (bf16[128,1024]{1,0:T(8,128)(2,1)S(1)}, bf16[128,1024]{1,0:T(8,128)(2,1)S(1)}, u32[]{:S(2)}, u32[]{:S(2)}) collective-permute-start(bf16[128,1024]{1,0:T(8,128)(2,1)S(1)} %bitcast.104), channel_id=1, source_target_pairs={{0,16},{4,20},{8,24},{12,28},{16,0},{20,4},{24,8},{28,12},{1,17},{... | collective-permute-start | bytes 786440 | tf_op jit(solution)/shard_map/ppermute | solution.py:218
  77.8 10.2 %copy-start.5 = (bf16[2,128,1024]{2,1,0:T(8,128)(2,1)S(1)}, bf16[2,128,1024]{2,1,0:T(8,128)(2,1)}, u32[]{:S(2)}) copy-start(bf16[2,128,1024]{2,1,0:T(8,128)(2,1)} %copy-done.4) | copy-start | bytes 1572868
  77.8 10.2 %collective-permute-start.6 = (bf16[128,1024]{1,0:T(8,128)(2,1)}, bf16[128,1024]{1,0:T(8,128)(2,1)}, u32[]{:S(2)}, u32[]{:S(2)}) collective-permute-start(bf16[128,1024]{1,0:T(8,128)(2,1)} %bitcast.8), channel_id=1, source_target_pairs={{0,16},{4,20},{8,24},{12,28},{16,0},{20,4},{24,8},{28,12},{1,17},{... | collective-permute-start | bytes 786440 | tf_op jit(solution)/shard_map/ppermute | solution.py:218
  78.6 0.7 copy-start.10
  79.4 9.7 %collective-permute-start.10 = (bf16[128,1024]{1,0:T(8,128)(2,1)S(1)}, bf16[128,1024]{1,0:T(8,128)(2,1)}, u32[]{:S(2)}, u32[]{:S(2)}) collective-permute-start(bf16[128,1024]{1,0:T(8,128)(2,1)S(1)} %bitcast.92), channel_id=1, source_target_pairs={{0,4},{4,0},{8,12},{12,8},{16,20},{20,16},{24,28},{28,24},{1,5},{5... | collective-permute-start | bytes 786440 | tf_op jit(solution)/shard_map/ppermute | solution.py:218
  80.1 9.5 %collective-permute-start.9 = (bf16[128,1024]{1,0:T(8,128)(2,1)S(1)}, bf16[128,1024]{1,0:T(8,128)(2,1)}, u32[]{:S(2)}, u32[]{:S(2)}) collective-permute-start(bf16[128,1024]{1,0:T(8,128)(2,1)S(1)} %bitcast.93), channel_id=1, source_target_pairs={{0,8},{4,12},{8,0},{12,4},{16,24},{20,28},{24,16},{28,20},{1,9},{5... | collective-permute-start | bytes 786440 | tf_op jit(solution)/shard_map/ppermute | solution.py:218
  82.1 13.0 %collective-permute-start.15 = (bf16[9,128,128]{2,1,0:T(8,128)(2,1)}, bf16[9,128,128]{2,1,0:T(8,128)(2,1)}, u32[]{:S(2)}, u32[]{:S(2)}) collective-permute-start(bf16[9,128,128]{2,1,0:T(8,128)(2,1)} %collective-permute-done.7.refs_1_), channel_id=1, source_target_pairs={{0,4},{4,0},{8,12},{12,8},{16,20},{20,16},{24,28},{28,24},{1,5},{5... | collective-permute-start | bytes 884744 | tf_op jit(solution)/shard_map/ppermute | solution.py:218
  82.1 16.6 %copy-start.9 = (bf16[2,128,1024]{2,1,0:T(8,128)(2,1)S(1)}, bf16[2,128,1024]{2,1,0:T(8,128)(2,1)}, u32[]{:S(2)}) copy-start(bf16[2,128,1024]{2,1,0:T(8,128)(2,1)} %copy-done.8) | copy-start | bytes 1572868
  82.1 16.6 %copy-start.11 = (bf16[9,128,128]{2,1,0:T(8,128)(2,1)S(1)}, bf16[9,128,128]{2,1,0:T(8,128)(2,1)}, u32[]{:S(2)}) copy-start(bf16[9,128,128]{2,1,0:T(8,128)(2,1)} %copy-done.10) | copy-start | bytes 884740
  89.6 17.3 %collective-permute-start.12 = (bf16[128,1024]{1,0:T(8,128)(2,1)S(1)}, bf16[128,1024]{1,0:T(8,128)(2,1)S(1)}, u32[]{:S(2)}, u32[]{:S(2)}) collective-permute-start(bf16[128,1024]{1,0:T(8,128)(2,1)S(1)} %bitcast.95), channel_id=1, source_target_pairs={{0,4},{4,0},{8,12},{12,8},{16,20},{20,16},{24,28},{28,24},{1,5},{5... | collective-permute-start | bytes 786440 | tf_op jit(solution)/shard_map/ppermute | solution.py:234
  91.6 15.3 %collective-permute-start.13 = (bf16[128,1024]{1,0:T(8,128)(2,1)S(1)}, bf16[128,1024]{1,0:T(8,128)(2,1)S(1)}, u32[]{:S(2)}, u32[]{:S(2)}) collective-permute-start(bf16[128,1024]{1,0:T(8,128)(2,1)S(1)} %bitcast.96), channel_id=1, source_target_pairs={{0,8},{4,12},{8,0},{12,4},{16,24},{20,28},{24,16},{28,20},{1,9},{5... | collective-permute-start | bytes 786440 | tf_op jit(solution)/shard_map/ppermute | solution.py:234
  91.6 15.3 %collective-permute-start.14 = (bf16[128,1024]{1,0:T(8,128)(2,1)S(1)}, bf16[128,1024]{1,0:T(8,128)(2,1)S(1)}, u32[]{:S(2)}, u32[]{:S(2)}) collective-permute-start(bf16[128,1024]{1,0:T(8,128)(2,1)S(1)} %bitcast.97), channel_id=1, source_target_pairs={{0,12},{4,8},{8,4},{12,0},{16,28},{20,24},{24,20},{28,16},{1,13},{... | collective-permute-start | bytes 786440 | tf_op jit(solution)/shard_map/ppermute | solution.py:234
  93.1 13.8 %collective-permute-start.11 = (bf16[128,1024]{1,0:T(8,128)(2,1)}, bf16[128,1024]{1,0:T(8,128)(2,1)S(1)}, u32[]{:S(2)}, u32[]{:S(2)}) collective-permute-start(bf16[128,1024]{1,0:T(8,128)(2,1)} %collective-permute-done.9.refs_2_), channel_id=1, source_target_pairs={{0,4},{4,0},{8,12},{12,8},{16,20},{20,16},{24,28},{28,24},{1,5},{5... | collective-permute-start | bytes 786440 | tf_op jit(solution)/shard_map/ppermute | solution.py:218
  95.2 17.4 %collective-permute-start.16 = (bf16[128,1024]{1,0:T(8,128)(2,1)S(1)}, bf16[128,1024]{1,0:T(8,128)(2,1)S(1)}, u32[]{:S(2)}, u32[]{:S(2)}) collective-permute-start(bf16[128,1024]{1,0:T(8,128)(2,1)S(1)} %fusion.28), channel_id=1, source_target_pairs={{0,16},{4,20},{8,24},{12,28},{16,0},{20,4},{24,8},{28,12},{1,17},{... | collective-permute-start | bytes 786440 | tf_op jit(solution)/shard_map/ppermute | solution.py:218
  98.8 13.8 %copy-start.19 = (f32[2,128,1024]{2,1,0:T(8,128)S(1)}, f32[2,128,1024]{2,1,0:T(8,128)}, u32[]{:S(2)}) copy-start(f32[2,128,1024]{2,1,0:T(8,128)} %param.11) | copy-start | bytes 3145732
  109.7 22.8 %collective-permute-start.21 = (bf16[2,128,1024]{2,1,0:T(8,128)(2,1)S(1)}, bf16[2,128,1024]{2,1,0:T(8,128)(2,1)S(1)}, u32[]{:S(2)}, u32[]{:S(2)}) collective-permute-start(bf16[2,128,1024]{2,1,0:T(8,128)(2,1)S(1)} %bitcast.100), channel_id=1, source_target_pairs={{0,16},{4,20},{8,24},{12,28},{16,0},{20,4},{24,8},{28,12},{1,17},{... | collective-permute-start | bytes 1572872 | tf_op jit(solution)/shard_map/ppermute | solution.py:218
  110.7 21.8 %collective-permute-start.22 = (bf16[2,128,1024]{2,1,0:T(8,128)(2,1)S(1)}, bf16[2,128,1024]{2,1,0:T(8,128)(2,1)S(1)}, u32[]{:S(2)}, u32[]{:S(2)}) collective-permute-start(bf16[2,128,1024]{2,1,0:T(8,128)(2,1)S(1)} %bitcast.101), channel_id=1, source_target_pairs={{0,8},{4,12},{8,0},{12,4},{16,24},{20,28},{24,16},{28,20},{1,9},{5... | collective-permute-start | bytes 1572872 | tf_op jit(solution)/shard_map/ppermute | solution.py:218
  111.6 20.8 %collective-permute-start.23 = (bf16[2,128,1024]{2,1,0:T(8,128)(2,1)S(1)}, bf16[2,128,1024]{2,1,0:T(8,128)(2,1)S(1)}, u32[]{:S(2)}, u32[]{:S(2)}) collective-permute-start(bf16[2,128,1024]{2,1,0:T(8,128)(2,1)S(1)} %bitcast.102), channel_id=1, source_target_pairs={{0,4},{4,0},{8,12},{12,8},{16,20},{20,16},{24,28},{28,24},{1,5},{5... | collective-permute-start | bytes 1572872 | tf_op jit(solution)/shard_map/ppermute | solution.py:218
  115.4 1.3 collective-permute-start.17
  115.5 6.7 %copy-start.15 = (f32[2,128,1024]{2,1,0:T(8,128)S(1)}, f32[2,128,1024]{2,1,0:T(8,128)}, u32[]{:S(2)}) copy-start(f32[2,128,1024]{2,1,0:T(8,128)} %param.8) | copy-start | bytes 3145732
  115.5 6.7 %copy-start.18 = (f32[2,128,1024]{2,1,0:T(8,128)S(1)}, f32[2,128,1024]{2,1,0:T(8,128)}, u32[]{:S(2)}) copy-start(f32[2,128,1024]{2,1,0:T(8,128)} %param.7) | copy-start | bytes 3145732
  117.4 3.7 %collective-permute-start.18 = (f32[8,128]{1,0:T(8,128)S(1)}, f32[8,128]{1,0:T(8,128)S(1)}, u32[]{:S(2)}, u32[]{:S(2)}) collective-permute-start(f32[8,128]{1,0:T(8,128)S(1)} %fusion.40), channel_id=1, source_target_pairs={{0,2},{1,3},{2,0},{3,1},{4,6},{5,7},{6,4},{7,5},{8,10},{9,11},{10,... | collective-permute-start | bytes 12296 | tf_op jit(solution)/shard_map/ppermute | solution.py:335
  121.1 3.6 %collective-permute-start.19 = (f32[8,128]{1,0:T(8,128)S(1)}, f32[8,128]{1,0:T(8,128)S(1)}, u32[]{:S(2)}, u32[]{:S(2)}) collective-permute-start(f32[8,128]{1,0:T(8,128)S(1)} %add.108), channel_id=1, source_target_pairs={{0,4},{4,0},{8,12},{12,8},{16,20},{20,16},{24,28},{28,24},{1,5},{5... | collective-permute-start | bytes 12296 | tf_op jit(solution)/shard_map/ppermute | solution.py:218
  124.7 8.1 %collective-permute-start.20 = (f32[8,128]{1,0:T(8,128)S(1)}, f32[8,128]{1,0:T(8,128)S(1)}, u32[]{:S(2)}, u32[]{:S(2)}) collective-permute-start(f32[8,128]{1,0:T(8,128)S(1)} %add.109), channel_id=1, source_target_pairs={{0,16},{4,20},{8,24},{12,28},{16,0},{20,4},{24,8},{28,12},{1,17},{... | collective-permute-start | bytes 12296 | tf_op jit(solution)/shard_map/ppermute | solution.py:218
  132.6 36.3 %collective-permute-start.25 = (bf16[2,2,128,1024]{3,2,1,0:T(8,128)(2,1)S(1)}, bf16[2,2,128,1024]{3,2,1,0:T(8,128)(2,1)S(1)}, u32[]{:S(2)}, u32[]{:S(2)}) collective-permute-start(bf16[2,2,128,1024]{3,2,1,0:T(8,128)(2,1)S(1)} %pad_maximum_fusion), channel_id=1, source_target_pairs={{0,4},{4,0},{8,12},{12,8},{16,20},{20,16},{24,28},{28,24},{1,5},{5... | collective-permute-start | bytes 3145736 | tf_op jit(solution)/shard_map/ppermute | solution.py:218
  132.8 6.3 %collective-permute-start.24 = (f32[8,128]{1,0:T(8,128)S(1)}, f32[8,128]{1,0:T(8,128)S(1)}, u32[]{:S(2)}, u32[]{:S(2)}) collective-permute-start(f32[8,128]{1,0:T(8,128)S(1)} %add.110), channel_id=1, source_target_pairs={{0,8},{4,12},{8,0},{12,4},{16,24},{20,28},{24,16},{28,20},{1,9},{5... | collective-permute-start | bytes 12296 | tf_op jit(solution)/shard_map/ppermute | solution.py:218
  133.7 35.6 %collective-permute-start.26 = (bf16[2,128,1024]{2,1,0:T(8,128)(2,1)S(1)}, bf16[2,128,1024]{2,1,0:T(8,128)(2,1)S(1)}, u32[]{:S(2)}, u32[]{:S(2)}) collective-permute-start(bf16[2,128,1024]{2,1,0:T(8,128)(2,1)S(1)} %collective-permute-done.21), channel_id=1, source_target_pairs={{0,12},{4,8},{8,4},{12,0},{16,28},{20,24},{24,20},{28,16},{1,13},{... | collective-permute-start | bytes 1572872 | tf_op jit(solution)/shard_map/ppermute | solution.py:361
  136.5 34.1 %collective-permute-start.27 = (bf16[2,128,1024]{2,1,0:T(8,128)(2,1)S(1)}, bf16[2,128,1024]{2,1,0:T(8,128)(2,1)S(1)}, u32[]{:S(2)}, u32[]{:S(2)}) collective-permute-start(bf16[2,128,1024]{2,1,0:T(8,128)(2,1)S(1)} %collective-permute-done.21), channel_id=1, source_target_pairs={{0,8},{4,12},{8,0},{12,4},{16,24},{20,28},{24,16},{28,20},{1,9},{5... | collective-permute-start | bytes 1572872 | tf_op jit(solution)/shard_map/ppermute | solution.py:361
  136.5 34.2 %collective-permute-start.28 = (bf16[2,128,1024]{2,1,0:T(8,128)(2,1)S(1)}, bf16[2,128,1024]{2,1,0:T(8,128)(2,1)S(1)}, u32[]{:S(2)}, u32[]{:S(2)}) collective-permute-start(bf16[2,128,1024]{2,1,0:T(8,128)(2,1)S(1)} %pad_maximum_fusion.5), channel_id=1, source_target_pairs={{0,16},{4,20},{8,24},{12,28},{16,0},{20,4},{24,8},{28,12},{1,17},{... | collective-permute-start | bytes 1572872 | tf_op jit(solution)/shard_map/ppermute | solution.py:218
  141.6 29.1 %copy-start.13 = (f32[2,128,1024]{2,1,0:T(8,128)S(1)}, f32[2,128,1024]{2,1,0:T(8,128)}, u32[]{:S(2)}) copy-start(f32[2,128,1024]{2,1,0:T(8,128)} %param.8) | copy-start | bytes 3145732
  141.6 29.1 %copy-start.16 = (f32[2,128,1024]{2,1,0:T(8,128)S(1)}, f32[2,128,1024]{2,1,0:T(8,128)}, u32[]{:S(2)}) copy-start(f32[2,128,1024]{2,1,0:T(8,128)} %param.7) | copy-start | bytes 3145732
  170.6 2.0 %copy-start.12 = (bf16[2,2,4,128,1024]{4,3,2,1,0:T(8,128)(2,1)}, bf16[2,2,4,128,1024]{4,3,2,1,0:T(8,128)(2,1)S(1)}, u32[]{:S(2)}) copy-start(bf16[2,2,4,128,1024]{4,3,2,1,0:T(8,128)(2,1)S(1)} %fusion.20) | copy-start | bytes 12582916
  170.9 2.1 %copy-start.14 = (f32[2,128,1024]{2,1,0:T(8,128)}, f32[2,128,1024]{2,1,0:T(8,128)S(1)}, u32[]{:S(2)}) copy-start(f32[2,128,1024]{2,1,0:T(8,128)S(1)} %get-tuple-element.68) | copy-start | bytes 3145732
  170.9 2.4 %copy-start.17 = (f32[2,128,1024]{2,1,0:T(8,128)}, f32[2,128,1024]{2,1,0:T(8,128)S(1)}, u32[]{:S(2)}) copy-start(f32[2,128,1024]{2,1,0:T(8,128)S(1)} %get-tuple-element.69) | copy-start | bytes 3145732
